TPU v7x, 32 devices: a whole 2x2x4 slice. The times are simulated.
32 devices in a mesh: groups: 2 (over x), pop: 8 (over z, y), tensor: 2 (over core).
Axes of the slice: x: 2, y: 2, z: 4, core: 2. Of those that a mesh axis runs over, the one named last changes fastest.
Arguments:
- prompts: bfloat16 [48, 8192], P('groups'), parts along dimension 0, may hold values from -6 to 6
- gate_weight: bfloat16 [8192, 14848], P('pop', 'tensor'), may hold values from -0.0625 to 0.0625
- up_weight: bfloat16 [8192, 14848], P('pop', 'tensor'), may hold values from -0.0625 to 0.0625
- down_weight_matrix: bfloat16 [14848, 8192], P('tensor', 'pop'), may hold values from -0.046875 to 0.046875
- gate_in: bfloat16 [16, 8192, 4], P(('groups', 'pop')), parts along dimension 0, may hold values from -6 to 6
- gate_output_factors: bfloat16 [16, 14848, 4], P(('groups', 'pop'), 'tensor'), parts along dimension 0, may hold values from -6 to 6
- up_in: bfloat16 [16, 8192, 4], P(('groups', 'pop')), parts along dimension 0, may hold values from -6 to 6
- up_output_factors: bfloat16 [16, 14848, 4], P(('groups', 'pop'), 'tensor'), parts along dimension 0, may hold values from -6 to 6
- down_input_factors: bfloat16 [16, 14848, 4], P('groups', 'tensor'), parts along dimension 0, may hold values from -6 to 6
- down_out: bfloat16 [16, 8192, 4], P('groups', 'pop'), parts along dimension 0, may hold values from -6 to 6
- label_head: bfloat16 [8192, 128], P('tensor'), may hold values from -0.1875 to 0.1875
- targets: int32 [48], P('groups'), parts along dimension 0, may hold values from 0 to 127
Outputs:
- update: bfloat16 [29696, 8192], P(('groups', 'tensor'), 'pop'), parts along dimension 0
- scores: float32 [16], P(('groups', 'pop')), parts along dimension 0
There are 2 independent parts, one for each index of `groups`. A program takes and returns all parts, laid end to end along the dimension named above; an argument that names none is the same for every part. Nothing has to cross between parts.
All inputs are finite; a program needn't handle non-finite values.
Results may differ from a plain program's by a relative error of at most 0.023.
Values may be sent and summed in bfloat16 or wider, within the bound.
No kernel may reach another device: no remote copies, remote signals or barrier semaphores. Data moves between devices by JAX's collectives and lax.ppermute only.
A program may use at most 256 MiB of HBM per device.

v0:
```python
import math

import jax
import jax.numpy as jnp
from jax import lax
from jax.sharding import PartitionSpec as P

noise_scale = 0.2
norm_eps = 1e-06


def scaled_rows(values):
    return values * lax.rsqrt(jnp.mean(values * values, axis=-1, keepdims=True) + norm_eps)


def build_hidden(
    gate_baseline, up_baseline, lowrank_gate, lowrank_up, gate_output_factors, up_output_factors
):
    gate_activation = gate_baseline.astype(jnp.float32)[None] + jnp.einsum(
        "hvw,hpw->hvp", lowrank_gate, gate_output_factors, preferred_element_type=jnp.float32
    )
    upper_bound = up_baseline.astype(jnp.float32)[None] + jnp.einsum(
        "hvw,hpw->hvp", lowrank_up, up_output_factors, preferred_element_type=jnp.float32
    )
    return (jax.nn.silu(gate_activation) * upper_bound).astype(jnp.bfloat16)


def label_terms(logits, targets):
    labels = logits.shape[1]
    picks = targets[:, None] == jnp.arange(labels, dtype=jnp.int32)[None, :]
    picked = jnp.sum(jnp.where(picks, logits, 0.0), axis=1)
    return picked - jnp.log(jnp.sum(jnp.exp(logits), axis=1))


def body(
    prompts,
    gate_weight,
    up_weight,
    down_weight_matrix,
    gate_in,
    gate_output_factors,
    up_in,
    up_output_factors,
    down_input_factors,
    down_out,
    label_head,
    targets,
):
    member = lax.axis_index("pop")
    width = prompts.shape[1]
    in_block = gate_weight.shape[0]
    ffn_half = gate_output_factors.shape[1]
    total_ff = ffn_half * lax.axis_size("tensor")
    members = down_input_factors.shape[0]
    rank = down_input_factors.shape[2]
    prompt_f = prompts.astype(jnp.float32)
    normed = scaled_rows(prompt_f).astype(jnp.bfloat16)
    own_cols = lax.dynamic_slice_in_dim(normed, member * in_block, in_block, 1)
    part_gate = jnp.dot(own_cols, gate_weight, preferred_element_type=jnp.float32)
    part_up = jnp.dot(own_cols, up_weight, preferred_element_type=jnp.float32)
    total_gate, total_up = lax.psum((part_gate, part_up), "pop")
    gate_baseline = total_gate.astype(jnp.bfloat16)
    up_baseline = total_up.astype(jnp.bfloat16)
    in_scale = noise_scale / math.sqrt(width)
    lowrank_gate = (
        in_scale * jnp.einsum("rd,mdk->mrk", normed, gate_in, preferred_element_type=jnp.float32)
    ).astype(jnp.bfloat16)
    lowrank_up = (
        in_scale * jnp.einsum("rd,mdk->mrk", normed, up_in, preferred_element_type=jnp.float32)
    ).astype(jnp.bfloat16)
    down_scale = noise_scale / math.sqrt(total_ff)
    hidden_state = build_hidden(
        gate_baseline, up_baseline, lowrank_gate, lowrank_up, gate_output_factors, up_output_factors
    )
    hidden_portion = lax.all_gather(hidden_state, "pop", axis=0, tiled=True)
    out_piece = down_out.astype(jnp.float32)
    entry_point = jnp.einsum(
        "uaz,zh->uah", hidden_portion, down_weight_matrix, preferred_element_type=jnp.float32
    )
    low_part = down_scale * jnp.einsum(
        "lpq,lqb->lpb", hidden_portion, down_input_factors, preferred_element_type=jnp.float32
    )
    partial_rows = entry_point + jnp.einsum(
        "mrk,mdk->mrd", low_part, out_piece, precision=lax.Precision.HIGHEST
    )
    rows_here = lax.all_to_all(partial_rows, "pop", split_axis=0, concat_axis=2, tiled=True)
    summed = lax.psum(rows_here, "tensor")[0]
    output = prompt_f + summed
    final = scaled_rows(output).astype(jnp.bfloat16)
    half = label_head.shape[0]
    own_half = lax.dynamic_slice_in_dim(final, lax.axis_index("tensor") * half, half, 1)
    logits = lax.psum(jnp.dot(own_half, label_head, preferred_element_type=jnp.float32), "tensor")
    reward = jnp.mean(label_terms(logits, targets))
    rewards = lax.all_gather(reward.reshape(1), "pop", axis=0, tiled=True)
    centre = jnp.mean(rewards)
    spread = jnp.mean((rewards - centre) * (rewards - centre))
    scores = (rewards - centre) * lax.rsqrt(spread + norm_eps)
    weighted = (scores[:, None, None] * down_out.astype(jnp.float32)).astype(jnp.bfloat16)
    update = jnp.einsum(
        "mfk,mdk->fd", down_input_factors, weighted, preferred_element_type=jnp.float32
    ) * (1.0 / math.sqrt(members * rank))
    own_score = lax.dynamic_slice_in_dim(scores, member, 1, 0)
    return (update.astype(jnp.bfloat16), own_score)


def solution(mesh):
    placed = (
        P("groups", None),
        P("pop", "tensor"),
        P("pop", "tensor"),
        P("tensor", "pop"),
        P(("groups", "pop"), None, None),
        P(("groups", "pop"), "tensor", None),
        P(("groups", "pop"), None, None),
        P(("groups", "pop"), "tensor", None),
        P("groups", "tensor", None),
        P("groups", "pop", None),
        P("tensor", None),
        P("groups"),
    )
    return jax.shard_map(
        body,
        mesh=mesh,
        in_specs=placed,
        out_specs=(P(("groups", "tensor"), "pop"), P(("groups", "pop"))),
        check_vma=False,
    )
```

profile of v0, /device:TPU:0, one launch (start us, length us, event | category | flops | bytes accessed | tf_op | source)
XLA Modules:
  0.0 282.9 jit_solution(8416717195286552256)
XLA Ops:
  7.2 0.0 copy-start
  7.2 0.0 all-gather.3.cloned.1.call-start
  7.2 1.3 fusion.8
  8.5 1.1 fusion.9
  9.6 0.0 copy-start.2
  9.7 7.6 %fusion.21 = f32[24,7424]{1,0:T(8,128)S(1)} fusion(bf16[1024,7424]{1,0:T(8,128)(2,1)} %param.14, bf16[24,8192]{1,0:T(8,128)(2,1)S(1)} %fusion.9, s32[]{:T(128)S(6)} %select_n.13), kind=kOutput, calls=%fused_computation.31 | convolution fusion | flops 364904448 | bytes 15966212 | tf_op jit(solution)/shard_map/dot_general | solution.py:60
  17.2 2.1 copy-done.2
  19.3 0.0 copy-start.4
  19.3 2.1 fusion.23
  21.4 79.3 %all-reduce.6 = (bf16[24,7424]{1,0:T(8,128)(2,1)S(1)}, bf16[24,7424]{1,0:T(8,128)(2,1)}) all-reduce(f32[24,7424]{1,0:T(8,128)S(1)} %fusion.23, f32[24,7424]{1,0:T(8,128)S(1)} %fusion.21), channel_id=1, replica_groups=mesh['groups'=2,'pop'=8,'tensor'=2] {'pop'}, use_global_device_ids=true, to_apply=%region_1.0 | all-reduce | flops 356352 | bytes 2138112 | tf_op jit(solution)/shard_map/psum | solution.py:61
  100.7 0.0 copy-done.4
  100.7 0.0 copy-done.6
  100.7 0.7 convolution_add_fusion.1
  101.4 0.0 copy-done.9
  101.4 0.0 copy-done.10
  101.4 2.4 fusion.5
  103.8 0.0 all-gather.3.cloned.1.call-update
  103.8 0.0 all-reduce.5.cloned.1.call-start
  103.9 57.8 %all-gather.3.cloned.1.call-done = bf16[192,7424]{1,0:T(8,128)(2,1)} async-done(((bf16[24,7424]{1,0:T(8,128)(2,1)}), bf16[192,7424]{1,0:T(8,128)(2,1)}) %all-gather.3.cloned.1.call-update) | async-done | bytes 2850832 | tf_op jit(solution)/shard_map/all_gather | solution.py:75
  161.6 2.8 convolution_multiply_fusion
  164.4 0.0 copy-start.7
  164.4 0.0 copy-start.8
  164.5 7.9 %fusion.1 = f32[8,24,1024]{2,1,0:T(8,128)S(1)} fusion(bf16[8,24,7424]{2,1,0:T(8,128)(2,1)} %bitcast.50, bf16[7424,1024]{1,0:T(8,128)(2,1)} %param.15), kind=kOutput, calls=%fused_computation.2 | convolution fusion | flops 2919235584 | bytes 18841600 | tf_op jit(solution)/shard_map/uaz,zh->uah/dot_general | solution.py:77
  172.4 0.0 copy-done.5
  172.4 0.6 convolution_add_fusion.2
  173.0 23.2 %all_to_all.18 = f32[8,24,1024]{2,1,0:T(8,128)S(1)} all-to-all(f32[8,24,1024]{2,1,0:T(8,128)S(1)} %convolution_add_fusion.2), channel_id=1, replica_groups=mesh['groups'=2,'pop'=8,'tensor'=2] {'pop'}, dimensions={0} | all-to-all | bytes 1572864 | tf_op jit(solution)/shard_map/all_to_all | solution.py:86
  196.2 0.9 copy.23
  197.1 0.0 all-reduce.5.cloned.1.call-update
  197.1 0.0 copy-done.11
  197.1 0.6 dynamic-slice
  197.8 17.7 %all-reduce.5.cloned.1.call-done = f32[24,8192]{1,0:T(8,128)} async-done(((f32[24,8192]{1,0:T(8,128)}), f32[24,8192]{1,0:T(8,128)}) %all-reduce.5.cloned.1.call-update) | async-done | bytes 786448 | tf_op jit(solution)/shard_map/psum | solution.py:87
  215.5 0.0 copy-done.3
  215.5 1.4 multiply_reduce_fusion
  216.8 0.0 copy-done
  216.9 0.3 fusion.11
  217.2 3.3 %psum.31 = f32[24,128]{1,0:T(8,128)S(1)} all-reduce(f32[24,128]{1,0:T(8,128)S(1)} %fusion.11), channel_id=1, replica_groups=mesh['groups'=2,'pop'=8,'tensor'=2] {'tensor'}, use_global_device_ids=true, to_apply=%region_5.6 | all-reduce | flops 3072 | bytes 24576 | tf_op jit(solution)/shard_map/psum | solution.py:92
  220.5 0.0 copy-done.7
  220.5 0.2 exponential_reduce_fusion
  220.7 0.6 subtract_reduce_fusion
  222.0 0.7 dynamic-update-slice
  222.7 21.9 %all-reduce = f32[8]{0:T(128)S(1)} all-reduce(f32[8]{0:T(128)S(1)} %dynamic-update-slice), channel_id=1, replica_groups=mesh['groups'=2,'pop'=8,'tensor'=2] {'pop'}, use_global_device_ids=true, to_apply=%add | all-reduce | flops 8 | bytes 64
  244.6 0.6 reduce_sum.68
  245.8 0.6 multiply_reduce_fusion.1
  247.1 0.0 copy-done.8
  247.1 8.0 %fusion.3 = bf16[7424,1024]{0,1:T(8,128)(2,1)} fusion(bf16[8,7424,4]{1,2,0:T(4,128)(2,1)S(1)} %copy-done.8, bf16[8,1024,4]{1,2,0:T(4,128)(2,1)S(1)} %copy-done.5, f32[8]{0:T(128)S(1)} %subtract_multiply_fusion), kind=kOutput, calls=%fused_computation.4 | convolution fusion | flops 501841920 | bytes 15745056 | tf_op jit(solution)/shard_map/mfk,mdk->fd/dot_general | solution.py:99
  255.1 0.6 dynamic_slice.11
  255.7 20.4 %copy.20 = bf16[7424,1024]{1,0:T(8,128)(2,1)} copy(bf16[7424,1024]{0,1:T(8,128)(2,1)} %fusion.3) | data formatting | bytes 30408704
  276.1 0.0 copy-done.1
  (11 shorter events, 0.0 us)
Async XLA Ops:
  7.2 209.7 %copy-start = (bf16[4096,128]{1,0:T(8,128)(2,1)S(1)}, bf16[4096,128]{1,0:T(8,128)(2,1)}, u32[]{:S(2)}) copy-start(bf16[4096,128]{1,0:T(8,128)(2,1)} %param.22) | copy-start | bytes 3145732
  7.2 154.5 %all-gather.3.cloned.1.call-start = ((), (), s32[]{:S(2)}) async-start(), calls=%async_computation.2 | async-start | bytes 3207168 | tf_op jit(solution)/shard_map/all_gather | solution.py:75
  9.6 9.7 %copy-start.2 = (bf16[1024,7424]{1,0:T(8,128)(2,1)S(1)}, bf16[1024,7424]{1,0:T(8,128)(2,1)}, u32[]{:S(2)}) copy-start(bf16[1024,7424]{1,0:T(8,128)(2,1)} %param.13) | copy-start | bytes 45613060
  19.3 81.4 %copy-start.4 = (bf16[1,8192,4]{1,2,0:T(4,128)(2,1)S(1)}, bf16[1,8192,4]{1,2,0:T(4,128)(2,1)}, u32[]{:S(2)}) copy-start(bf16[1,8192,4]{1,2,0:T(4,128)(2,1)} %param.16) | copy-start | bytes 196612
  19.3 81.4 %copy-start.6 = (bf16[1,7424,4]{1,2,0:T(4,128)(2,1)S(1)}, bf16[1,7424,4]{1,2,0:T(4,128)(2,1)}, u32[]{:S(2)}) copy-start(bf16[1,7424,4]{1,2,0:T(4,128)(2,1)} %param.17) | copy-start | bytes 178180
  19.3 82.1 %copy-start.9 = (bf16[1,8192,4]{1,2,0:T(4,128)(2,1)S(1)}, bf16[1,8192,4]{1,2,0:T(4,128)(2,1)}, u32[]{:S(2)}) copy-start(bf16[1,8192,4]{1,2,0:T(4,128)(2,1)} %param.18) | copy-start | bytes 196612
  19.3 82.1 %copy-start.10 = (bf16[1,7424,4]{1,2,0:T(4,128)(2,1)S(1)}, bf16[1,7424,4]{1,2,0:T(4,128)(2,1)}, u32[]{:S(2)}) copy-start(bf16[1,7424,4]{1,2,0:T(4,128)(2,1)} %param.19) | copy-start | bytes 178180
  103.8 111.6 %all-reduce.5.cloned.1.call-start = ((), (), s32[]{:S(2)}) async-start(), calls=%async_computation.1 | async-start | bytes 1572864 | tf_op jit(solution)/shard_map/psum | solution.py:87
  161.6 10.8 %copy-start.5 = (bf16[8,1024,4]{1,2,0:T(4,128)(2,1)S(1)}, bf16[8,1024,4]{1,2,0:T(4,128)(2,1)}, u32[]{:S(2)}) copy-start(bf16[8,1024,4]{1,2,0:T(4,128)(2,1)} %param.21) | copy-start | bytes 196612
  164.4 32.7 %copy-start.11 = (u32[32]{0:T(128)S(1)}, u32[32]{0:T(128)}, u32[]{:S(2)}) copy-start(u32[32]{0:T(128)} %constant.49) | copy-start | bytes 388
  164.4 51.0 %copy-start.3 = (bf16[24,8192]{1,0:T(8,128)(2,1)S(1)}, bf16[24,8192]{1,0:T(8,128)(2,1)}, u32[]{:S(2)}) copy-start(bf16[24,8192]{1,0:T(8,128)(2,1)} %param.12) | copy-start | bytes 1179652
  164.4 56.1 %copy-start.7 = (s32[24]{0:T(128)S(1)}, s32[24]{0:T(128)}, u32[]{:S(2)}) copy-start(s32[24]{0:T(128)} %param.23) | copy-start | bytes 292
  164.4 82.7 %copy-start.8 = (bf16[8,7424,4]{1,2,0:T(4,128)(2,1)S(1)}, bf16[8,7424,4]{1,2,0:T(4,128)(2,1)}, u32[]{:S(2)}) copy-start(bf16[8,7424,4]{1,2,0:T(4,128)(2,1)} %param.20) | copy-start | bytes 1425412
  255.1 21.0 %copy-start.1 = (bf16[4096,128]{1,0:T(8,128)(2,1)S(1)}, bf16[4096,128]{1,0:T(8,128)(2,1)}, u32[]{:S(2)}) copy-start(bf16[4096,128]{1,0:T(8,128)(2,1)} %param.22) | copy-start | bytes 3145732
Sparse Core Ops, SparseCore 0:
  104.0 57.6 all-gather.2
  197.2 18.1 all-reduce.4
where the time goes:
time: 284 us; the launch traced here: 283 us
  blocking collectives  128 us (45%)
  waiting for transfers between devices  75.5 us (27%)
  matrix products  32.3 us (11%)
  local copies, waits for them, and re-layouts  25.4 us (9%)
  between operations  16.2 us (6%)
  other arithmetic  5.78 us (2%)
    psum x1, blocking collectives, body(): total_gate, total_up = lax.psum((part_gate, part_up), 'pop')  79.3 us
    all_gather x1, waiting for transfers between devices, body(): hidden_portion = lax.all_gather(hidden_state, 'pop', axis=0, tiled=True)  57.8 us
    unnamed x29, local copies, waits for them, and re-layouts  24.8 us
    all_to_all x1, blocking collectives, body(): lax.all_to_all(partial_rows, 'pop', split_axis=0, concat_axis=2, tiled=True)  23.2 us
    unnamed x1, blocking collectives  21.9 us
    psum x1, waiting for transfers between devices, body(): summed = lax.psum(rows_here, 'tensor')[0]  17.7 us
    dot_general x1, matrix products, body(): jnp.einsum('mfk,mdk->fd', down_input_factors, weighted, preferred_element...  7.97 us
    dot_general x1, matrix products, body(): jnp.einsum('uaz,zh->uah', hidden_portion, down_weight_matrix, preferred_e...  7.93 us
  transfers between devices with their start and end apart: 2, of which 2 were waited for; matrix products, arithmetic and copies ran while one was open for 0% of the time, Pallas kernels for 0%

commit v1 on v0

--- a/solution.py
+++ b/solution.py
@@ -1,12 +1,33 @@
+import functools
 import math
 
 import jax
 import jax.numpy as jnp
 from jax import lax
+from jax.experimental import pallas as pl
+from jax.experimental.pallas import tpu as pltpu
 from jax.sharding import PartitionSpec as P
 
 noise_scale = 0.2
 norm_eps = 1e-06
+lane = 128
+bf16 = jnp.bfloat16
+f32 = jnp.float32
+MiB = 1 << 20
+in_vmem = pl.BlockSpec(memory_space=pltpu.VMEM)
+in_any = pl.BlockSpec(memory_space=pl.ANY)
+
+
+def dot_nn(a, b, **kw):
+    return lax.dot_general(a, b, (((1,), (0,)), ((), ())), preferred_element_type=f32, **kw)
+
+
+def dot_nt(a, b, **kw):
+    return lax.dot_general(a, b, (((1,), (1,)), ((), ())), preferred_element_type=f32, **kw)
+
+
+def dot_tn(a, b, **kw):
+    return lax.dot_general(a, b, (((0,), (0,)), ((), ())), preferred_element_type=f32, **kw)
 
 
 def scaled_rows(values):
@@ -32,7 +53,7 @@
     return picked - jnp.log(jnp.sum(jnp.exp(logits), axis=1))
 
 
-def body(
+def general_body(
     prompts,
     gate_weight,
     up_weight,
@@ -103,6 +124,453 @@
     return (update.astype(jnp.bfloat16), own_score)
 
 
+def cube():
+    p = lax.axis_index("pop")
+    return p, p & 1, (p >> 1) & 1, p >> 2
+
+
+class Tiles:
+    def __init__(self, units):
+        self.half = units // lane // 2
+        self.wide = (self.half + 1) // 2
+        self.step = self.half - self.wide
+        self.repeat = 2 * self.wide - self.half
+        self.cols = self.wide * lane
+
+    def start(self, y, z1):
+        return pl.multiple_of((y * self.half + z1 * self.step) * lane, lane)
+
+
+def chunks_of(cols, most):
+    tiles = cols // lane
+    for n in range(1, tiles + 1):
+        if tiles % n == 0 and cols // n <= most:
+            return n, cols // n
+    return tiles, lane
+
+
+def swap(x, axis, bit, size):
+    return lax.ppermute(x, axis, [(i, i ^ bit) for i in range(size)])
+
+
+def prep_kernel(x_ref, gin_ref, uin_ref, gof_ref, uof_ref, xn_ref, fac_ref, norm_ref, fac32, low32):
+    p = cube()[0]
+    rows, width = x_ref.shape
+    units = gof_ref.shape[1]
+    rank = gof_ref.shape[0]
+    block = xn_ref.shape[1]
+    x = x_ref[...].astype(f32)
+    normed = scaled_rows(x).astype(bf16)
+    norm_ref[...] = normed
+    xn_ref[...] = norm_ref[:, pl.ds(pl.multiple_of(p * block, lane), block)]
+    fac32[0:rank, :] = gof_ref[...].astype(f32)
+    fac32[rank : 2 * rank, :] = uof_ref[...].astype(f32)
+    fac_ref[:, 0:units] = fac32[...].astype(bf16)
+    scale = noise_scale / math.sqrt(width)
+    low32[...] = jnp.zeros_like(low32)
+    low32[0:rank, 0:rows] = scale * dot_nt(gin_ref[...], normed)
+    low32[rank : 2 * rank, 0:rows] = scale * dot_nt(uin_ref[...], normed)
+    fac_ref[:, units : units + lane] = low32[...].astype(bf16)
+
+
+def prep(prompts, gin, uin, gof, uof, block):
+    rows, width = prompts.shape
+    rank, units = gof.shape
+    return pl.pallas_call(
+        prep_kernel,
+        out_shape=(
+            jax.ShapeDtypeStruct((rows, block), bf16),
+            jax.ShapeDtypeStruct((2 * rank, units + lane), bf16),
+        ),
+        in_specs=[in_vmem] * 5,
+        out_specs=(in_vmem, in_vmem),
+        scratch_shapes=[
+            pltpu.VMEM((rows, width), bf16),
+            pltpu.VMEM((2 * rank, units), f32),
+            pltpu.VMEM((2 * rank, lane), f32),
+        ],
+        compiler_params=pltpu.CompilerParams(vmem_limit_bytes=16 * MiB),
+        name="prep",
+    )(prompts, gin, uin, gof, uof)
+
+
+def base_kernel(tiles, dy, dz1, n, width, xn_ref, wg_ref, wu_ref, out_ref, wg, wu, sems):
+    p, y, z1, z2 = cube()
+    at = tiles.start(y ^ dy, z1 ^ dz1)
+    jobs = [(wg_ref, wg, 1 - z2, 0), (wu_ref, wu, z2, 1)]
+    copies = []
+    for c in range(n):
+        for src, dst, slot, s in jobs:
+            copy = pltpu.make_async_copy(
+                src.at[:, pl.ds(pl.multiple_of(at + c * width, lane), width)],
+                dst.at[:, pl.ds(c * width, width)],
+                sems.at[s, c],
+            )
+            copy.start()
+            copies.append((copy, dst, slot, c))
+    xn = xn_ref[...]
+    for copy, dst, slot, c in copies:
+        copy.wait()
+        span = pl.ds(c * width, width)
+        out_ref[slot, :, span] = dot_nn(xn, dst[:, span]).astype(out_ref.dtype)
+
+
+def base_part(xn, wg, wu, tiles, dy, dz1, dtype):
+    n, width = chunks_of(tiles.cols, 512)
+    rows, depth = xn.shape
+    return pl.pallas_call(
+        functools.partial(base_kernel, tiles, dy, dz1, n, width),
+        out_shape=jax.ShapeDtypeStruct((2, rows, tiles.cols), dtype),
+        in_specs=[in_vmem, in_any, in_any],
+        out_specs=in_vmem,
+        scratch_shapes=[
+            pltpu.VMEM((depth, tiles.cols), bf16),
+            pltpu.VMEM((depth, tiles.cols), bf16),
+            pltpu.SemaphoreType.DMA((2, n)),
+        ],
+        compiler_params=pltpu.CompilerParams(vmem_limit_bytes=16 * MiB),
+        cost_estimate=pl.CostEstimate(
+            flops=4 * rows * depth * tiles.cols,
+            bytes_accessed=4 * depth * tiles.cols,
+            transcendentals=0,
+        ),
+        name=f"base_y{dy}_z{dz1}",
+    )(xn, wg, wu)
+
+
+def flip3(q):
+    return ((q & 1) << 2) | (q & 2) | (q >> 2)
+
+
+def count_steps(index, size, times):
+    total = jnp.zeros_like(index)
+    for i in range(1, times):
+        total = total + (index >= i * size).astype(jnp.int32)
+    return total
+
+
+def mix_kernel(rows, near_ref, far_ref, mix_ref, low_ref):
+    p = cube()[0]
+    members = 8
+    group = near_ref.shape[1]
+    rank = group // 2
+    units = near_ref.shape[2] - lane
+    low_ref[...] = jnp.zeros_like(low_ref)
+    for q in range(members):
+        ref = near_ref if q < 4 else far_ref
+        low_ref[q * group : (q + 1) * group, :] = ref[q % 4, :, units : units + lane].astype(f32)
+    height, depth = mix_ref.shape
+    r0 = lax.broadcasted_iota(jnp.int32, (height, lane), 0)
+    c0 = lax.broadcasted_iota(jnp.int32, (height, lane), 1)
+    picks = (r0 - rows * count_steps(r0, rows, 2 * members) == c0).astype(f32).astype(bf16)
+    spread = dot_nt(picks, low_ref[...].astype(bf16))
+    r = lax.broadcasted_iota(jnp.int32, (height, depth), 0)
+    c = lax.broadcasted_iota(jnp.int32, (height, depth), 1)
+    step = count_steps(r, rows, 2 * members)
+    in_rows = r - rows * step
+    kind = (step >= members).astype(jnp.int32)
+    member = step - members * kind
+    q = c // group if group & (group - 1) else c >> (group.bit_length() - 1)
+    rel = ((q & 1) << 2) | (q & 2) | ((q >> 2) & 1)
+    second = ((c - q * group) >= rank).astype(jnp.int32)
+    top = members * group
+    own = (c < top) & ((member ^ p) == rel) & (second == kind)
+    base = (c >= top) & (c - top - rows * kind == in_rows)
+    mix_ref[...] = (jnp.where(own, spread, 0.0) + jnp.where(base, 1.0, 0.0)).astype(bf16)
+
+
+def mixing(near, far, rows):
+    group = near.shape[1]
+    depth = 8 * group + 2 * rows
+    return pl.pallas_call(
+        functools.partial(mix_kernel, rows),
+        out_shape=jax.ShapeDtypeStruct((16 * rows, depth), bf16),
+        in_specs=[in_vmem] * 2,
+        out_specs=in_vmem,
+        scratch_shapes=[pltpu.VMEM((depth, lane), f32)],
+        compiler_params=pltpu.CompilerParams(vmem_limit_bytes=8 * MiB),
+        name="mixing",
+    )(near, far)
+
+
+def hidden_kernel(
+    tiles, dy, dz1, n, width, first, last, rows, down_scale, mix_ref, near_ref, far_ref, pair_ref, wd_ref, dif_ref, *rest
+):
+    p, y, z1, z2 = cube()
+    rest = list(rest)
+    acc_in, low_in = (None, None) if first else (rest.pop(0), rest.pop(0))
+    if last:
+        dout_ref, send_ref, keep_ref = rest.pop(0), rest.pop(0), rest.pop(0)
+    else:
+        acc_out, low_out = rest.pop(0), rest.pop(0)
+    right_ref, wd, sems = rest[:3]
+    group = near_ref.shape[1]
+    zb = z1 ^ dz1
+    at = tiles.start(y ^ dy, zb)
+    copies = []
+    for c in range(n):
+        copy = pltpu.make_async_copy(
+            wd_ref.at[pl.ds(pl.multiple_of(at + c * width, lane), width), :],
+            wd.at[pl.ds(c * width, width), :],
+            sems.at[c],
+        )
+        copy.start()
+        copies.append(copy)
+    for q in range(8):
+        ref = near_ref if q < 4 else far_ref
+        right_ref[q * group : (q + 1) * group, :] = ref[q % 4, :, pl.ds(at, tiles.cols)]
+    top = 8 * group
+    right_ref[top : top + rows, :] = pair_ref[z2]
+    right_ref[top + rows : top + 2 * rows, :] = pair_ref[1 - z2]
+    mix = mix_ref[...]
+    height = mix.shape[0] // 2
+    acc = None if first else acc_in[...]
+    low = None if first else low_in[...]
+    for c in range(n):
+        span = pl.ds(c * width, width)
+        both = dot_nn(mix, right_ref[:, span])
+        gate, up = both[:height], both[height:]
+        hidden = gate / (1.0 + jnp.exp(-gate)) * up
+        if c * width < tiles.repeat * lane:
+            col = lax.broadcasted_iota(jnp.int32, hidden.shape, 1) + c * width
+            hidden = jnp.where(col >= zb * (tiles.repeat * lane), hidden, 0.0)
+        hidden = hidden.astype(bf16)
+        more_low = dot_nt(hidden, dif_ref[:, pl.ds(pl.multiple_of(at + c * width, lane), width)])
+        copies[c].wait()
+        more = dot_nn(hidden, wd[span, :])
+        acc = more if acc is None else acc + more
+        low = more_low if low is None else low + more_low
+    if not last:
+        acc_out[...] = acc
+        low_out[...] = low
+        return
+    t = lax.axis_index("tensor")
+    terms = dif_ref.shape[0]
+    rank = terms // 8
+    r = lax.broadcasted_iota(jnp.int32, (height, terms), 0)
+    c = lax.broadcasted_iota(jnp.int32, (height, terms), 1)
+    mine = count_steps(r, rows, 8) == count_steps(c, rank, 8)
+    low = jnp.where(mine, low * down_scale, 0.0)
+    total = rest[3]
+    total[...] = acc + dot_nn(low, dout_ref[...].astype(f32), precision=lax.Precision.HIGHEST)
+    part = height // 2
+    keep_ref[...] = total[pl.ds(pl.multiple_of(t * part, 8), part), :]
+    send_ref[...] = total[pl.ds(pl.multiple_of((1 - t) * part, 8), part), :]
+
+
+def hidden_step(mix, near, far, pair, wd, dif, tiles, dy, dz1, rows, scale, state=None, dout=None):
+    n, width = chunks_of(tiles.cols, 640)
+    height = mix.shape[0] // 2
+    out = wd.shape[1]
+    terms = dif.shape[0]
+    first, last = state is None, dout is not None
+    args = [mix, near, far, pair, wd, dif]
+    specs = [in_vmem] * 4 + [in_any, in_vmem]
+    if not first:
+        args += list(state)
+        specs += [in_vmem] * 2
+    scratch = [
+        pltpu.VMEM((mix.shape[1], tiles.cols), bf16),
+        pltpu.VMEM((tiles.cols, out), bf16),
+        pltpu.SemaphoreType.DMA((n,)),
+    ]
+    if last:
+        args.append(dout)
+        specs.append(in_vmem)
+        shapes = [jax.ShapeDtypeStruct((height // 2, out), f32)] * 2
+        scratch.append(pltpu.VMEM((height, out), f32))
+    else:
+        shapes = [jax.ShapeDtypeStruct((height, out), f32), jax.ShapeDtypeStruct((height, terms), f32)]
+    return pl.pallas_call(
+        functools.partial(hidden_kernel, tiles, dy, dz1, n, width, first, last, rows, scale),
+        out_shape=tuple(shapes),
+        in_specs=specs,
+        out_specs=(in_vmem, in_vmem),
+        scratch_shapes=scratch,
+        compiler_params=pltpu.CompilerParams(vmem_limit_bytes=24 * MiB),
+        cost_estimate=pl.CostEstimate(
+            flops=2 * height * out * tiles.cols,
+            bytes_accessed=2 * out * tiles.cols,
+            transcendentals=height * tiles.cols,
+        ),
+        name=f"hidden_y{dy}_z{dz1}",
+    )(*args)
+
+
+def logit_kernel(keep_ref, recv_ref, x_ref, head_ref, out_ref):
+    p = cube()[0]
+    height, block = keep_ref.shape
+    rows = x_ref.shape[0]
+    x = x_ref[:, pl.ds(pl.multiple_of(p * block, lane), block)].astype(f32)
+    total = keep_ref[...] + recv_ref[...] + jnp.concatenate([x] * (height // rows), axis=0)
+    squares = jnp.sum(total * total, axis=1, keepdims=True)
+    high = total.astype(bf16)
+    rest = (total - high.astype(f32)).astype(bf16)
+    head = head_ref[...]
+    out_ref[0:height, :] = dot_nn(high, head) + dot_nn(rest, head)
+    wide = jnp.concatenate([jnp.broadcast_to(squares, (height, lane)), jnp.zeros((lane - height, lane), f32)], axis=0)
+    out_ref[height : height + 8, :] = wide.T[0:8, :]
+
+
+def part_logits(keep, recv, prompts, head):
+    height = keep.shape[0]
+    return pl.pallas_call(
+        logit_kernel,
+        out_shape=jax.ShapeDtypeStruct((height + 8, lane), f32),
+        in_specs=[in_vmem] * 4,
+        out_specs=in_vmem,
+        compiler_params=pltpu.CompilerParams(vmem_limit_bytes=12 * MiB),
+        name="part_logits",
+    )(keep, recv, prompts, head)
+
+
+def reward_kernel(rows, width, a_ref, b_ref, targets_ref, out_ref):
+    t = lax.axis_index("tensor")
+    height = a_ref.shape[0] - 8
+    total = a_ref[...] + b_ref[...]
+    wide = jnp.concatenate([jnp.broadcast_to(total[height : height + 1, :], (lane, lane))], axis=0).T
+    scale = lax.rsqrt(wide[0:height, :] * (1.0 / width) + norm_eps)
+    logits = total[0:height, :] * scale
+    target = jnp.concatenate([targets_ref[...]] * (height // rows), axis=0)
+    labels = lax.broadcasted_iota(jnp.int32, (height, lane), 1)
+    picked = jnp.sum(jnp.where(target == labels, logits, 0.0), axis=1, keepdims=True)
+    terms = picked - jnp.log(jnp.sum(jnp.exp(logits), axis=1, keepdims=True))
+    here = height // rows
+    place = lax.broadcasted_iota(jnp.int32, (8, lane), 0)
+    out = jnp.zeros((8, lane), f32)
+    for i in range(here):
+        reward = jnp.sum(terms[i * rows : (i + 1) * rows], axis=0, keepdims=True) * (1.0 / rows)
+        out = jnp.where(place == t * here + i, jnp.broadcast_to(reward, (8, lane)), out)
+    out_ref[...] = out
+
+
+def part_rewards(a, b, targets, rows, width):
+    return pl.pallas_call(
+        functools.partial(reward_kernel, rows, width),
+        out_shape=jax.ShapeDtypeStruct((8, lane), f32),
+        in_specs=[in_vmem] * 3,
+        out_specs=in_vmem,
+        compiler_params=pltpu.CompilerParams(vmem_limit_bytes=8 * MiB),
+        name="part_rewards",
+    )(a, b, targets)
+
+
+def update_kernel(n, high, a_ref, b_ref, dif_ref, dout_ref, out_ref, score_ref, buf, sems):
+    p = cube()[0]
+    rewards = a_ref[...] + b_ref[...]
+    centre = jnp.mean(rewards, axis=0, keepdims=True)
+    away = rewards - centre
+    spread = jnp.mean(away * away, axis=0, keepdims=True)
+    scores = away * lax.rsqrt(spread + norm_eps)
+    place = lax.broadcasted_iota(jnp.int32, (8, lane), 0)
+    score_ref[...] = jnp.sum(jnp.where(place == p, scores, 0.0), axis=0, keepdims=True)
+    terms, out = dout_ref.shape
+    rank = terms // 8
+    member = count_steps(lax.broadcasted_iota(jnp.int32, (terms, lane), 0), rank, 8)
+    factor = jnp.zeros((terms, lane), f32)
+    for m in range(8):
+        factor = jnp.where(member == m, jnp.broadcast_to(scores[m : m + 1, :], (terms, lane)), factor)
+    weighted = (factor[:, 0:1] * dout_ref[...].astype(f32)).astype(bf16)
+    scale = 1.0 / math.sqrt(terms)
+    copies = []
+    for c in range(n):
+        span = pl.ds(c * high, high)
+        buf[span, :] = (dot_tn(dif_ref[:, span], weighted) * scale).astype(bf16)
+        copy = pltpu.make_async_copy(buf.at[span, :], out_ref.at[span, :], sems.at[c])
+        copy.start()
+        copies.append(copy)
+    for copy in copies:
+        copy.wait()
+
+
+def updates(a, b, dif, dout):
+    units = dif.shape[1]
+    out = dout.shape[1]
+    n, high = chunks_of(units, 256)
+    return pl.pallas_call(
+        functools.partial(update_kernel, n, high),
+        out_shape=(jax.ShapeDtypeStruct((units, out), bf16), jax.ShapeDtypeStruct((1, lane), f32)),
+        in_specs=[in_vmem] * 4,
+        out_specs=(in_any, in_vmem),
+        scratch_shapes=[pltpu.VMEM((units, out), bf16), pltpu.SemaphoreType.DMA((n,))],
+        compiler_params=pltpu.CompilerParams(vmem_limit_bytes=24 * MiB),
+        name="updates",
+    )(a, b, dif, dout)
+
+
+def cube_body(
+    prompts,
+    gate_weight,
+    up_weight,
+    down_weight_matrix,
+    gate_in,
+    gate_output_factors,
+    up_in,
+    up_output_factors,
+    down_input_factors,
+    down_out,
+    label_head,
+    targets,
+):
+    p = lax.axis_index("pop")
+    t = lax.axis_index("tensor")
+    rows, width = prompts.shape
+    block, units = gate_weight.shape
+    members, _, rank = down_input_factors.shape
+    tiles = Tiles(units)
+    down_scale = noise_scale / math.sqrt(units * lax.axis_size("tensor"))
+    over_y = lambda x: swap(x, "pop", 1, 8)
+    over_z1 = lambda x: swap(x, "pop", 2, 8)
+    over_z2 = lambda x: swap(x, "pop", 4, 8)
+    over_t = lambda x: swap(x, "tensor", 1, 2)
+    turned = lambda x: jnp.swapaxes(x, 1, 2)
+    dif = turned(down_input_factors).reshape(members * rank, units)
+    dout = turned(down_out).reshape(members * rank, block)
+
+    xn, fac = prep(
+        prompts,
+        turned(gate_in)[0],
+        turned(up_in)[0],
+        turned(gate_output_factors)[0],
+        turned(up_output_factors)[0],
+        block,
+    )
+    two = jnp.stack([fac, over_z2(fac)])
+
+    part = functools.partial(base_part, xn, gate_weight, up_weight, tiles)
+    far0 = over_y(part(1, 1, bf16))
+    far1 = over_y(part(1, 0, bf16))
+    four = jnp.concatenate([two, over_z1(two)])
+    near0 = part(0, 1, f32)
+    from_z1 = over_z1((near0 + far0.astype(f32)).astype(bf16))
+    near1 = part(0, 0, f32)
+    far_four = over_y(four)
+    mine = near1 + far1.astype(f32) + from_z1.astype(f32)
+    total = (mine[1] + over_z2(mine[0].astype(bf16)).astype(f32)).astype(bf16)
+
+    head_rows = lax.dynamic_slice_in_dim(label_head, (p * block) % label_head.shape[0], block, 0)
+    head = jnp.where((p * block) // label_head.shape[0] == t, head_rows, over_t(head_rows))
+
+    mix = mixing(four, far_four, rows)
+    step = functools.partial(hidden_step, mix, four, far_four)
+    tail = (down_weight_matrix, dif, tiles)
+    pair = jnp.stack([total, over_z2(total)])
+    pair_z = over_z1(pair)
+    pair_y = over_y(pair)
+    state = step(pair, *tail, 0, 0, rows, down_scale)
+    pair_yz = over_y(pair_z)
+    state = step(pair_z, *tail, 0, 1, rows, down_scale, state)
+    state = step(pair_y, *tail, 1, 0, rows, down_scale, state)
+    send, keep = step(pair_yz, *tail, 1, 1, rows, down_scale, state, dout)
+
+    logits = part_logits(keep, over_t(send), prompts, head)
+    logits = logits + over_y(logits)
+    logits = logits + over_z1(logits)
+    rewards = part_rewards(logits, over_z2(logits), targets.reshape(rows, 1), rows, width)
+    update, score = updates(rewards, over_t(rewards), dif, dout)
+    return (update, score[0, 0:1])
+
+
 def solution(mesh):
     placed = (
         P("groups", None),
@@ -118,8 +586,9 @@
         P("tensor", None),
         P("groups"),
     )
+    on_cube = mesh.shape["pop"] == 8 and mesh.shape["tensor"] == 2
     return jax.shard_map(
-        body,
+        cube_body if on_cube else general_body,
         mesh=mesh,
         in_specs=placed,
         out_specs=(P(("groups", "tensor"), "pop"), P(("groups", "pop"))),

time: 284 us -> 113 us (0.40)
  blocking collectives: 128 us -> 0 us
  waiting for transfers between devices: 75.5 us -> 27.5 us
  Pallas kernels: 0 us -> 33.7 us
  matrix products: 32.3 us -> 0 us
  starting transfers between devices: 0.08 us -> 21.7 us
  between operations: 16.2 us -> 1.09 us
  other arithmetic: 5.78 us -> 1.3 us
    psum x2 -> x0, blocking collectives: 82.7 us -> none  [the longest x1 79.3 us: body(): total_gate, total_up = lax.psum((part_gate, part_up), 'pop')]
    all_gather x1 -> x0, waiting for transfers between devices: 57.8 us -> none  [body(): hidden_portion = lax.all_gather(hidden_state, 'pop', axis=0, tiled=True)]
    pallas_call x0 -> x13, Pallas kernels: none -> 33.7 us  [the longest x4 13.9 us: base_part(): pl.pallas_call(functools.partial(base_kernel, tiles, dy, dz1, n, width),...]
    dot_general x9 -> x0, matrix products: 32.3 us -> none  [the longest x1 7.97 us: body(): jnp.einsum('mfk,mdk->fd', down_input_factors, weighted, preferred_element...]
    ppermute x0 -> x17, waiting for transfers between devices: none -> 27.5 us  [swap(): return lax.ppermute(x, axis, [(i, i ^ bit) for i in range(size)])]
    all_to_all x1 -> x0, blocking collectives: 23.2 us -> none  [body(): lax.all_to_all(partial_rows, 'pop', split_axis=0, concat_axis=2, tiled=True)]
    unnamed x1 -> x0, blocking collectives: 21.9 us -> none
    ppermute x0 -> x17, starting transfers between devices: none -> 21.7 us  [swap(): return lax.ppermute(x, axis, [(i, i ^ bit) for i in range(size)])]
  transfers between devices with their start and end apart: 2 -> 17, of which waited for: 2 -> 10; matrix products, arithmetic and copies ran while one was open for 0% -> 2% of each run, Pallas kernels for 0% -> 20%
where the time goes in v1:
time: 113 us; the launch traced here: 112 us
  Pallas kernels  33.7 us (30%)
  waiting for transfers between devices  27.5 us (24%)
  local copies, waits for them, and re-layouts  26.8 us (24%)
  starting transfers between devices  21.7 us (19%)
  other arithmetic  1.3 us (1%)
    ppermute x17, waiting for transfers between devices, swap(): return lax.ppermute(x, axis, [(i, i ^ bit) for i in range(size)])  27.5 us
    unnamed x26, local copies, waits for them, and re-layouts  25.6 us
    ppermute x17, starting transfers between devices, swap(): return lax.ppermute(x, axis, [(i, i ^ bit) for i in range(size)])  21.7 us
    pallas_call x4, Pallas kernels, base_part(): pl.pallas_call(functools.partial(base_kernel, tiles, dy, dz1, n, width),...  13.9 us
    pallas_call x4, Pallas kernels, hidden_step(): pl.pallas_call(functools.partial(hidden_kernel, tiles, dy, dz1, n, width,...  12.1 us
    pallas_call x1, Pallas kernels, updates(): pl.pallas_call(functools.partial(update_kernel, n, high), out_shape=(jax....  6.46 us
  transfers between devices with their start and end apart: 17, of which 10 were waited for; matrix products, arithmetic and copies ran while one was open for 2% of the time, Pallas kernels for 20%

profile of v1, /device:TPU:0, one launch (start us, length us, event | category | flops | bytes accessed | tf_op | source)
XLA Modules:
  0.0 112.1 jit_solution(14305343027596441530)
XLA Ops:
  0.6 1.0 copy-done.4
  1.6 0.8 copy-done.6
  2.5 0.8 copy-done.7
  3.3 0.8 copy-done.8
  4.1 0.8 copy-done.9
  5.0 0.6 prep.1
  5.6 5.3 %copy-done = bf16[1024,7424]{1,0:T(8,128)(2,1)S(1)} copy-done((bf16[1024,7424]{1,0:T(8,128)(2,1)S(1)}, bf16[1024,7424]{1,0:T(8,128)(2,1)}, u32[]{:S(2)}) %copy-start) | copy-done | bytes 15204376
  10.9 5.3 %copy-done.1 = bf16[1024,7424]{1,0:T(8,128)(2,1)S(1)} copy-done((bf16[1024,7424]{1,0:T(8,128)(2,1)S(1)}, bf16[1024,7424]{1,0:T(8,128)(2,1)}, u32[]{:S(2)}) %copy-start.1) | copy-done | bytes 15204376
  16.2 3.5 %base_y1_z1.1 = bf16[2,24,1920]{2,1,0:T(8,128)(2,1)S(1)} custom-call(bf16[24,1024]{1,0:T(8,128)(2,1)S(1)} %get-tuple-element.15.xn_ref, bf16[1024,7424]{1,0:T(8,128)(2,1)S(1)} %copy-done, bf16[1024,7424]{1,0:T(8,128)(2,1)S(1)} %copy-done.1), custom_call_target="tpu_custom_call" | custom-call | flops 188743680 | bytes 7864320 | tf_op jit(solution)/shard_map/base_y1_z1/pallas_call | solution.py:221
  19.7 3.0 %collective-permute-start.4 = (bf16[2,24,1920]{2,1,0:T(8,128)(2,1)S(1)}, bf16[2,24,1920]{2,1,0:T(8,128)(2,1)S(1)}, u32[]{:S(2)}, u32[]{:S(2)}) collective-permute-start(bf16[2,24,1920]{2,1,0:T(8,128)(2,1)S(1)} %base_y1_z1.1), channel_id=1, source_target_pairs={{0,2},{2,0},{4,6},{6,4},{8,10},{10,8},{12,14},{14,12},{1,3},{3,1},... | collective-permute-start | bytes 552968 | tf_op jit(solution)/shard_map/ppermute | solution.py:153
  22.7 3.5 %base_y1_z0.1 = bf16[2,24,1920]{2,1,0:T(8,128)(2,1)S(1)} custom-call(bf16[24,1024]{1,0:T(8,128)(2,1)S(1)} %get-tuple-element.15.xn_ref, bf16[1024,7424]{1,0:T(8,128)(2,1)S(1)} %copy-done, bf16[1024,7424]{1,0:T(8,128)(2,1)S(1)} %copy-done.1), custom_call_target="tpu_custom_call" | custom-call | flops 188743680 | bytes 7864320 | tf_op jit(solution)/shard_map/base_y1_z0/pallas_call | solution.py:221
  26.3 3.5 %base_y0_z1.1 = f32[2,24,1920]{2,1,0:T(8,128)S(1)} custom-call(bf16[24,1024]{1,0:T(8,128)(2,1)S(1)} %get-tuple-element.15.xn_ref, bf16[1024,7424]{1,0:T(8,128)(2,1)S(1)} %copy-done, bf16[1024,7424]{1,0:T(8,128)(2,1)S(1)} %copy-done.1), custom_call_target="tpu_custom_call" | custom-call | flops 188743680 | bytes 7864320 | tf_op jit(solution)/shard_map/base_y0_z1/pallas_call | solution.py:221
  29.8 2.1 %collective-permute-start.5 = (bf16[2,24,1920]{2,1,0:T(8,128)(2,1)S(1)}, bf16[2,24,1920]{2,1,0:T(8,128)(2,1)S(1)}, u32[]{:S(2)}, u32[]{:S(2)}) collective-permute-start(bf16[2,24,1920]{2,1,0:T(8,128)(2,1)S(1)} %add_convert_fusion), channel_id=1, source_target_pairs={{0,4},{2,6},{4,0},{6,2},{8,12},{10,14},{12,8},{14,10},{1,5},{3,7},... | collective-permute-start | bytes 552968 | tf_op jit(solution)/shard_map/ppermute | solution.py:153
  31.9 2.6 %collective-permute-start = (bf16[8,7552]{1,0:T(8,128)(2,1)S(1)}, bf16[8,7552]{1,0:T(8,128)(2,1)S(1)}, u32[]{:S(2)}, u32[]{:S(2)}) collective-permute-start(bf16[8,7552]{1,0:T(8,128)(2,1)S(1)} %get-tuple-element.14), channel_id=1, source_target_pairs={{0,8},{2,10},{4,12},{6,14},{8,0},{10,2},{12,4},{14,6},{1,9},{3,11}... | collective-permute-start | bytes 362504 | tf_op jit(solution)/shard_map/ppermute | solution.py:153
  34.5 3.5 %base_y0_z0.1 = f32[2,24,1920]{2,1,0:T(8,128)S(1)} custom-call(bf16[24,1024]{1,0:T(8,128)(2,1)S(1)} %get-tuple-element.15.xn_ref, bf16[1024,7424]{1,0:T(8,128)(2,1)S(1)} %copy-done, bf16[1024,7424]{1,0:T(8,128)(2,1)S(1)} %copy-done.1), custom_call_target="tpu_custom_call" | custom-call | flops 188743680 | bytes 7864320 | tf_op jit(solution)/shard_map/base_y0_z0/pallas_call | solution.py:221
  38.0 0.2 collective-permute-done.5
  38.3 2.3 %collective-permute-start.6 = (bf16[24,1920]{1,0:T(8,128)(2,1)S(1)}, bf16[24,1920]{1,0:T(8,128)(2,1)S(1)}, u32[]{:S(2)}, u32[]{:S(2)}) collective-permute-start(bf16[24,1920]{1,0:T(8,128)(2,1)S(1)} %fusion.2), channel_id=1, source_target_pairs={{0,8},{2,10},{4,12},{6,14},{8,0},{10,2},{12,4},{14,6},{1,9},{3,11}... | collective-permute-start | bytes 276488 | tf_op jit(solution)/shard_map/ppermute | solution.py:153
  40.7 2.4 %collective-permute-start.1 = (bf16[2,8,7552]{2,1,0:T(8,128)(2,1)S(1)}, bf16[2,8,7552]{2,1,0:T(8,128)(2,1)S(1)}, u32[]{:S(2)}, u32[]{:S(2)}) collective-permute-start(bf16[2,8,7552]{2,1,0:T(8,128)(2,1)S(1)} %pad_maximum_fusion.1), channel_id=1, source_target_pairs={{0,4},{2,6},{4,0},{6,2},{8,12},{10,14},{12,8},{14,10},{1,5},{3,7},... | collective-permute-start | bytes 725000 | tf_op jit(solution)/shard_map/ppermute | solution.py:153
  43.2 1.1 %collective-permute-done.6 = bf16[24,1920]{1,0:T(8,128)(2,1)S(1)} collective-permute-done((bf16[24,1920]{1,0:T(8,128)(2,1)S(1)}, bf16[24,1920]{1,0:T(8,128)(2,1)S(1)}, u32[]{:S(2)}, u32[]{:S(2)}) %collective-permute-start.6) | collective-permute-done | bytes 92192 | tf_op jit(solution)/shard_map/ppermute | solution.py:153
  44.3 2.8 %collective-permute-start.7 = (bf16[24,1920]{1,0:T(8,128)(2,1)S(1)}, bf16[24,1920]{1,0:T(8,128)(2,1)S(1)}, u32[]{:S(2)}, u32[]{:S(2)}) collective-permute-start(bf16[24,1920]{1,0:T(8,128)(2,1)S(1)} %fusion.1), channel_id=1, source_target_pairs={{0,8},{2,10},{4,12},{6,14},{8,0},{10,2},{12,4},{14,6},{1,9},{3,11}... | collective-permute-start | bytes 276488 | tf_op jit(solution)/shard_map/ppermute | solution.py:153
  47.1 3.6 %collective-permute-done.1 = bf16[2,8,7552]{2,1,0:T(8,128)(2,1)S(1)} collective-permute-done((bf16[2,8,7552]{2,1,0:T(8,128)(2,1)S(1)}, bf16[2,8,7552]{2,1,0:T(8,128)(2,1)S(1)}, u32[]{:S(2)}, u32[]{:S(2)}) %collective-permute-start.1) | collective-permute-done | bytes 241696 | tf_op jit(solution)/shard_map/ppermute | solution.py:153
  50.8 1.6 %collective-permute-start.2 = (bf16[4,8,7552]{2,1,0:T(8,128)(2,1)S(1)}, bf16[4,8,7552]{2,1,0:T(8,128)(2,1)S(1)}, u32[]{:S(2)}, u32[]{:S(2)}) collective-permute-start(bf16[4,8,7552]{2,1,0:T(8,128)(2,1)S(1)} %pad_maximum_fusion.near_ref), channel_id=1, source_target_pairs={{0,2},{2,0},{4,6},{6,4},{8,10},{10,8},{12,14},{14,12},{1,3},{3,1},... | collective-permute-start | bytes 1449992 | tf_op jit(solution)/shard_map/ppermute | solution.py:153
  52.4 0.7 collective-permute-start.8
  53.1 0.7 collective-permute-start.10
  53.9 1.0 constant_dynamic-slice_fusion
  55.0 0.1 reshape.14.dif_ref
  55.1 2.9 %collective-permute-done.8.pair_ref = bf16[2,24,1920]{2,1,0:T(8,128)(2,1)S(1)} collective-permute-done((bf16[2,24,1920]{2,1,0:T(8,128)(2,1)S(1)}, bf16[2,24,1920]{2,1,0:T(8,128)(2,1)S(1)}, u32[]{:S(2)}, u32[]{:S(2)}) %collective-permute-start.8) | collective-permute-done | bytes 184352 | tf_op jit(solution)/shard_map/ppermute | solution.py:153
  58.0 0.5 collective-permute-start.9
  58.5 6.3 %collective-permute-done.2.far_ref = bf16[4,8,7552]{2,1,0:T(8,128)(2,1)S(1)} collective-permute-done((bf16[4,8,7552]{2,1,0:T(8,128)(2,1)S(1)}, bf16[4,8,7552]{2,1,0:T(8,128)(2,1)S(1)}, u32[]{:S(2)}, u32[]{:S(2)}) %collective-permute-start.2) | collective-permute-done | bytes 483360 | tf_op jit(solution)/shard_map/ppermute | solution.py:153
  64.8 0.2 mixing.1.mix_ref
  65.0 5.3 %copy-done.2 = bf16[7424,1024]{1,0:T(8,128)(2,1)S(1)} copy-done((bf16[7424,1024]{1,0:T(8,128)(2,1)S(1)}, bf16[7424,1024]{1,0:T(8,128)(2,1)}, u32[]{:S(2)}) %copy-start.2) | copy-done | bytes 15204376
  70.4 2.7 %hidden_y0_z0.1 = (f32[192,1024]{1,0:T(8,128)S(1)}, f32[192,32]{1,0:T(8,128)S(1)}) custom-call(bf16[384,112]{1,0:T(8,128)(2,1)S(1)} %mixing.1.mix_ref, bf16[4,8,7552]{2,1,0:T(8,128)(2,1)S(1)} %pad_maximum_fusion.near_ref, bf16[4,8,7552]{2,1,0:T(8,128)(2,1)S(1)} %collective-permute-done.2.far_ref, bf16[2,24,1920]{2,1,0:T(8,128)(2,1)S(1)} %pad_maximum_fusion.2.pair_ref, ...), custom_call_target="tpu_custom_call" | custom-call | flops 754974720 | bytes 3932160 | tf_op jit(solution)/shard_map/hidden_y0_z0/pallas_call | solution.py:384
  73.1 5.3 %copy-done.3 = bf16[7424,1024]{1,0:T(8,128)(2,1)S(1)} copy-done((bf16[7424,1024]{1,0:T(8,128)(2,1)S(1)}, bf16[7424,1024]{1,0:T(8,128)(2,1)}, u32[]{:S(2)}) %copy-start.3) | copy-done | bytes 15204376
  78.4 3.0 %hidden_y0_z1.1 = (f32[192,1024]{1,0:T(8,128)S(1)}, f32[192,32]{1,0:T(8,128)S(1)}) custom-call(bf16[384,112]{1,0:T(8,128)(2,1)S(1)} %mixing.1.mix_ref, bf16[4,8,7552]{2,1,0:T(8,128)(2,1)S(1)} %pad_maximum_fusion.near_ref, bf16[4,8,7552]{2,1,0:T(8,128)(2,1)S(1)} %collective-permute-done.2.far_ref, bf16[2,24,1920]{2,1,0:T(8,128)(2,1)S(1)} %collective-permute-done.8.pair_ref, ...), custom_call_target="tpu_custom_call" | custom-call | flops 754974720 | bytes 3932160 | tf_op jit(solution)/shard_map/hidden_y0_z1/pallas_call | solution.py:384
  81.5 2.9 %hidden_y1_z0.1 = (f32[192,1024]{1,0:T(8,128)S(1)}, f32[192,32]{1,0:T(8,128)S(1)}) custom-call(bf16[384,112]{1,0:T(8,128)(2,1)S(1)} %mixing.1.mix_ref, bf16[4,8,7552]{2,1,0:T(8,128)(2,1)S(1)} %pad_maximum_fusion.near_ref, bf16[4,8,7552]{2,1,0:T(8,128)(2,1)S(1)} %collective-permute-done.2.far_ref, bf16[2,24,1920]{2,1,0:T(8,128)(2,1)S(1)} %collective-permute-done.10.pair_ref, ...), custom_call_target="tpu_custom_call" | custom-call | flops 754974720 | bytes 3932160 | tf_op jit(solution)/shard_map/hidden_y1_z0/pallas_call | solution.py:384
  84.3 3.5 %hidden_y1_z1.1 = (f32[96,1024]{1,0:T(8,128)S(1)}, f32[96,1024]{1,0:T(8,128)S(1)}) custom-call(bf16[384,112]{1,0:T(8,128)(2,1)S(1)} %mixing.1.mix_ref, bf16[4,8,7552]{2,1,0:T(8,128)(2,1)S(1)} %pad_maximum_fusion.near_ref, bf16[4,8,7552]{2,1,0:T(8,128)(2,1)S(1)} %collective-permute-done.2.far_ref, bf16[2,24,1920]{2,1,0:T(8,128)(2,1)S(1)} %collective-permute-done.9.pair_ref, ...), custom_call_target="tpu_custom_call" | custom-call | flops 754974720 | bytes 3932160 | tf_op jit(solution)/shard_map/hidden_y1_z1/pallas_call | solution.py:384
  88.0 1.0 broadcast_select_fusion.head_ref
  89.0 0.6 collective-permute-done.11.recv_ref
  89.7 0.3 part_logits.1
  90.0 1.6 %collective-permute-start.13 = (f32[104,128]{1,0:T(8,128)S(1)}, f32[104,128]{1,0:T(8,128)S(1)}, u32[]{:S(2)}, u32[]{:S(2)}) collective-permute-start(f32[104,128]{1,0:T(8,128)S(1)} %part_logits.1), channel_id=1, source_target_pairs={{0,2},{2,0},{4,6},{6,4},{8,10},{10,8},{12,14},{14,12},{1,3},{3,1},... | collective-permute-start | bytes 159752 | tf_op jit(solution)/shard_map/ppermute | solution.py:153
  91.6 2.6 %collective-permute-done.13 = f32[104,128]{1,0:T(8,128)S(1)} collective-permute-done((f32[104,128]{1,0:T(8,128)S(1)}, f32[104,128]{1,0:T(8,128)S(1)}, u32[]{:S(2)}, u32[]{:S(2)}) %collective-permute-start.13) | collective-permute-done | bytes 53280 | tf_op jit(solution)/shard_map/ppermute | solution.py:153
  94.2 0.7 collective-permute-start.14
  94.9 3.5 %collective-permute-done.14 = f32[104,128]{1,0:T(8,128)S(1)} collective-permute-done((f32[104,128]{1,0:T(8,128)S(1)}, f32[104,128]{1,0:T(8,128)S(1)}, u32[]{:S(2)}, u32[]{:S(2)}) %collective-permute-start.14) | collective-permute-done | bytes 53280 | tf_op jit(solution)/shard_map/ppermute | solution.py:153
  98.4 0.2 collective-permute-start.15
  98.7 5.3 %collective-permute-done.15.b_ref = f32[104,128]{1,0:T(8,128)S(1)} collective-permute-done((f32[104,128]{1,0:T(8,128)S(1)}, f32[104,128]{1,0:T(8,128)S(1)}, u32[]{:S(2)}, u32[]{:S(2)}) %collective-permute-start.15) | collective-permute-done | bytes 53280 | tf_op jit(solution)/shard_map/ppermute | solution.py:153
  104.1 0.2 part_rewards.1.a_ref
  104.4 1.2 %collective-permute-done.16.b_ref = f32[8,128]{1,0:T(8,128)S(1)} collective-permute-done((f32[8,128]{1,0:T(8,128)S(1)}, f32[8,128]{1,0:T(8,128)S(1)}, u32[]{:S(2)}, u32[]{:S(2)}) %collective-permute-start.16) | collective-permute-done | bytes 4128 | tf_op jit(solution)/shard_map/ppermute | solution.py:153
  105.5 6.5 %updates.1 = (bf16[7424,1024]{1,0:T(8,128)(2,1)}, f32[1,128]{1,0:T(1,128)}) custom-call(f32[8,128]{1,0:T(8,128)S(1)} %part_rewards.1.a_ref, f32[8,128]{1,0:T(8,128)S(1)} %collective-permute-done.16.b_ref, bf16[32,7424]{1,0:T(8,128)(2,1)S(1)} %reshape.14.dif_ref, bf16[32,1024]{1,0:T(8,128)(2,1)S(1)} %reshape.15.rest_2_.dout_ref), custom_call_target="tpu_custom_call" | custom-call | tf_op jit(solution)/shard_map/updates/pallas_call | solution.py:490
  (39 shorter events, 0.8 us)
Async XLA Ops:
  0.6 1.0 copy-start.4
  1.6 0.8 copy-start.6
  2.5 0.8 copy-start.7
  3.3 0.8 copy-start.8
  4.1 0.8 copy-start.9
  5.6 5.3 %copy-start = (bf16[1024,7424]{1,0:T(8,128)(2,1)S(1)}, bf16[1024,7424]{1,0:T(8,128)(2,1)}, u32[]{:S(2)}) copy-start(bf16[1024,7424]{1,0:T(8,128)(2,1)} %wg_ref.7) | copy-start | bytes 45613060
  10.9 5.3 %copy-start.1 = (bf16[1024,7424]{1,0:T(8,128)(2,1)S(1)}, bf16[1024,7424]{1,0:T(8,128)(2,1)}, u32[]{:S(2)}) copy-start(bf16[1024,7424]{1,0:T(8,128)(2,1)} %wu_ref.7) | copy-start | bytes 45613060
  19.7 10.1 %collective-permute-start.4 = (bf16[2,24,1920]{2,1,0:T(8,128)(2,1)S(1)}, bf16[2,24,1920]{2,1,0:T(8,128)(2,1)S(1)}, u32[]{:S(2)}, u32[]{:S(2)}) collective-permute-start(bf16[2,24,1920]{2,1,0:T(8,128)(2,1)S(1)} %base_y1_z1.1), channel_id=1, source_target_pairs={{0,2},{2,0},{4,6},{6,4},{8,10},{10,8},{12,14},{14,12},{1,3},{3,1},... | collective-permute-start | bytes 552968 | tf_op jit(solution)/shard_map/ppermute | solution.py:153
  26.2 11.8 %collective-permute-start.3 = (bf16[2,24,1920]{2,1,0:T(8,128)(2,1)S(1)}, bf16[2,24,1920]{2,1,0:T(8,128)(2,1)S(1)}, u32[]{:S(2)}, u32[]{:S(2)}) collective-permute-start(bf16[2,24,1920]{2,1,0:T(8,128)(2,1)S(1)} %base_y1_z0.1), channel_id=1, source_target_pairs={{0,2},{2,0},{4,6},{6,4},{8,10},{10,8},{12,14},{14,12},{1,3},{3,1},... | collective-permute-start | bytes 552968 | tf_op jit(solution)/shard_map/ppermute | solution.py:153
  29.8 8.4 %collective-permute-start.5 = (bf16[2,24,1920]{2,1,0:T(8,128)(2,1)S(1)}, bf16[2,24,1920]{2,1,0:T(8,128)(2,1)S(1)}, u32[]{:S(2)}, u32[]{:S(2)}) collective-permute-start(bf16[2,24,1920]{2,1,0:T(8,128)(2,1)S(1)} %add_convert_fusion), channel_id=1, source_target_pairs={{0,4},{2,6},{4,0},{6,2},{8,12},{10,14},{12,8},{14,10},{1,5},{3,7},... | collective-permute-start | bytes 552968 | tf_op jit(solution)/shard_map/ppermute | solution.py:153
  31.9 23.0 %copy-start.11 = (bf16[8,1024,4]{1,2,0:T(4,128)(2,1)S(1)}, bf16[8,1024,4]{1,2,0:T(4,128)(2,1)}, u32[]{:S(2)}) copy-start(bf16[8,1024,4]{1,2,0:T(4,128)(2,1)} %param.21) | copy-start | bytes 196612
  31.9 23.0 %copy-start.10 = (bf16[8,7424,4]{1,2,0:T(4,128)(2,1)S(1)}, bf16[8,7424,4]{1,2,0:T(4,128)(2,1)}, u32[]{:S(2)}) copy-start(bf16[8,7424,4]{1,2,0:T(4,128)(2,1)} %param.20) | copy-start | bytes 1425412
  31.9 8.8 %collective-permute-start = (bf16[8,7552]{1,0:T(8,128)(2,1)S(1)}, bf16[8,7552]{1,0:T(8,128)(2,1)S(1)}, u32[]{:S(2)}, u32[]{:S(2)}) collective-permute-start(bf16[8,7552]{1,0:T(8,128)(2,1)S(1)} %get-tuple-element.14), channel_id=1, source_target_pairs={{0,8},{2,10},{4,12},{6,14},{8,0},{10,2},{12,4},{14,6},{1,9},{3,11}... | collective-permute-start | bytes 362504 | tf_op jit(solution)/shard_map/ppermute | solution.py:153
  38.3 6.0 %collective-permute-start.6 = (bf16[24,1920]{1,0:T(8,128)(2,1)S(1)}, bf16[24,1920]{1,0:T(8,128)(2,1)S(1)}, u32[]{:S(2)}, u32[]{:S(2)}) collective-permute-start(bf16[24,1920]{1,0:T(8,128)(2,1)S(1)} %fusion.2), channel_id=1, source_target_pairs={{0,8},{2,10},{4,12},{6,14},{8,0},{10,2},{12,4},{14,6},{1,9},{3,11}... | collective-permute-start | bytes 276488 | tf_op jit(solution)/shard_map/ppermute | solution.py:153
  40.7 10.0 %collective-permute-start.1 = (bf16[2,8,7552]{2,1,0:T(8,128)(2,1)S(1)}, bf16[2,8,7552]{2,1,0:T(8,128)(2,1)S(1)}, u32[]{:S(2)}, u32[]{:S(2)}) collective-permute-start(bf16[2,8,7552]{2,1,0:T(8,128)(2,1)S(1)} %pad_maximum_fusion.1), channel_id=1, source_target_pairs={{0,4},{2,6},{4,0},{6,2},{8,12},{10,14},{12,8},{14,10},{1,5},{3,7},... | collective-permute-start | bytes 725000 | tf_op jit(solution)/shard_map/ppermute | solution.py:153
  44.3 8.1 %collective-permute-start.7 = (bf16[24,1920]{1,0:T(8,128)(2,1)S(1)}, bf16[24,1920]{1,0:T(8,128)(2,1)S(1)}, u32[]{:S(2)}, u32[]{:S(2)}) collective-permute-start(bf16[24,1920]{1,0:T(8,128)(2,1)S(1)} %fusion.1), channel_id=1, source_target_pairs={{0,8},{2,10},{4,12},{6,14},{8,0},{10,2},{12,4},{14,6},{1,9},{3,11}... | collective-permute-start | bytes 276488 | tf_op jit(solution)/shard_map/ppermute | solution.py:153
  50.8 14.0 %collective-permute-start.2 = (bf16[4,8,7552]{2,1,0:T(8,128)(2,1)S(1)}, bf16[4,8,7552]{2,1,0:T(8,128)(2,1)S(1)}, u32[]{:S(2)}, u32[]{:S(2)}) collective-permute-start(bf16[4,8,7552]{2,1,0:T(8,128)(2,1)S(1)} %pad_maximum_fusion.near_ref), channel_id=1, source_target_pairs={{0,2},{2,0},{4,6},{6,4},{8,10},{10,8},{12,14},{14,12},{1,3},{3,1},... | collective-permute-start | bytes 1449992 | tf_op jit(solution)/shard_map/ppermute | solution.py:153
  52.4 5.6 %collective-permute-start.8 = (bf16[2,24,1920]{2,1,0:T(8,128)(2,1)S(1)}, bf16[2,24,1920]{2,1,0:T(8,128)(2,1)S(1)}, u32[]{:S(2)}, u32[]{:S(2)}) collective-permute-start(bf16[2,24,1920]{2,1,0:T(8,128)(2,1)S(1)} %pad_maximum_fusion.2.pair_ref), channel_id=1, source_target_pairs={{0,4},{2,6},{4,0},{6,2},{8,12},{10,14},{12,8},{14,10},{1,5},{3,7},... | collective-permute-start | bytes 552968 | tf_op jit(solution)/shard_map/ppermute | solution.py:153
  53.1 28.3 %collective-permute-start.10 = (bf16[2,24,1920]{2,1,0:T(8,128)(2,1)S(1)}, bf16[2,24,1920]{2,1,0:T(8,128)(2,1)S(1)}, u32[]{:S(2)}, u32[]{:S(2)}) collective-permute-start(bf16[2,24,1920]{2,1,0:T(8,128)(2,1)S(1)} %pad_maximum_fusion.2.pair_ref), channel_id=1, source_target_pairs={{0,2},{2,0},{4,6},{6,4},{8,10},{10,8},{12,14},{14,12},{1,3},{3,1},... | collective-permute-start | bytes 552968 | tf_op jit(solution)/shard_map/ppermute | solution.py:153
  54.8 33.2 %collective-permute-start.12 = (bf16[1024,128]{1,0:T(8,128)(2,1)S(1)}, bf16[1024,128]{1,0:T(8,128)(2,1)}, u32[]{:S(2)}, u32[]{:S(2)}) collective-permute-start(bf16[1024,128]{1,0:T(8,128)(2,1)S(1)} %constant_dynamic-slice_fusion), channel_id=1, source_target_pairs={{0,1},{1,0},{2,3},{3,2},{4,5},{5,4},{6,7},{7,6},{8,9},{9,8},{10,11... | collective-permute-start | bytes 786440 | tf_op jit(solution)/shard_map/ppermute | solution.py:153
  58.0 26.3 %collective-permute-start.9 = (bf16[2,24,1920]{2,1,0:T(8,128)(2,1)S(1)}, bf16[2,24,1920]{2,1,0:T(8,128)(2,1)S(1)}, u32[]{:S(2)}, u32[]{:S(2)}) collective-permute-start(bf16[2,24,1920]{2,1,0:T(8,128)(2,1)S(1)} %collective-permute-done.8.pair_ref), channel_id=1, source_target_pairs={{0,2},{2,0},{4,6},{6,4},{8,10},{10,8},{12,14},{14,12},{1,3},{3,1},... | collective-permute-start | bytes 552968 | tf_op jit(solution)/shard_map/ppermute | solution.py:153
  65.0 5.3 %copy-start.2 = (bf16[7424,1024]{1,0:T(8,128)(2,1)S(1)}, bf16[7424,1024]{1,0:T(8,128)(2,1)}, u32[]{:S(2)}) copy-start(bf16[7424,1024]{1,0:T(8,128)(2,1)} %wd_ref.7) | copy-start | bytes 45613060
  73.1 5.3 %copy-start.3 = (bf16[7424,1024]{1,0:T(8,128)(2,1)S(1)}, bf16[7424,1024]{1,0:T(8,128)(2,1)}, u32[]{:S(2)}) copy-start(bf16[7424,1024]{1,0:T(8,128)(2,1)} %wd_ref.7) | copy-start | bytes 45613060
  81.4 8.2 %copy-start.5 = (bf16[24,8192]{1,0:T(8,128)(2,1)S(1)}, bf16[24,8192]{1,0:T(8,128)(2,1)}, u32[]{:S(2)}) copy-start(bf16[24,8192]{1,0:T(8,128)(2,1)} %x_ref.3) | copy-start | bytes 1179652
  81.5 17.2 %copy-start.12 = (s32[24]{0:T(128)S(1)}, s32[24]{0:T(128)}, u32[]{:S(2)}) copy-start(s32[24]{0:T(128)} %param.23) | copy-start | bytes 292
  87.9 1.8 %collective-permute-start.11 = (f32[96,1024]{1,0:T(8,128)S(1)}, f32[96,1024]{1,0:T(8,128)S(1)}, u32[]{:S(2)}, u32[]{:S(2)}) collective-permute-start(f32[96,1024]{1,0:T(8,128)S(1)} %get-tuple-element.23), channel_id=1, source_target_pairs={{0,1},{1,0},{2,3},{3,2},{4,5},{5,4},{6,7},{7,6},{8,9},{9,8},{10,11... | collective-permute-start | bytes 1179656 | tf_op jit(solution)/shard_map/ppermute | solution.py:153
  90.0 4.2 %collective-permute-start.13 = (f32[104,128]{1,0:T(8,128)S(1)}, f32[104,128]{1,0:T(8,128)S(1)}, u32[]{:S(2)}, u32[]{:S(2)}) collective-permute-start(f32[104,128]{1,0:T(8,128)S(1)} %part_logits.1), channel_id=1, source_target_pairs={{0,2},{2,0},{4,6},{6,4},{8,10},{10,8},{12,14},{14,12},{1,3},{3,1},... | collective-permute-start | bytes 159752 | tf_op jit(solution)/shard_map/ppermute | solution.py:153
  94.2 4.2 %collective-permute-start.14 = (f32[104,128]{1,0:T(8,128)S(1)}, f32[104,128]{1,0:T(8,128)S(1)}, u32[]{:S(2)}, u32[]{:S(2)}) collective-permute-start(f32[104,128]{1,0:T(8,128)S(1)} %add.32), channel_id=1, source_target_pairs={{0,4},{2,6},{4,0},{6,2},{8,12},{10,14},{12,8},{14,10},{1,5},{3,7},... | collective-permute-start | bytes 159752 | tf_op jit(solution)/shard_map/ppermute | solution.py:153
  98.4 5.7 %collective-permute-start.15 = (f32[104,128]{1,0:T(8,128)S(1)}, f32[104,128]{1,0:T(8,128)S(1)}, u32[]{:S(2)}, u32[]{:S(2)}) collective-permute-start(f32[104,128]{1,0:T(8,128)S(1)} %add.33.a_ref), channel_id=1, source_target_pairs={{0,8},{2,10},{4,12},{6,14},{8,0},{10,2},{12,4},{14,6},{1,9},{3,11}... | collective-permute-start | bytes 159752 | tf_op jit(solution)/shard_map/ppermute | solution.py:153
  104.3 1.2 %collective-permute-start.16 = (f32[8,128]{1,0:T(8,128)S(1)}, f32[8,128]{1,0:T(8,128)S(1)}, u32[]{:S(2)}, u32[]{:S(2)}) collective-permute-start(f32[8,128]{1,0:T(8,128)S(1)} %part_rewards.1.a_ref), channel_id=1, source_target_pairs={{0,1},{1,0},{2,3},{3,2},{4,5},{5,4},{6,7},{7,6},{8,9},{9,8},{10,11... | collective-permute-start | bytes 12296 | tf_op jit(solution)/shard_map/ppermute | solution.py:153

commit v2 on v1

--- a/solution.py
+++ b/solution.py
@@ -14,8 +14,9 @@
 bf16 = jnp.bfloat16
 f32 = jnp.float32
 MiB = 1 << 20
+small_cost = pl.CostEstimate(flops=1024, bytes_accessed=1024, transcendentals=0)
 in_vmem = pl.BlockSpec(memory_space=pltpu.VMEM)
-in_any = pl.BlockSpec(memory_space=pl.ANY)
+in_hbm = pl.BlockSpec(memory_space=pltpu.HBM)
 
 
 def dot_nn(a, b, **kw):
@@ -153,11 +154,10 @@
     return lax.ppermute(x, axis, [(i, i ^ bit) for i in range(size)])
 
 
-def prep_kernel(x_ref, gin_ref, uin_ref, gof_ref, uof_ref, xn_ref, fac_ref, norm_ref, fac32, low32):
+def prep_steps(x_ref, gin_ref, uin_ref, gof_ref, uof_ref, xn_ref, fac_ref, norm_ref, fac32, low32):
     p = cube()[0]
     rows, width = x_ref.shape
-    units = gof_ref.shape[1]
-    rank = gof_ref.shape[0]
+    rank, units = gof_ref.shape
     block = xn_ref.shape[1]
     x = x_ref[...].astype(f32)
     normed = scaled_rows(x).astype(bf16)
@@ -173,46 +173,82 @@
     fac_ref[:, units : units + lane] = low32[...].astype(bf16)
 
 
-def prep(prompts, gin, uin, gof, uof, block):
-    rows, width = prompts.shape
-    rank, units = gof.shape
-    return pl.pallas_call(
-        prep_kernel,
-        out_shape=(
-            jax.ShapeDtypeStruct((rows, block), bf16),
-            jax.ShapeDtypeStruct((2 * rank, units + lane), bf16),
-        ),
-        in_specs=[in_vmem] * 5,
-        out_specs=(in_vmem, in_vmem),
-        scratch_shapes=[
-            pltpu.VMEM((rows, width), bf16),
-            pltpu.VMEM((2 * rank, units), f32),
-            pltpu.VMEM((2 * rank, lane), f32),
-        ],
-        compiler_params=pltpu.CompilerParams(vmem_limit_bytes=16 * MiB),
-        name="prep",
-    )(prompts, gin, uin, gof, uof)
-
-
-def base_kernel(tiles, dy, dz1, n, width, xn_ref, wg_ref, wu_ref, out_ref, wg, wu, sems):
+def weight_copies(tiles, dy, dz1, n, width, wg_ref, wu_ref, wg, wu, sems):
     p, y, z1, z2 = cube()
     at = tiles.start(y ^ dy, z1 ^ dz1)
-    jobs = [(wg_ref, wg, 1 - z2, 0), (wu_ref, wu, z2, 1)]
     copies = []
     for c in range(n):
-        for src, dst, slot, s in jobs:
+        for src, dst, slot, s in ((wg_ref, wg, 1 - z2, 0), (wu_ref, wu, z2, 1)):
             copy = pltpu.make_async_copy(
                 src.at[:, pl.ds(pl.multiple_of(at + c * width, lane), width)],
                 dst.at[:, pl.ds(c * width, width)],
                 sems.at[s, c],
             )
-            copy.start()
-            copies.append((copy, dst, slot, c))
+            copies.append((copy, dst, slot, pl.ds(c * width, width)))
+    return copies
+
+
+def products(xn_ref, copies, out_ref):
     xn = xn_ref[...]
-    for copy, dst, slot, c in copies:
+    for copy, dst, slot, span in copies:
         copy.wait()
-        span = pl.ds(c * width, width)
         out_ref[slot, :, span] = dot_nn(xn, dst[:, span]).astype(out_ref.dtype)
+
+
+def base_kernel(tiles, dy, dz1, n, width, xn_ref, wg_ref, wu_ref, out_ref, wg, wu, sems):
+    copies = weight_copies(tiles, dy, dz1, n, width, wg_ref, wu_ref, wg, wu, sems)
+    for job in copies:
+        job[0].start()
+    products(xn_ref, copies, out_ref)
+
+
+def first_kernel(tiles, dy, dz1, n, width, *refs):
+    inputs, refs = refs[:5], refs[5:]
+    wg_ref, wu_ref, xn_ref, fac_ref, out_ref = refs[:5]
+    held, refs = refs[5:10], refs[10:]
+    wg, wu, norm_ref, fac32, low32, in_sems, sems = refs
+    ins = [pltpu.make_async_copy(a, b, in_sems.at[i]) for i, (a, b) in enumerate(zip(inputs, held))]
+    for copy in ins:
+        copy.start()
+    copies = weight_copies(tiles, dy, dz1, n, width, wg_ref, wu_ref, wg, wu, sems)
+    for job in copies[:2]:
+        job[0].start()
+    for copy in ins:
+        copy.wait()
+    for job in copies[2:]:
+        job[0].start()
+    prep_steps(*held, xn_ref, fac_ref, norm_ref, fac32, low32)
+    products(xn_ref, copies, out_ref)
+
+
+def first_part(ins, wg, wu, tiles, dy, dz1, dtype):
+    n, width = chunks_of(tiles.cols, 512)
+    rows, features = ins[0].shape
+    rank, units = ins[3].shape
+    depth = wg.shape[0]
+    return pl.pallas_call(
+        functools.partial(first_kernel, tiles, dy, dz1, n, width),
+        out_shape=(
+            jax.ShapeDtypeStruct((rows, depth), bf16),
+            jax.ShapeDtypeStruct((2 * rank, units + lane), bf16),
+            jax.ShapeDtypeStruct((2, rows, tiles.cols), dtype),
+        ),
+        in_specs=[in_hbm] * 7,
+        out_specs=(in_vmem,) * 3,
+        scratch_shapes=[pltpu.VMEM(x.shape, x.dtype) for x in ins]
+        + [
+            pltpu.VMEM((depth, tiles.cols), bf16),
+            pltpu.VMEM((depth, tiles.cols), bf16),
+            pltpu.VMEM((rows, features), bf16),
+            pltpu.VMEM((2 * rank, units), f32),
+            pltpu.VMEM((2 * rank, lane), f32),
+            pltpu.SemaphoreType.DMA((5,)),
+            pltpu.SemaphoreType.DMA((2, n)),
+        ],
+        compiler_params=pltpu.CompilerParams(vmem_limit_bytes=62 * MiB),
+        cost_estimate=small_cost,
+        name="first",
+    )(*ins, wg, wu)
 
 
 def base_part(xn, wg, wu, tiles, dy, dz1, dtype):
@@ -221,25 +257,17 @@
     return pl.pallas_call(
         functools.partial(base_kernel, tiles, dy, dz1, n, width),
         out_shape=jax.ShapeDtypeStruct((2, rows, tiles.cols), dtype),
-        in_specs=[in_vmem, in_any, in_any],
+        in_specs=[in_vmem, in_hbm, in_hbm],
         out_specs=in_vmem,
         scratch_shapes=[
             pltpu.VMEM((depth, tiles.cols), bf16),
             pltpu.VMEM((depth, tiles.cols), bf16),
             pltpu.SemaphoreType.DMA((2, n)),
         ],
-        compiler_params=pltpu.CompilerParams(vmem_limit_bytes=16 * MiB),
-        cost_estimate=pl.CostEstimate(
-            flops=4 * rows * depth * tiles.cols,
-            bytes_accessed=4 * depth * tiles.cols,
-            transcendentals=0,
-        ),
+        compiler_params=pltpu.CompilerParams(vmem_limit_bytes=44 * MiB),
+        cost_estimate=small_cost,
         name=f"base_y{dy}_z{dz1}",
     )(xn, wg, wu)
-
-
-def flip3(q):
-    return ((q & 1) << 2) | (q & 2) | (q >> 2)
 
 
 def count_steps(index, size, times):
@@ -276,7 +304,8 @@
     top = members * group
     own = (c < top) & ((member ^ p) == rel) & (second == kind)
     base = (c >= top) & (c - top - rows * kind == in_rows)
-    mix_ref[...] = (jnp.where(own, spread, 0.0) + jnp.where(base, 1.0, 0.0)).astype(bf16)
+    share = jnp.where(kind == 0, 0.5, 1.0)
+    mix_ref[...] = (share * (jnp.where(own, spread, 0.0) + jnp.where(base, 1.0, 0.0))).astype(bf16)
 
 
 def mixing(near, far, rows):
@@ -294,7 +323,7 @@
 
 
 def hidden_kernel(
-    tiles, dy, dz1, n, width, first, last, rows, down_scale, mix_ref, near_ref, far_ref, pair_ref, wd_ref, dif_ref, *rest
+    tiles, dy, dz1, first, last, rows, down_scale, mix_ref, near_ref, far_ref, pair_ref, wd_ref, dif_ref, *rest
 ):
     p, y, z1, z2 = cube()
     rest = list(rest)
@@ -303,19 +332,12 @@
         dout_ref, send_ref, keep_ref = rest.pop(0), rest.pop(0), rest.pop(0)
     else:
         acc_out, low_out = rest.pop(0), rest.pop(0)
-    right_ref, wd, sems = rest[:3]
+    right_ref, hid_ref, wd, sem = rest[:4]
     group = near_ref.shape[1]
     zb = z1 ^ dz1
     at = tiles.start(y ^ dy, zb)
-    copies = []
-    for c in range(n):
-        copy = pltpu.make_async_copy(
-            wd_ref.at[pl.ds(pl.multiple_of(at + c * width, lane), width), :],
-            wd.at[pl.ds(c * width, width), :],
-            sems.at[c],
-        )
-        copy.start()
-        copies.append(copy)
+    copy = pltpu.make_async_copy(wd_ref.at[pl.ds(at, tiles.cols), :], wd, sem)
+    copy.start()
     for q in range(8):
         ref = near_ref if q < 4 else far_ref
         right_ref[q * group : (q + 1) * group, :] = ref[q % 4, :, pl.ds(at, tiles.cols)]
@@ -324,75 +346,75 @@
     right_ref[top + rows : top + 2 * rows, :] = pair_ref[1 - z2]
     mix = mix_ref[...]
     height = mix.shape[0] // 2
-    acc = None if first else acc_in[...]
-    low = None if first else low_in[...]
+    n, width = chunks_of(tiles.cols, 640)
     for c in range(n):
         span = pl.ds(c * width, width)
         both = dot_nn(mix, right_ref[:, span])
         gate, up = both[:height], both[height:]
-        hidden = gate / (1.0 + jnp.exp(-gate)) * up
+        hidden = (gate + gate * jnp.tanh(gate)) * up
         if c * width < tiles.repeat * lane:
             col = lax.broadcasted_iota(jnp.int32, hidden.shape, 1) + c * width
             hidden = jnp.where(col >= zb * (tiles.repeat * lane), hidden, 0.0)
-        hidden = hidden.astype(bf16)
-        more_low = dot_nt(hidden, dif_ref[:, pl.ds(pl.multiple_of(at + c * width, lane), width)])
-        copies[c].wait()
-        more = dot_nn(hidden, wd[span, :])
-        acc = more if acc is None else acc + more
-        low = more_low if low is None else low + more_low
+        hid_ref[:, span] = hidden.astype(bf16)
+    hidden = hid_ref[...]
+    low = dot_nt(hidden, dif_ref[:, pl.ds(at, tiles.cols)])
+    low = low if first else low + low_in[...]
     if not last:
-        acc_out[...] = acc
         low_out[...] = low
-        return
-    t = lax.axis_index("tensor")
-    terms = dif_ref.shape[0]
-    rank = terms // 8
-    r = lax.broadcasted_iota(jnp.int32, (height, terms), 0)
-    c = lax.broadcasted_iota(jnp.int32, (height, terms), 1)
-    mine = count_steps(r, rows, 8) == count_steps(c, rank, 8)
-    low = jnp.where(mine, low * down_scale, 0.0)
-    total = rest[3]
-    total[...] = acc + dot_nn(low, dout_ref[...].astype(f32), precision=lax.Precision.HIGHEST)
+    else:
+        t = lax.axis_index("tensor")
+        terms = dif_ref.shape[0]
+        rank = terms // 8
+        r = lax.broadcasted_iota(jnp.int32, (height, terms), 0)
+        c = lax.broadcasted_iota(jnp.int32, (height, terms), 1)
+        mine = count_steps(r, rows, 8) == count_steps(c, rank, 8)
+        low = jnp.where(mine, low * down_scale, 0.0)
+        low_ref = rest[4]
+        low_ref[...] = low
+    out = wd_ref.shape[1]
     part = height // 2
-    keep_ref[...] = total[pl.ds(pl.multiple_of(t * part, 8), part), :]
-    send_ref[...] = total[pl.ds(pl.multiple_of((1 - t) * part, 8), part), :]
+    copy.wait()
+    for c in range(out // 256):
+        cols = pl.ds(c * 256, 256)
+        acc = dot_nn(hidden, wd[:, cols])
+        if not first:
+            acc = acc + acc_in[:, cols]
+        if not last:
+            acc_out[:, cols] = acc
+        else:
+            acc = acc + dot_nn(low, dout_ref[:, cols].astype(f32), precision=lax.Precision.HIGHEST)
+            keep_ref[:, cols] = jnp.where(t == 0, acc[:part], acc[part:])
+            send_ref[:, cols] = jnp.where(t == 0, acc[part:], acc[:part])
 
 
 def hidden_step(mix, near, far, pair, wd, dif, tiles, dy, dz1, rows, scale, state=None, dout=None):
-    n, width = chunks_of(tiles.cols, 640)
     height = mix.shape[0] // 2
     out = wd.shape[1]
     terms = dif.shape[0]
     first, last = state is None, dout is not None
     args = [mix, near, far, pair, wd, dif]
-    specs = [in_vmem] * 4 + [in_any, in_vmem]
     if not first:
         args += list(state)
-        specs += [in_vmem] * 2
     scratch = [
         pltpu.VMEM((mix.shape[1], tiles.cols), bf16),
+        pltpu.VMEM((height, tiles.cols), bf16),
         pltpu.VMEM((tiles.cols, out), bf16),
-        pltpu.SemaphoreType.DMA((n,)),
+        pltpu.SemaphoreType.DMA,
     ]
     if last:
         args.append(dout)
-        specs.append(in_vmem)
         shapes = [jax.ShapeDtypeStruct((height // 2, out), f32)] * 2
-        scratch.append(pltpu.VMEM((height, out), f32))
+        scratch.append(pltpu.VMEM((height, terms), f32))
     else:
         shapes = [jax.ShapeDtypeStruct((height, out), f32), jax.ShapeDtypeStruct((height, terms), f32)]
     return pl.pallas_call(
-        functools.partial(hidden_kernel, tiles, dy, dz1, n, width, first, last, rows, scale),
+        functools.partial(hidden_kernel, tiles, dy, dz1, first, last, rows, scale),
         out_shape=tuple(shapes),
-        in_specs=specs,
+        in_specs=[in_vmem] * 4 + [in_hbm] + [in_vmem] * (len(args) - 5),
         out_specs=(in_vmem, in_vmem),
         scratch_shapes=scratch,
-        compiler_params=pltpu.CompilerParams(vmem_limit_bytes=24 * MiB),
-        cost_estimate=pl.CostEstimate(
-            flops=2 * height * out * tiles.cols,
-            bytes_accessed=2 * out * tiles.cols,
-            transcendentals=height * tiles.cols,
-        ),
+        compiler_params=pltpu.CompilerParams(vmem_limit_bytes=44 * MiB),
+        cost_estimate=small_cost,
         name=f"hidden_y{dy}_z{dz1}",
     )(*args)
 
@@ -491,7 +513,7 @@
         functools.partial(update_kernel, n, high),
         out_shape=(jax.ShapeDtypeStruct((units, out), bf16), jax.ShapeDtypeStruct((1, lane), f32)),
         in_specs=[in_vmem] * 4,
-        out_specs=(in_any, in_vmem),
+        out_specs=(in_hbm, in_vmem),
         scratch_shapes=[pltpu.VMEM((units, out), bf16), pltpu.SemaphoreType.DMA((n,))],
         compiler_params=pltpu.CompilerParams(vmem_limit_bytes=24 * MiB),
         name="updates",
@@ -527,41 +549,48 @@
     dif = turned(down_input_factors).reshape(members * rank, units)
     dout = turned(down_out).reshape(members * rank, block)
 
-    xn, fac = prep(
+    ins = (
         prompts,
         turned(gate_in)[0],
         turned(up_in)[0],
         turned(gate_output_factors)[0],
         turned(up_output_factors)[0],
-        block,
-    )
-    two = jnp.stack([fac, over_z2(fac)])
-
-    part = functools.partial(base_part, xn, gate_weight, up_weight, tiles)
-    far0 = over_y(part(1, 1, bf16))
-    far1 = over_y(part(1, 0, bf16))
-    four = jnp.concatenate([two, over_z1(two)])
-    near0 = part(0, 1, f32)
+    )
+    after = lambda x, *done: lax.optimization_barrier((x, *done))[0]
+    part = lambda x, *a: base_part(x, gate_weight, up_weight, tiles, *a)
+
+    xn, fac, far0 = first_part(ins, gate_weight, up_weight, tiles, 1, 1, bf16)
+    far0 = over_y(far0)
+    fac_z2 = over_z2(fac)
+    far1 = part(xn, 1, 0, bf16)
+    xn, dif, dout = lax.optimization_barrier((xn, dif, dout, far1, fac_z2))[:3]
+    far1 = over_y(far1)
+    two = jnp.stack([fac, fac_z2])
+    two_z1 = over_z1(two)
+    near0 = part(xn, 0, 1, f32)
     from_z1 = over_z1((near0 + far0.astype(f32)).astype(bf16))
-    near1 = part(0, 0, f32)
+    near1 = part(after(xn, near0), 0, 0, f32)
+    four = jnp.concatenate([two, two_z1])
     far_four = over_y(four)
-    mine = near1 + far1.astype(f32) + from_z1.astype(f32)
-    total = (mine[1] + over_z2(mine[0].astype(bf16)).astype(f32)).astype(bf16)
 
     head_rows = lax.dynamic_slice_in_dim(label_head, (p * block) % label_head.shape[0], block, 0)
     head = jnp.where((p * block) // label_head.shape[0] == t, head_rows, over_t(head_rows))
 
+    mine = near1 + far1.astype(f32) + from_z1.astype(f32)
+    send = mine[0].astype(bf16)
+    total = (mine[1] + over_z2(send).astype(f32)).astype(bf16)
+    pair = jnp.stack([total, after(over_z2(total), head)])
+
     mix = mixing(four, far_four, rows)
     step = functools.partial(hidden_step, mix, four, far_four)
-    tail = (down_weight_matrix, dif, tiles)
-    pair = jnp.stack([total, over_z2(total)])
+    tail, wd = (dif, tiles), down_weight_matrix
     pair_z = over_z1(pair)
     pair_y = over_y(pair)
-    state = step(pair, *tail, 0, 0, rows, down_scale)
+    state = step(pair, wd, *tail, 0, 0, rows, down_scale)
     pair_yz = over_y(pair_z)
-    state = step(pair_z, *tail, 0, 1, rows, down_scale, state)
-    state = step(pair_y, *tail, 1, 0, rows, down_scale, state)
-    send, keep = step(pair_yz, *tail, 1, 1, rows, down_scale, state, dout)
+    state = step(pair_z, wd, *tail, 0, 1, rows, down_scale, state)
+    state = step(pair_y, wd, *tail, 1, 0, rows, down_scale, state)
+    send, keep = step(pair_yz, wd, *tail, 1, 1, rows, down_scale, state, dout)
 
     logits = part_logits(keep, over_t(send), prompts, head)
     logits = logits + over_y(logits)

time: 113 us -> 91.9 us (0.81)
  local copies, waits for them, and re-layouts: 26.8 us -> 1.07 us
  Pallas kernels: 33.7 us -> 39.6 us
  starting transfers between devices: 21.7 us -> 25.4 us
  waiting for transfers between devices: 27.5 us -> 24.1 us
    unnamed x26 -> x16, local copies, waits for them, and re-layouts: 25.6 us -> 0.82 us
    pallas_call x5, Pallas kernels: 12.7 us -> 21 us  [the longest x4 15.8 us: hidden_step(): pl.pallas_call(functools.partial(hidden_kernel, tiles, dy, dz1, first, la...]
    ppermute x17, starting transfers between devices: 21.7 us -> 25.4 us  [swap(): return lax.ppermute(x, axis, [(i, i ^ bit) for i in range(size)])]
    ppermute x17, waiting for transfers between devices: 27.5 us -> 24.1 us  [swap(): return lax.ppermute(x, axis, [(i, i ^ bit) for i in range(size)])]
    pallas_call x4 -> x3, Pallas kernels: 13.9 us -> 11.4 us  [base_part(): pl.pallas_call(functools.partial(base_kernel, tiles, dy, dz1, n, width),...]
  transfers between devices with their start and end apart: 17 -> 17, of which waited for: 10 -> 11; matrix products, arithmetic and copies ran while one was open for 2% -> 1% of each run, Pallas kernels for 20% -> 25%
where the time goes in v2:
time: 91.9 us; the launch traced here: 91.6 us
  Pallas kernels  39.6 us (43%)
  starting transfers between devices  25.4 us (28%)
  waiting for transfers between devices  24.1 us (26%)
  local copies, waits for them, and re-layouts  1.07 us (1%)
  between operations  1.06 us (1%)
    ppermute x17, starting transfers between devices, swap(): return lax.ppermute(x, axis, [(i, i ^ bit) for i in range(size)])  25.4 us
    ppermute x17, waiting for transfers between devices, swap(): return lax.ppermute(x, axis, [(i, i ^ bit) for i in range(size)])  24.1 us
    pallas_call x4, Pallas kernels, hidden_step(): pl.pallas_call(functools.partial(hidden_kernel, tiles, dy, dz1, first, la...  15.8 us
    pallas_call x3, Pallas kernels, base_part(): pl.pallas_call(functools.partial(base_kernel, tiles, dy, dz1, n, width),...  11.4 us
    pallas_call x1, Pallas kernels, updates(): pl.pallas_call(functools.partial(update_kernel, n, high), out_shape=(jax....  6.46 us
    pallas_call x1, Pallas kernels, first_part(): pl.pallas_call(functools.partial(first_kernel, tiles, dy, dz1, n, width),...  5.23 us
  transfers between devices with their start and end apart: 17, of which 11 were waited for; matrix products, arithmetic and copies ran while one was open for 1% of the time, Pallas kernels for 25%

profile of v2, /device:TPU:0, one launch (start us, length us, event | category | flops | bytes accessed | tf_op | source)
XLA Modules:
  0.0 91.6 jit_solution(14697960323427913852)
XLA Ops:
  0.6 5.2 %first.1 = (bf16[24,1024]{1,0:T(8,128)(2,1)}, bf16[8,7552]{1,0:T(8,128)(2,1)}, bf16[2,24,1920]{2,1,0:T(8,128)(2,1)}) custom-call(bf16[24,8192]{1,0:T(8,128)(2,1)} %x_ref.1, bf16[4,8192]{1,0:T(4,128)(2,1)} %bitcast.36, bf16[4,8192]{1,0:T(4,128)(2,1)} %bitcast.37, bf16[4,7424]{1,0:T(4,128)(2,1)} %bitcast.39, bf16[4,7424]{1,0:T(4,128)(2,1)} %bitcast.40, ...), custom_call_target="tpu_custom_call" | custom-call | flops 1024 | bytes 1024 | tf_op jit(solution)/shard_map/first/pallas_call | solution.py:229
  5.9 3.0 %collective-permute-start.4 = (bf16[2,24,1920]{2,1,0:T(8,128)(2,1)}, bf16[2,24,1920]{2,1,0:T(8,128)(2,1)S(1)}, u32[]{:S(2)}, u32[]{:S(2)}) collective-permute-start(bf16[2,24,1920]{2,1,0:T(8,128)(2,1)} %get-tuple-element.24), channel_id=1, source_target_pairs={{0,2},{2,0},{4,6},{6,4},{8,10},{10,8},{12,14},{14,12},{1,3},{3,1},... | collective-permute-start | bytes 552968 | tf_op jit(solution)/shard_map/ppermute | solution.py:154
  8.9 2.6 %collective-permute-start = (bf16[8,7552]{1,0:T(8,128)(2,1)}, bf16[8,7552]{1,0:T(8,128)(2,1)S(1)}, u32[]{:S(2)}, u32[]{:S(2)}) collective-permute-start(bf16[8,7552]{1,0:T(8,128)(2,1)} %get-tuple-element.20), channel_id=1, source_target_pairs={{0,8},{2,10},{4,12},{6,14},{8,0},{10,2},{12,4},{14,6},{1,9},{3,11}... | collective-permute-start | bytes 362504 | tf_op jit(solution)/shard_map/ppermute | solution.py:154
  11.5 0.1 collective-permute-start.8
  11.6 0.8 copy-done.1
  12.4 3.9 %base_y1_z0.1 = bf16[2,24,1920]{2,1,0:T(8,128)(2,1)S(1)} custom-call(bf16[24,1024]{1,0:T(8,128)(2,1)S(1)} %copy-done.1, bf16[1024,7424]{1,0:T(8,128)(2,1)} %wg_ref.5, bf16[1024,7424]{1,0:T(8,128)(2,1)} %wu_ref.5), custom_call_target="tpu_custom_call" | custom-call | flops 1024 | bytes 1024 | tf_op jit(solution)/shard_map/base_y1_z0/pallas_call | solution.py:257
  16.3 0.6 collective-permute-start.3
  16.9 0.1 reshape.14.dif_ref
  17.0 0.3 collective-permute-done
  17.3 3.8 %base_y0_z1.1 = f32[2,24,1920]{2,1,0:T(8,128)S(1)} custom-call(bf16[24,1024]{1,0:T(8,128)(2,1)S(1)} %copy-done.2, bf16[1024,7424]{1,0:T(8,128)(2,1)} %wg_ref.5, bf16[1024,7424]{1,0:T(8,128)(2,1)} %wu_ref.5), custom_call_target="tpu_custom_call" | custom-call | flops 1024 | bytes 1024 | tf_op jit(solution)/shard_map/base_y0_z1/pallas_call | solution.py:257
  21.2 1.4 %collective-permute-start.5 = (bf16[2,24,1920]{2,1,0:T(8,128)(2,1)S(1)}, bf16[2,24,1920]{2,1,0:T(8,128)(2,1)S(1)}, u32[]{:S(2)}, u32[]{:S(2)}) collective-permute-start(bf16[2,24,1920]{2,1,0:T(8,128)(2,1)S(1)} %add_convert_fusion), channel_id=1, source_target_pairs={{0,4},{2,6},{4,0},{6,2},{8,12},{10,14},{12,8},{14,10},{1,5},{3,7},... | collective-permute-start | bytes 552968 | tf_op jit(solution)/shard_map/ppermute | solution.py:154
  22.6 0.8 collective-permute-start.1
  23.4 3.8 %base_y0_z0.1 = f32[2,24,1920]{2,1,0:T(8,128)S(1)} custom-call(bf16[24,1024]{1,0:T(8,128)(2,1)S(1)} %copy-done.2, bf16[1024,7424]{1,0:T(8,128)(2,1)} %wg_ref.5, bf16[1024,7424]{1,0:T(8,128)(2,1)} %wu_ref.5), custom_call_target="tpu_custom_call" | custom-call | flops 1024 | bytes 1024 | tf_op jit(solution)/shard_map/base_y0_z0/pallas_call | solution.py:257
  27.2 1.6 %collective-permute-done.5 = bf16[2,24,1920]{2,1,0:T(8,128)(2,1)S(1)} collective-permute-done((bf16[2,24,1920]{2,1,0:T(8,128)(2,1)S(1)}, bf16[2,24,1920]{2,1,0:T(8,128)(2,1)S(1)}, u32[]{:S(2)}, u32[]{:S(2)}) %collective-permute-start.5) | collective-permute-done | bytes 184352 | tf_op jit(solution)/shard_map/ppermute | solution.py:154
  28.8 0.1 convert_add_fusion
  28.9 2.0 %collective-permute-start.6 = (bf16[24,1920]{1,0:T(8,128)(2,1)S(1)}, bf16[24,1920]{1,0:T(8,128)(2,1)S(1)}, u32[]{:S(2)}, u32[]{:S(2)}) collective-permute-start(bf16[24,1920]{1,0:T(8,128)(2,1)S(1)} %fusion.2), channel_id=1, source_target_pairs={{0,8},{2,10},{4,12},{6,14},{8,0},{10,2},{12,4},{14,6},{1,9},{3,11}... | collective-permute-start | bytes 276488 | tf_op jit(solution)/shard_map/ppermute | solution.py:154
  30.9 0.1 broadcast_select_fusion.head_ref
  31.0 3.7 %collective-permute-done.6 = bf16[24,1920]{1,0:T(8,128)(2,1)S(1)} collective-permute-done((bf16[24,1920]{1,0:T(8,128)(2,1)S(1)}, bf16[24,1920]{1,0:T(8,128)(2,1)S(1)}, u32[]{:S(2)}, u32[]{:S(2)}) %collective-permute-start.6) | collective-permute-done | bytes 92192 | tf_op jit(solution)/shard_map/ppermute | solution.py:154
  34.7 2.9 %collective-permute-start.7 = (bf16[24,1920]{1,0:T(8,128)(2,1)S(1)}, bf16[24,1920]{1,0:T(8,128)(2,1)S(1)}, u32[]{:S(2)}, u32[]{:S(2)}) collective-permute-start(bf16[24,1920]{1,0:T(8,128)(2,1)S(1)} %fusion.1), channel_id=1, source_target_pairs={{0,8},{2,10},{4,12},{6,14},{8,0},{10,2},{12,4},{14,6},{1,9},{3,11}... | collective-permute-start | bytes 276488 | tf_op jit(solution)/shard_map/ppermute | solution.py:154
  37.6 0.1 pad_maximum_fusion.near_ref
  37.6 1.6 %collective-permute-start.2 = (bf16[4,8,7552]{2,1,0:T(8,128)(2,1)S(1)}, bf16[4,8,7552]{2,1,0:T(8,128)(2,1)S(1)}, u32[]{:S(2)}, u32[]{:S(2)}) collective-permute-start(bf16[4,8,7552]{2,1,0:T(8,128)(2,1)S(1)} %pad_maximum_fusion.near_ref), channel_id=1, source_target_pairs={{0,2},{2,0},{4,6},{6,4},{8,10},{10,8},{12,14},{14,12},{1,3},{3,1},... | collective-permute-start | bytes 1449992 | tf_op jit(solution)/shard_map/ppermute | solution.py:154
  39.2 2.0 %collective-permute-done.7 = bf16[24,1920]{1,0:T(8,128)(2,1)S(1)} collective-permute-done((bf16[24,1920]{1,0:T(8,128)(2,1)S(1)}, bf16[24,1920]{1,0:T(8,128)(2,1)S(1)}, u32[]{:S(2)}, u32[]{:S(2)}) %collective-permute-start.7) | collective-permute-done | bytes 92192 | tf_op jit(solution)/shard_map/ppermute | solution.py:154
  41.2 1.7 %collective-permute-start.9 = (bf16[2,24,1920]{2,1,0:T(8,128)(2,1)S(1)}, bf16[2,24,1920]{2,1,0:T(8,128)(2,1)S(1)}, u32[]{:S(2)}, u32[]{:S(2)}) collective-permute-start(bf16[2,24,1920]{2,1,0:T(8,128)(2,1)S(1)} %pad_maximum_fusion.2.pair_ref), channel_id=1, source_target_pairs={{0,4},{2,6},{4,0},{6,2},{8,12},{10,14},{12,8},{14,10},{1,5},{3,7},... | collective-permute-start | bytes 552968 | tf_op jit(solution)/shard_map/ppermute | solution.py:154
  42.9 1.2 %collective-permute-start.11 = (bf16[2,24,1920]{2,1,0:T(8,128)(2,1)S(1)}, bf16[2,24,1920]{2,1,0:T(8,128)(2,1)S(1)}, u32[]{:S(2)}, u32[]{:S(2)}) collective-permute-start(bf16[2,24,1920]{2,1,0:T(8,128)(2,1)S(1)} %pad_maximum_fusion.2.pair_ref), channel_id=1, source_target_pairs={{0,2},{2,0},{4,6},{6,4},{8,10},{10,8},{12,14},{14,12},{1,3},{3,1},... | collective-permute-start | bytes 552968 | tf_op jit(solution)/shard_map/ppermute | solution.py:154
  44.1 2.7 %collective-permute-done.9.pair_ref = bf16[2,24,1920]{2,1,0:T(8,128)(2,1)S(1)} collective-permute-done((bf16[2,24,1920]{2,1,0:T(8,128)(2,1)S(1)}, bf16[2,24,1920]{2,1,0:T(8,128)(2,1)S(1)}, u32[]{:S(2)}, u32[]{:S(2)}) %collective-permute-start.9) | collective-permute-done | bytes 184352 | tf_op jit(solution)/shard_map/ppermute | solution.py:154
  46.8 2.7 %collective-permute-start.10 = (bf16[2,24,1920]{2,1,0:T(8,128)(2,1)S(1)}, bf16[2,24,1920]{2,1,0:T(8,128)(2,1)S(1)}, u32[]{:S(2)}, u32[]{:S(2)}) collective-permute-start(bf16[2,24,1920]{2,1,0:T(8,128)(2,1)S(1)} %collective-permute-done.9.pair_ref), channel_id=1, source_target_pairs={{0,2},{2,0},{4,6},{6,4},{8,10},{10,8},{12,14},{14,12},{1,3},{3,1},... | collective-permute-start | bytes 552968 | tf_op jit(solution)/shard_map/ppermute | solution.py:154
  49.6 2.1 %collective-permute-done.2.far_ref = bf16[4,8,7552]{2,1,0:T(8,128)(2,1)S(1)} collective-permute-done((bf16[4,8,7552]{2,1,0:T(8,128)(2,1)S(1)}, bf16[4,8,7552]{2,1,0:T(8,128)(2,1)S(1)}, u32[]{:S(2)}, u32[]{:S(2)}) %collective-permute-start.2) | collective-permute-done | bytes 483360 | tf_op jit(solution)/shard_map/ppermute | solution.py:154
  51.7 0.2 mixing.1.mix_ref
  51.9 3.8 %hidden_y0_z0.1 = (f32[192,1024]{1,0:T(8,128)S(1)}, f32[192,32]{1,0:T(8,128)S(1)}) custom-call(bf16[384,112]{1,0:T(8,128)(2,1)S(1)} %mixing.1.mix_ref, bf16[4,8,7552]{2,1,0:T(8,128)(2,1)S(1)} %pad_maximum_fusion.near_ref, bf16[4,8,7552]{2,1,0:T(8,128)(2,1)S(1)} %collective-permute-done.2.far_ref, bf16[2,24,1920]{2,1,0:T(8,128)(2,1)S(1)} %pad_maximum_fusion.2.pair_ref, ...), custom_call_target="tpu_custom_call" | custom-call | flops 1024 | bytes 1024 | tf_op jit(solution)/shard_map/hidden_y0_z0/pallas_call | solution.py:410
  55.7 3.8 %hidden_y0_z1.1 = (f32[192,1024]{1,0:T(8,128)S(1)}, f32[192,32]{1,0:T(8,128)S(1)}) custom-call(bf16[384,112]{1,0:T(8,128)(2,1)S(1)} %mixing.1.mix_ref, bf16[4,8,7552]{2,1,0:T(8,128)(2,1)S(1)} %pad_maximum_fusion.near_ref, bf16[4,8,7552]{2,1,0:T(8,128)(2,1)S(1)} %collective-permute-done.2.far_ref, bf16[2,24,1920]{2,1,0:T(8,128)(2,1)S(1)} %collective-permute-done.9.pair_ref, ...), custom_call_target="tpu_custom_call" | custom-call | flops 1024 | bytes 1024 | tf_op jit(solution)/shard_map/hidden_y0_z1/pallas_call | solution.py:410
  59.5 0.0 copy-start
  59.5 0.0 copy-start.7
  59.5 3.8 %hidden_y1_z0.1 = (f32[192,1024]{1,0:T(8,128)S(1)}, f32[192,32]{1,0:T(8,128)S(1)}) custom-call(bf16[384,112]{1,0:T(8,128)(2,1)S(1)} %mixing.1.mix_ref, bf16[4,8,7552]{2,1,0:T(8,128)(2,1)S(1)} %pad_maximum_fusion.near_ref, bf16[4,8,7552]{2,1,0:T(8,128)(2,1)S(1)} %collective-permute-done.2.far_ref, bf16[2,24,1920]{2,1,0:T(8,128)(2,1)S(1)} %collective-permute-done.11.pair_ref, ...), custom_call_target="tpu_custom_call" | custom-call | flops 1024 | bytes 1024 | tf_op jit(solution)/shard_map/hidden_y1_z0/pallas_call | solution.py:410
  63.3 4.5 %hidden_y1_z1.1 = (f32[96,1024]{1,0:T(8,128)S(1)}, f32[96,1024]{1,0:T(8,128)S(1)}) custom-call(bf16[384,112]{1,0:T(8,128)(2,1)S(1)} %mixing.1.mix_ref, bf16[4,8,7552]{2,1,0:T(8,128)(2,1)S(1)} %pad_maximum_fusion.near_ref, bf16[4,8,7552]{2,1,0:T(8,128)(2,1)S(1)} %collective-permute-done.2.far_ref, bf16[2,24,1920]{2,1,0:T(8,128)(2,1)S(1)} %collective-permute-done.10.pair_ref, ...), custom_call_target="tpu_custom_call" | custom-call | flops 1024 | bytes 1024 | tf_op jit(solution)/shard_map/hidden_y1_z1/pallas_call | solution.py:410
  67.8 0.1 collective-permute-start.12
  67.8 1.7 %collective-permute-done.12.recv_ref = f32[96,1024]{1,0:T(8,128)S(1)} collective-permute-done((f32[96,1024]{1,0:T(8,128)S(1)}, f32[96,1024]{1,0:T(8,128)S(1)}, u32[]{:S(2)}, u32[]{:S(2)}) %collective-permute-start.12) | collective-permute-done | bytes 393248 | tf_op jit(solution)/shard_map/ppermute | solution.py:154
  69.5 0.3 part_logits.1
  69.8 1.6 %collective-permute-start.13 = (f32[104,128]{1,0:T(8,128)S(1)}, f32[104,128]{1,0:T(8,128)S(1)}, u32[]{:S(2)}, u32[]{:S(2)}) collective-permute-start(f32[104,128]{1,0:T(8,128)S(1)} %part_logits.1), channel_id=1, source_target_pairs={{0,2},{2,0},{4,6},{6,4},{8,10},{10,8},{12,14},{14,12},{1,3},{3,1},... | collective-permute-start | bytes 159752 | tf_op jit(solution)/shard_map/ppermute | solution.py:154
  71.4 2.6 %collective-permute-done.13 = f32[104,128]{1,0:T(8,128)S(1)} collective-permute-done((f32[104,128]{1,0:T(8,128)S(1)}, f32[104,128]{1,0:T(8,128)S(1)}, u32[]{:S(2)}, u32[]{:S(2)}) %collective-permute-start.13) | collective-permute-done | bytes 53280 | tf_op jit(solution)/shard_map/ppermute | solution.py:154
  74.1 2.3 %collective-permute-start.14 = (f32[104,128]{1,0:T(8,128)S(1)}, f32[104,128]{1,0:T(8,128)S(1)}, u32[]{:S(2)}, u32[]{:S(2)}) collective-permute-start(f32[104,128]{1,0:T(8,128)S(1)} %add.32), channel_id=1, source_target_pairs={{0,4},{2,6},{4,0},{6,2},{8,12},{10,14},{12,8},{14,10},{1,5},{3,7},... | collective-permute-start | bytes 159752 | tf_op jit(solution)/shard_map/ppermute | solution.py:154
  76.3 2.1 %collective-permute-done.14 = f32[104,128]{1,0:T(8,128)S(1)} collective-permute-done((f32[104,128]{1,0:T(8,128)S(1)}, f32[104,128]{1,0:T(8,128)S(1)}, u32[]{:S(2)}, u32[]{:S(2)}) %collective-permute-start.14) | collective-permute-done | bytes 53280 | tf_op jit(solution)/shard_map/ppermute | solution.py:154
  78.4 0.9 collective-permute-start.15
  79.3 0.1 copy.14.targets_ref
  79.4 4.1 %collective-permute-done.15.b_ref = f32[104,128]{1,0:T(8,128)S(1)} collective-permute-done((f32[104,128]{1,0:T(8,128)S(1)}, f32[104,128]{1,0:T(8,128)S(1)}, u32[]{:S(2)}, u32[]{:S(2)}) %collective-permute-start.15) | collective-permute-done | bytes 53280 | tf_op jit(solution)/shard_map/ppermute | solution.py:154
  83.5 0.2 part_rewards.1.a_ref
  83.7 0.1 collective-permute-start.16
  83.8 1.2 %collective-permute-done.16.b_ref = f32[8,128]{1,0:T(8,128)S(1)} collective-permute-done((f32[8,128]{1,0:T(8,128)S(1)}, f32[8,128]{1,0:T(8,128)S(1)}, u32[]{:S(2)}, u32[]{:S(2)}) %collective-permute-start.16) | collective-permute-done | bytes 4128 | tf_op jit(solution)/shard_map/ppermute | solution.py:154
  85.0 6.5 %updates.1 = (bf16[7424,1024]{1,0:T(8,128)(2,1)}, f32[1,128]{1,0:T(1,128)}) custom-call(f32[8,128]{1,0:T(8,128)S(1)} %part_rewards.1.a_ref, f32[8,128]{1,0:T(8,128)S(1)} %collective-permute-done.16.b_ref, bf16[32,7424]{1,0:T(8,128)(2,1)S(1)} %reshape.14.dif_ref, bf16[32,1024]{1,0:T(8,128)(2,1)S(1)} %reshape.15.rest_2_.dout_ref), custom_call_target="tpu_custom_call" | custom-call | tf_op jit(solution)/shard_map/updates/pallas_call | solution.py:512
  (28 shorter events, 0.2 us)
Async XLA Ops:
  0.6 10.9 %copy-start.5 = (bf16[4096,128]{1,0:T(8,128)(2,1)S(1)}, bf16[4096,128]{1,0:T(8,128)(2,1)}, u32[]{:S(2)}) copy-start(bf16[4096,128]{1,0:T(8,128)(2,1)} %param.22) | copy-start | bytes 3145732
  5.9 15.3 %collective-permute-start.4 = (bf16[2,24,1920]{2,1,0:T(8,128)(2,1)}, bf16[2,24,1920]{2,1,0:T(8,128)(2,1)S(1)}, u32[]{:S(2)}, u32[]{:S(2)}) collective-permute-start(bf16[2,24,1920]{2,1,0:T(8,128)(2,1)} %get-tuple-element.24), channel_id=1, source_target_pairs={{0,2},{2,0},{4,6},{6,4},{8,10},{10,8},{12,14},{14,12},{1,3},{3,1},... | collective-permute-start | bytes 552968 | tf_op jit(solution)/shard_map/ppermute | solution.py:154
  8.9 8.4 %collective-permute-start = (bf16[8,7552]{1,0:T(8,128)(2,1)}, bf16[8,7552]{1,0:T(8,128)(2,1)S(1)}, u32[]{:S(2)}, u32[]{:S(2)}) collective-permute-start(bf16[8,7552]{1,0:T(8,128)(2,1)} %get-tuple-element.20), channel_id=1, source_target_pairs={{0,8},{2,10},{4,12},{6,14},{8,0},{10,2},{12,4},{14,6},{1,9},{3,11}... | collective-permute-start | bytes 362504 | tf_op jit(solution)/shard_map/ppermute | solution.py:154
  11.5 19.4 %collective-permute-start.8 = (bf16[1024,128]{1,0:T(8,128)(2,1)S(1)}, bf16[1024,128]{1,0:T(8,128)(2,1)S(1)}, u32[]{:S(2)}, u32[]{:S(2)}) collective-permute-start(bf16[1024,128]{1,0:T(8,128)(2,1)S(1)} %constant_dynamic-slice_fusion), channel_id=1, source_target_pairs={{0,1},{1,0},{2,3},{3,2},{4,5},{5,4},{6,7},{7,6},{8,9},{9,8},{10,11... | collective-permute-start | bytes 786440 | tf_op jit(solution)/shard_map/ppermute | solution.py:154
  11.6 0.8 copy-start.1
  12.4 4.4 %copy-start.6 = (bf16[8,1024,4]{1,2,0:T(4,128)(2,1)S(1)}, bf16[8,1024,4]{1,2,0:T(4,128)(2,1)}, u32[]{:S(2)}) copy-start(bf16[8,1024,4]{1,2,0:T(4,128)(2,1)} %param.21) | copy-start | bytes 196612
  12.4 4.5 %copy-start.4 = (bf16[8,7424,4]{1,2,0:T(4,128)(2,1)S(1)}, bf16[8,7424,4]{1,2,0:T(4,128)(2,1)}, u32[]{:S(2)}) copy-start(bf16[8,7424,4]{1,2,0:T(4,128)(2,1)} %param.20) | copy-start | bytes 1425412
  12.4 4.9 %copy-start.2 = (bf16[24,1024]{1,0:T(8,128)(2,1)S(1)}, bf16[24,1024]{1,0:T(8,128)(2,1)}, u32[]{:S(2)}) copy-start(bf16[24,1024]{1,0:T(8,128)(2,1)} %get-tuple-element.23.xn_ref) | copy-start | bytes 147460
  16.3 10.9 %collective-permute-start.3 = (bf16[2,24,1920]{2,1,0:T(8,128)(2,1)S(1)}, bf16[2,24,1920]{2,1,0:T(8,128)(2,1)S(1)}, u32[]{:S(2)}, u32[]{:S(2)}) collective-permute-start(bf16[2,24,1920]{2,1,0:T(8,128)(2,1)S(1)} %base_y1_z0.1), channel_id=1, source_target_pairs={{0,2},{2,0},{4,6},{6,4},{8,10},{10,8},{12,14},{14,12},{1,3},{3,1},... | collective-permute-start | bytes 552968 | tf_op jit(solution)/shard_map/ppermute | solution.py:154
  17.0 5.6 %copy-start.3 = (bf16[8,7552]{1,0:T(8,128)(2,1)S(1)}, bf16[8,7552]{1,0:T(8,128)(2,1)}, u32[]{:S(2)}) copy-start(bf16[8,7552]{1,0:T(8,128)(2,1)} %get-tuple-element.20) | copy-start | bytes 362500
  21.2 7.6 %collective-permute-start.5 = (bf16[2,24,1920]{2,1,0:T(8,128)(2,1)S(1)}, bf16[2,24,1920]{2,1,0:T(8,128)(2,1)S(1)}, u32[]{:S(2)}, u32[]{:S(2)}) collective-permute-start(bf16[2,24,1920]{2,1,0:T(8,128)(2,1)S(1)} %add_convert_fusion), channel_id=1, source_target_pairs={{0,4},{2,6},{4,0},{6,2},{8,12},{10,14},{12,8},{14,10},{1,5},{3,7},... | collective-permute-start | bytes 552968 | tf_op jit(solution)/shard_map/ppermute | solution.py:154
  22.6 15.0 %collective-permute-start.1 = (bf16[2,8,7552]{2,1,0:T(8,128)(2,1)S(1)}, bf16[2,8,7552]{2,1,0:T(8,128)(2,1)S(1)}, u32[]{:S(2)}, u32[]{:S(2)}) collective-permute-start(bf16[2,8,7552]{2,1,0:T(8,128)(2,1)S(1)} %pad_maximum_fusion.1), channel_id=1, source_target_pairs={{0,4},{2,6},{4,0},{6,2},{8,12},{10,14},{12,8},{14,10},{1,5},{3,7},... | collective-permute-start | bytes 725000 | tf_op jit(solution)/shard_map/ppermute | solution.py:154
  28.9 5.8 %collective-permute-start.6 = (bf16[24,1920]{1,0:T(8,128)(2,1)S(1)}, bf16[24,1920]{1,0:T(8,128)(2,1)S(1)}, u32[]{:S(2)}, u32[]{:S(2)}) collective-permute-start(bf16[24,1920]{1,0:T(8,128)(2,1)S(1)} %fusion.2), channel_id=1, source_target_pairs={{0,8},{2,10},{4,12},{6,14},{8,0},{10,2},{12,4},{14,6},{1,9},{3,11}... | collective-permute-start | bytes 276488 | tf_op jit(solution)/shard_map/ppermute | solution.py:154
  34.7 6.5 %collective-permute-start.7 = (bf16[24,1920]{1,0:T(8,128)(2,1)S(1)}, bf16[24,1920]{1,0:T(8,128)(2,1)S(1)}, u32[]{:S(2)}, u32[]{:S(2)}) collective-permute-start(bf16[24,1920]{1,0:T(8,128)(2,1)S(1)} %fusion.1), channel_id=1, source_target_pairs={{0,8},{2,10},{4,12},{6,14},{8,0},{10,2},{12,4},{14,6},{1,9},{3,11}... | collective-permute-start | bytes 276488 | tf_op jit(solution)/shard_map/ppermute | solution.py:154
  37.6 14.0 %collective-permute-start.2 = (bf16[4,8,7552]{2,1,0:T(8,128)(2,1)S(1)}, bf16[4,8,7552]{2,1,0:T(8,128)(2,1)S(1)}, u32[]{:S(2)}, u32[]{:S(2)}) collective-permute-start(bf16[4,8,7552]{2,1,0:T(8,128)(2,1)S(1)} %pad_maximum_fusion.near_ref), channel_id=1, source_target_pairs={{0,2},{2,0},{4,6},{6,4},{8,10},{10,8},{12,14},{14,12},{1,3},{3,1},... | collective-permute-start | bytes 1449992 | tf_op jit(solution)/shard_map/ppermute | solution.py:154
  41.2 5.6 %collective-permute-start.9 = (bf16[2,24,1920]{2,1,0:T(8,128)(2,1)S(1)}, bf16[2,24,1920]{2,1,0:T(8,128)(2,1)S(1)}, u32[]{:S(2)}, u32[]{:S(2)}) collective-permute-start(bf16[2,24,1920]{2,1,0:T(8,128)(2,1)S(1)} %pad_maximum_fusion.2.pair_ref), channel_id=1, source_target_pairs={{0,4},{2,6},{4,0},{6,2},{8,12},{10,14},{12,8},{14,10},{1,5},{3,7},... | collective-permute-start | bytes 552968 | tf_op jit(solution)/shard_map/ppermute | solution.py:154
  42.9 16.5 %collective-permute-start.11 = (bf16[2,24,1920]{2,1,0:T(8,128)(2,1)S(1)}, bf16[2,24,1920]{2,1,0:T(8,128)(2,1)S(1)}, u32[]{:S(2)}, u32[]{:S(2)}) collective-permute-start(bf16[2,24,1920]{2,1,0:T(8,128)(2,1)S(1)} %pad_maximum_fusion.2.pair_ref), channel_id=1, source_target_pairs={{0,2},{2,0},{4,6},{6,4},{8,10},{10,8},{12,14},{14,12},{1,3},{3,1},... | collective-permute-start | bytes 552968 | tf_op jit(solution)/shard_map/ppermute | solution.py:154
  46.8 16.4 %collective-permute-start.10 = (bf16[2,24,1920]{2,1,0:T(8,128)(2,1)S(1)}, bf16[2,24,1920]{2,1,0:T(8,128)(2,1)S(1)}, u32[]{:S(2)}, u32[]{:S(2)}) collective-permute-start(bf16[2,24,1920]{2,1,0:T(8,128)(2,1)S(1)} %collective-permute-done.9.pair_ref), channel_id=1, source_target_pairs={{0,2},{2,0},{4,6},{6,4},{8,10},{10,8},{12,14},{14,12},{1,3},{3,1},... | collective-permute-start | bytes 552968 | tf_op jit(solution)/shard_map/ppermute | solution.py:154
  59.5 10.1 %copy-start = (bf16[24,8192]{1,0:T(8,128)(2,1)S(1)}, bf16[24,8192]{1,0:T(8,128)(2,1)}, u32[]{:S(2)}) copy-start(bf16[24,8192]{1,0:T(8,128)(2,1)} %x_ref.1) | copy-start | bytes 1179652
  59.5 19.9 %copy-start.7 = (s32[24]{0:T(128)S(1)}, s32[24]{0:T(128)}, u32[]{:S(2)}) copy-start(s32[24]{0:T(128)} %param.23) | copy-start | bytes 292
  67.8 1.8 %collective-permute-start.12 = (f32[96,1024]{1,0:T(8,128)S(1)}, f32[96,1024]{1,0:T(8,128)S(1)}, u32[]{:S(2)}, u32[]{:S(2)}) collective-permute-start(f32[96,1024]{1,0:T(8,128)S(1)} %get-tuple-element.35), channel_id=1, source_target_pairs={{0,1},{1,0},{2,3},{3,2},{4,5},{5,4},{6,7},{7,6},{8,9},{9,8},{10,11... | collective-permute-start | bytes 1179656 | tf_op jit(solution)/shard_map/ppermute | solution.py:154
  69.8 4.2 %collective-permute-start.13 = (f32[104,128]{1,0:T(8,128)S(1)}, f32[104,128]{1,0:T(8,128)S(1)}, u32[]{:S(2)}, u32[]{:S(2)}) collective-permute-start(f32[104,128]{1,0:T(8,128)S(1)} %part_logits.1), channel_id=1, source_target_pairs={{0,2},{2,0},{4,6},{6,4},{8,10},{10,8},{12,14},{14,12},{1,3},{3,1},... | collective-permute-start | bytes 159752 | tf_op jit(solution)/shard_map/ppermute | solution.py:154
  74.1 4.4 %collective-permute-start.14 = (f32[104,128]{1,0:T(8,128)S(1)}, f32[104,128]{1,0:T(8,128)S(1)}, u32[]{:S(2)}, u32[]{:S(2)}) collective-permute-start(f32[104,128]{1,0:T(8,128)S(1)} %add.32), channel_id=1, source_target_pairs={{0,4},{2,6},{4,0},{6,2},{8,12},{10,14},{12,8},{14,10},{1,5},{3,7},... | collective-permute-start | bytes 159752 | tf_op jit(solution)/shard_map/ppermute | solution.py:154
  78.4 5.1 %collective-permute-start.15 = (f32[104,128]{1,0:T(8,128)S(1)}, f32[104,128]{1,0:T(8,128)S(1)}, u32[]{:S(2)}, u32[]{:S(2)}) collective-permute-start(f32[104,128]{1,0:T(8,128)S(1)} %add.33.a_ref), channel_id=1, source_target_pairs={{0,8},{2,10},{4,12},{6,14},{8,0},{10,2},{12,4},{14,6},{1,9},{3,11}... | collective-permute-start | bytes 159752 | tf_op jit(solution)/shard_map/ppermute | solution.py:154
  83.7 1.2 %collective-permute-start.16 = (f32[8,128]{1,0:T(8,128)S(1)}, f32[8,128]{1,0:T(8,128)S(1)}, u32[]{:S(2)}, u32[]{:S(2)}) collective-permute-start(f32[8,128]{1,0:T(8,128)S(1)} %part_rewards.1.a_ref), channel_id=1, source_target_pairs={{0,1},{1,0},{2,3},{3,2},{4,5},{5,4},{6,7},{7,6},{8,9},{9,8},{10,11... | collective-permute-start | bytes 12296 | tf_op jit(solution)/shard_map/ppermute | solution.py:154

commit v3 on v2

--- a/solution.py
+++ b/solution.py
@@ -154,7 +154,15 @@
     return lax.ppermute(x, axis, [(i, i ^ bit) for i in range(size)])
 
 
-def prep_steps(x_ref, gin_ref, uin_ref, gof_ref, uof_ref, xn_ref, fac_ref, norm_ref, fac32, low32):
+def prep_kernel(*refs):
+    inputs, (xn_ref, fac_ref), held = refs[:5], refs[5:7], refs[7:12]
+    norm_ref, fac32, low32, sems = refs[12:]
+    copies = [pltpu.make_async_copy(a, b, sems.at[i]) for i, (a, b) in enumerate(zip(inputs, held))]
+    for copy in copies:
+        copy.start()
+    for copy in copies:
+        copy.wait()
+    x_ref, gin_ref, uin_ref, gof_ref, uof_ref = held
     p = cube()[0]
     rows, width = x_ref.shape
     rank, units = gof_ref.shape
@@ -173,100 +181,74 @@
     fac_ref[:, units : units + lane] = low32[...].astype(bf16)
 
 
-def weight_copies(tiles, dy, dz1, n, width, wg_ref, wu_ref, wg, wu, sems):
-    p, y, z1, z2 = cube()
-    at = tiles.start(y ^ dy, z1 ^ dz1)
-    copies = []
-    for c in range(n):
-        for src, dst, slot, s in ((wg_ref, wg, 1 - z2, 0), (wu_ref, wu, z2, 1)):
-            copy = pltpu.make_async_copy(
-                src.at[:, pl.ds(pl.multiple_of(at + c * width, lane), width)],
-                dst.at[:, pl.ds(c * width, width)],
-                sems.at[s, c],
-            )
-            copies.append((copy, dst, slot, pl.ds(c * width, width)))
-    return copies
-
-
-def products(xn_ref, copies, out_ref):
-    xn = xn_ref[...]
-    for copy, dst, slot, span in copies:
-        copy.wait()
-        out_ref[slot, :, span] = dot_nn(xn, dst[:, span]).astype(out_ref.dtype)
-
-
-def base_kernel(tiles, dy, dz1, n, width, xn_ref, wg_ref, wu_ref, out_ref, wg, wu, sems):
-    copies = weight_copies(tiles, dy, dz1, n, width, wg_ref, wu_ref, wg, wu, sems)
-    for job in copies:
-        job[0].start()
-    products(xn_ref, copies, out_ref)
-
-
-def first_kernel(tiles, dy, dz1, n, width, *refs):
-    inputs, refs = refs[:5], refs[5:]
-    wg_ref, wu_ref, xn_ref, fac_ref, out_ref = refs[:5]
-    held, refs = refs[5:10], refs[10:]
-    wg, wu, norm_ref, fac32, low32, in_sems, sems = refs
-    ins = [pltpu.make_async_copy(a, b, in_sems.at[i]) for i, (a, b) in enumerate(zip(inputs, held))]
-    for copy in ins:
-        copy.start()
-    copies = weight_copies(tiles, dy, dz1, n, width, wg_ref, wu_ref, wg, wu, sems)
-    for job in copies[:2]:
-        job[0].start()
-    for copy in ins:
-        copy.wait()
-    for job in copies[2:]:
-        job[0].start()
-    prep_steps(*held, xn_ref, fac_ref, norm_ref, fac32, low32)
-    products(xn_ref, copies, out_ref)
-
-
-def first_part(ins, wg, wu, tiles, dy, dz1, dtype):
-    n, width = chunks_of(tiles.cols, 512)
+def prep(ins, block):
     rows, features = ins[0].shape
     rank, units = ins[3].shape
-    depth = wg.shape[0]
     return pl.pallas_call(
-        functools.partial(first_kernel, tiles, dy, dz1, n, width),
+        prep_kernel,
         out_shape=(
-            jax.ShapeDtypeStruct((rows, depth), bf16),
+            jax.ShapeDtypeStruct((rows, block), bf16),
             jax.ShapeDtypeStruct((2 * rank, units + lane), bf16),
-            jax.ShapeDtypeStruct((2, rows, tiles.cols), dtype),
         ),
-        in_specs=[in_hbm] * 7,
-        out_specs=(in_vmem,) * 3,
+        in_specs=[in_hbm] * 5,
+        out_specs=(in_vmem,) * 2,
         scratch_shapes=[pltpu.VMEM(x.shape, x.dtype) for x in ins]
         + [
-            pltpu.VMEM((depth, tiles.cols), bf16),
-            pltpu.VMEM((depth, tiles.cols), bf16),
             pltpu.VMEM((rows, features), bf16),
             pltpu.VMEM((2 * rank, units), f32),
             pltpu.VMEM((2 * rank, lane), f32),
             pltpu.SemaphoreType.DMA((5,)),
-            pltpu.SemaphoreType.DMA((2, n)),
         ],
         compiler_params=pltpu.CompilerParams(vmem_limit_bytes=62 * MiB),
         cost_estimate=small_cost,
-        name="first",
-    )(*ins, wg, wu)
-
-
-def base_part(xn, wg, wu, tiles, dy, dz1, dtype):
+        name="prep",
+    )(*ins)
+
+
+def base_kernel(tiles, blocks, n, width, xn_ref, wg_ref, wu_ref, *refs):
+    outs = refs[: len(blocks)]
+    wg, wu, sems = refs[len(blocks) :]
+    p, y, z1, z2 = cube()
+    jobs = []
+    for b, (dy, dz1) in enumerate(blocks):
+        at = tiles.start(y ^ dy, z1 ^ dz1)
+        for c in range(n):
+            for src, dst, slot, s in ((wg_ref, wg, 0, 0), (wu_ref, wu, 1, 1)):
+                span = pl.ds(c * width, width)
+                copy = pltpu.make_async_copy(
+                    src.at[:, pl.ds(pl.multiple_of(at + c * width, lane), width)],
+                    dst.at[b, :, span],
+                    sems.at[b, s, c],
+                )
+                jobs.append((copy, dst.at[b, :, span], outs[b], slot, span))
+    ahead = 2 * n
+    for job in jobs[:ahead]:
+        job[0].start()
+    xn = xn_ref[...]
+    for i, (copy, weights, out, slot, span) in enumerate(jobs):
+        copy.wait()
+        if i + ahead < len(jobs):
+            jobs[i + ahead][0].start()
+        out[slot, :, span] = dot_nn(xn, weights[...]).astype(out.dtype)
+
+
+def base_part(xn, wg, wu, tiles, blocks, dtype):
     n, width = chunks_of(tiles.cols, 512)
     rows, depth = xn.shape
+    k = len(blocks)
     return pl.pallas_call(
-        functools.partial(base_kernel, tiles, dy, dz1, n, width),
-        out_shape=jax.ShapeDtypeStruct((2, rows, tiles.cols), dtype),
+        functools.partial(base_kernel, tiles, blocks, n, width),
+        out_shape=(jax.ShapeDtypeStruct((2, rows, tiles.cols), dtype),) * k,
         in_specs=[in_vmem, in_hbm, in_hbm],
-        out_specs=in_vmem,
+        out_specs=(in_vmem,) * k,
         scratch_shapes=[
-            pltpu.VMEM((depth, tiles.cols), bf16),
-            pltpu.VMEM((depth, tiles.cols), bf16),
-            pltpu.SemaphoreType.DMA((2, n)),
+            pltpu.VMEM((k, depth, tiles.cols), bf16),
+            pltpu.VMEM((k, depth, tiles.cols), bf16),
+            pltpu.SemaphoreType.DMA((k, 2, n)),
         ],
         compiler_params=pltpu.CompilerParams(vmem_limit_bytes=44 * MiB),
         cost_estimate=small_cost,
-        name=f"base_y{dy}_z{dz1}",
+        name="base_" + "_".join(f"y{dy}z{dz1}" for dy, dz1 in blocks),
     )(xn, wg, wu)
 
 
@@ -322,100 +304,129 @@
     )(near, far)
 
 
-def hidden_kernel(
-    tiles, dy, dz1, first, last, rows, down_scale, mix_ref, near_ref, far_ref, pair_ref, wd_ref, dif_ref, *rest
-):
+def hidden_kernel(tiles, blocks, held, loads, first, last, ahead, rows, down_scale, *refs):
+    refs = list(refs)
+    take = lambda: refs.pop(0)
     p, y, z1, z2 = cube()
-    rest = list(rest)
-    acc_in, low_in = (None, None) if first else (rest.pop(0), rest.pop(0))
-    if last:
-        dout_ref, send_ref, keep_ref = rest.pop(0), rest.pop(0), rest.pop(0)
-    else:
-        acc_out, low_out = rest.pop(0), rest.pop(0)
-    right_ref, hid_ref, wd, sem = rest[:4]
+    mix_ref, near_ref, far_ref = take(), take(), take()
+    pair_refs = [take() for _ in blocks]
+    wd = [take() for _ in range(held)]
+    wd_ref = take() if loads else None
+    dif_ref = take()
+    acc_in, low_in = (None, None) if first else (take(), take())
+    dout_ref = take() if last else None
+    a_out, b_out = take(), take()
+    wd_out = take() if ahead else None
+    right_ref, hid_ref = take(), take()
+    starts = [tiles.start(y ^ dy, z1 ^ dz1) for dy, dz1 in blocks]
+    copies = []
+    if loads:
+        wd_held, sems = (take(), take()) if held < len(blocks) else (None, take())
+        places = []
+        for b in range(held, len(blocks)):
+            wd.append(wd_held.at[b - held])
+            places.append((starts[b], wd[b]))
+        if ahead:
+            places.append((tiles.start(y ^ ahead[0], z1 ^ ahead[1]), wd_out))
+        for b, (at, place) in enumerate(places):
+            copies.append(pltpu.make_async_copy(wd_ref.at[pl.ds(at, tiles.cols), :], place, sems.at[b]))
+        copies[0].start()
     group = near_ref.shape[1]
-    zb = z1 ^ dz1
-    at = tiles.start(y ^ dy, zb)
-    copy = pltpu.make_async_copy(wd_ref.at[pl.ds(at, tiles.cols), :], wd, sem)
-    copy.start()
-    for q in range(8):
-        ref = near_ref if q < 4 else far_ref
-        right_ref[q * group : (q + 1) * group, :] = ref[q % 4, :, pl.ds(at, tiles.cols)]
     top = 8 * group
-    right_ref[top : top + rows, :] = pair_ref[z2]
-    right_ref[top + rows : top + 2 * rows, :] = pair_ref[1 - z2]
     mix = mix_ref[...]
     height = mix.shape[0] // 2
+    out = wd[0].shape[1]
+    part = height // 2
+    started, waited = 1, 0
+    low = None if first else low_in[...]
     n, width = chunks_of(tiles.cols, 640)
-    for c in range(n):
-        span = pl.ds(c * width, width)
-        both = dot_nn(mix, right_ref[:, span])
-        gate, up = both[:height], both[height:]
-        hidden = (gate + gate * jnp.tanh(gate)) * up
-        if c * width < tiles.repeat * lane:
-            col = lax.broadcasted_iota(jnp.int32, hidden.shape, 1) + c * width
-            hidden = jnp.where(col >= zb * (tiles.repeat * lane), hidden, 0.0)
-        hid_ref[:, span] = hidden.astype(bf16)
-    hidden = hid_ref[...]
-    low = dot_nt(hidden, dif_ref[:, pl.ds(at, tiles.cols)])
-    low = low if first else low + low_in[...]
+    for b, ((dy, dz1), at, pair_ref) in enumerate(zip(blocks, starts, pair_refs)):
+        for q in range(8):
+            ref = near_ref if q < 4 else far_ref
+            right_ref[q * group : (q + 1) * group, :] = ref[q % 4, :, pl.ds(at, tiles.cols)]
+        right_ref[top : top + rows, :] = pair_ref[0]
+        right_ref[top + rows : top + 2 * rows, :] = pair_ref[1]
+        for c in range(n):
+            span = pl.ds(c * width, width)
+            both = dot_nn(mix, right_ref[:, span])
+            gate, up = both[:height], both[height:]
+            hidden = (gate + gate * jnp.tanh(gate)) * up
+            if c * width < tiles.repeat * lane:
+                col = lax.broadcasted_iota(jnp.int32, hidden.shape, 1) + c * width
+                hidden = jnp.where(col >= (z1 ^ dz1) * (tiles.repeat * lane), hidden, 0.0)
+            hid_ref[:, span] = hidden.astype(bf16)
+        hidden = hid_ref[...]
+        more = dot_nt(hidden, dif_ref[:, pl.ds(at, tiles.cols)])
+        low = more if low is None else low + more
+        if last:
+            t = lax.axis_index("tensor")
+            terms = dif_ref.shape[0]
+            r = lax.broadcasted_iota(jnp.int32, (height, terms), 0)
+            c = lax.broadcasted_iota(jnp.int32, (height, terms), 1)
+            mine = count_steps(r, rows, 8) == count_steps(c, terms // 8, 8)
+            low = jnp.where(mine, low * down_scale, 0.0)
+        if started < len(copies):
+            copies[started].start()
+            started += 1
+        if b >= held and copies:
+            copies[waited].wait()
+            waited += 1
+        for c in range(out // 256):
+            cols = pl.ds(c * 256, 256)
+            acc = dot_nn(hidden, wd[b][:, cols])
+            if b > 0:
+                acc = acc + a_out[:, cols]
+            elif not first:
+                acc = acc + acc_in[:, cols]
+            if not last:
+                a_out[:, cols] = acc
+            else:
+                acc = acc + dot_nn(low, dout_ref[:, cols].astype(f32), precision=lax.Precision.HIGHEST)
+                a_out[:, cols] = jnp.where(t == 0, acc[part:], acc[:part])
+                b_out[:, cols] = jnp.where(t == 0, acc[:part], acc[part:])
     if not last:
-        low_out[...] = low
-    else:
-        t = lax.axis_index("tensor")
-        terms = dif_ref.shape[0]
-        rank = terms // 8
-        r = lax.broadcasted_iota(jnp.int32, (height, terms), 0)
-        c = lax.broadcasted_iota(jnp.int32, (height, terms), 1)
-        mine = count_steps(r, rows, 8) == count_steps(c, rank, 8)
-        low = jnp.where(mine, low * down_scale, 0.0)
-        low_ref = rest[4]
-        low_ref[...] = low
-    out = wd_ref.shape[1]
-    part = height // 2
-    copy.wait()
-    for c in range(out // 256):
-        cols = pl.ds(c * 256, 256)
-        acc = dot_nn(hidden, wd[:, cols])
-        if not first:
-            acc = acc + acc_in[:, cols]
-        if not last:
-            acc_out[:, cols] = acc
-        else:
-            acc = acc + dot_nn(low, dout_ref[:, cols].astype(f32), precision=lax.Precision.HIGHEST)
-            keep_ref[:, cols] = jnp.where(t == 0, acc[:part], acc[part:])
-            send_ref[:, cols] = jnp.where(t == 0, acc[part:], acc[:part])
-
-
-def hidden_step(mix, near, far, pair, wd, dif, tiles, dy, dz1, rows, scale, state=None, dout=None):
+        b_out[...] = low
+    for copy in copies[waited:]:
+        copy.wait()
+
+
+def hidden_step(mix, near, far, pairs, wds, dif, tiles, blocks, rows, scale, state=None, dout=None, ahead=None):
     height = mix.shape[0] // 2
-    out = wd.shape[1]
+    out = wds[0].shape[1]
     terms = dif.shape[0]
-    first, last = state is None, dout is not None
-    args = [mix, near, far, pair, wd, dif]
+    first, last, k = state is None, dout is not None, len(blocks)
+    loads = wds[-1].shape[0] != tiles.cols
+    held = len(wds) - loads
+    args = [mix, near, far, *pairs, *wds, dif]
+    specs = [in_vmem] * (3 + k + held) + [in_hbm] * loads + [in_vmem]
     if not first:
         args += list(state)
+    if last:
+        args.append(dout)
+    specs += [in_vmem] * (len(args) - len(specs))
     scratch = [
         pltpu.VMEM((mix.shape[1], tiles.cols), bf16),
         pltpu.VMEM((height, tiles.cols), bf16),
-        pltpu.VMEM((tiles.cols, out), bf16),
-        pltpu.SemaphoreType.DMA,
     ]
     if last:
-        args.append(dout)
         shapes = [jax.ShapeDtypeStruct((height // 2, out), f32)] * 2
-        scratch.append(pltpu.VMEM((height, terms), f32))
     else:
         shapes = [jax.ShapeDtypeStruct((height, out), f32), jax.ShapeDtypeStruct((height, terms), f32)]
+    if loads:
+        if held < k:
+            scratch.append(pltpu.VMEM((k - held, tiles.cols, out), bf16))
+        scratch.append(pltpu.SemaphoreType.DMA((k + 1,)))
+    if ahead:
+        shapes.append(jax.ShapeDtypeStruct((tiles.cols, out), bf16))
     return pl.pallas_call(
-        functools.partial(hidden_kernel, tiles, dy, dz1, first, last, rows, scale),
+        functools.partial(hidden_kernel, tiles, blocks, held, loads, first, last, ahead, rows, scale),
         out_shape=tuple(shapes),
-        in_specs=[in_vmem] * 4 + [in_hbm] + [in_vmem] * (len(args) - 5),
-        out_specs=(in_vmem, in_vmem),
+        in_specs=specs,
+        out_specs=(in_vmem,) * len(shapes),
         scratch_shapes=scratch,
-        compiler_params=pltpu.CompilerParams(vmem_limit_bytes=44 * MiB),
+        compiler_params=pltpu.CompilerParams(vmem_limit_bytes=(41 if loads else 16) * MiB),
         cost_estimate=small_cost,
-        name=f"hidden_y{dy}_z{dz1}",
+        name="hidden_" + "_".join(f"y{dy}z{dz1}" for dy, dz1 in blocks),
     )(*args)
 
 
@@ -557,40 +568,36 @@
         turned(up_output_factors)[0],
     )
     after = lambda x, *done: lax.optimization_barrier((x, *done))[0]
-    part = lambda x, *a: base_part(x, gate_weight, up_weight, tiles, *a)
-
-    xn, fac, far0 = first_part(ins, gate_weight, up_weight, tiles, 1, 1, bf16)
-    far0 = over_y(far0)
+    part = lambda x, blocks, dtype: base_part(x, gate_weight, up_weight, tiles, blocks, dtype)
+
+    head_rows = lax.dynamic_slice_in_dim(label_head, (p * block) % label_head.shape[0], block, 0)
+    head = jnp.where((p * block) // label_head.shape[0] == t, head_rows, over_t(head_rows))
+
+    xn, fac = prep(ins, block)
     fac_z2 = over_z2(fac)
-    far1 = part(xn, 1, 0, bf16)
+    far0, far1 = part(xn, ((1, 1), (1, 0)), bf16)
     xn, dif, dout = lax.optimization_barrier((xn, dif, dout, far1, fac_z2))[:3]
-    far1 = over_y(far1)
+    far0, far1 = over_y(far0), over_y(far1)
     two = jnp.stack([fac, fac_z2])
     two_z1 = over_z1(two)
-    near0 = part(xn, 0, 1, f32)
+    (near0,) = part(xn, ((0, 1),), f32)
     from_z1 = over_z1((near0 + far0.astype(f32)).astype(bf16))
-    near1 = part(after(xn, near0), 0, 0, f32)
+    (near1,) = part(after(xn, near0, two_z1, head), ((0, 0),), f32)
     four = jnp.concatenate([two, two_z1])
     far_four = over_y(four)
 
-    head_rows = lax.dynamic_slice_in_dim(label_head, (p * block) % label_head.shape[0], block, 0)
-    head = jnp.where((p * block) // label_head.shape[0] == t, head_rows, over_t(head_rows))
-
     mine = near1 + far1.astype(f32) + from_z1.astype(f32)
-    send = mine[0].astype(bf16)
-    total = (mine[1] + over_z2(send).astype(f32)).astype(bf16)
-    pair = jnp.stack([total, after(over_z2(total), head)])
+    pair = (mine + over_z2(mine.astype(bf16)).astype(f32)).astype(bf16)
 
     mix = mixing(four, far_four, rows)
     step = functools.partial(hidden_step, mix, four, far_four)
     tail, wd = (dif, tiles), down_weight_matrix
     pair_z = over_z1(pair)
     pair_y = over_y(pair)
-    state = step(pair, wd, *tail, 0, 0, rows, down_scale)
-    pair_yz = over_y(pair_z)
-    state = step(pair_z, wd, *tail, 0, 1, rows, down_scale, state)
-    state = step(pair_y, wd, *tail, 1, 0, rows, down_scale, state)
-    send, keep = step(pair_yz, wd, *tail, 1, 1, rows, down_scale, state, dout)
+    *state, wd1 = step((pair,), (wd,), *tail, ((0, 0),), rows, down_scale, ahead=(0, 1))
+    pair_yz = over_y(after(pair_z, state[0]))
+    *state, wd3 = step((pair_z, pair_y), (wd1, wd), *tail, ((0, 1), (1, 0)), rows, down_scale, state, ahead=(1, 1))
+    send, keep = step((pair_yz,), (wd3,), *tail, ((1, 1),), rows, down_scale, state, dout)
 
     logits = part_logits(keep, over_t(send), prompts, head)
     logits = logits + over_y(logits)

time: 91.9 us -> 79.3 us (0.86)
  starting transfers between devices: 25.4 us -> 20 us
  Pallas kernels: 39.6 us -> 35 us
  waiting for transfers between devices: 24.1 us -> 19.6 us
  other arithmetic: 0.34 us -> 1.35 us
  local copies, waits for them, and re-layouts: 1.07 us -> 2 us
    ppermute x17 -> x16, starting transfers between devices: 25.4 us -> 20 us  [swap(): return lax.ppermute(x, axis, [(i, i ^ bit) for i in range(size)])]
    pallas_call x8 -> x7, Pallas kernels: 32.5 us -> 27.9 us  [the longest x3 14.2 us: base_part(): pl.pallas_call(functools.partial(base_kernel, tiles, blocks, n, width), o...]
    ppermute x17 -> x16, waiting for transfers between devices: 24.1 us -> 19.6 us  [swap(): return lax.ppermute(x, axis, [(i, i ^ bit) for i in range(size)])]
    select_n x1, other arithmetic: 0.07 us -> 1.02 us  [cube_body(): jnp.where(p * block // label_head.shape[0] == t, head_rows, over_t(head_r...]
    dynamic_slice x1, local copies, waits for them, and re-layouts: 0.02 us -> 0.97 us  [cube_body(): lax.dynamic_slice_in_dim(label_head, p * block % label_head.shape[0], blo...]
  transfers between devices with their start and end apart: 17 -> 16, of which waited for: 11 -> 6; matrix products, arithmetic and copies ran while one was open for 1% -> 3% of each run, Pallas kernels for 25% -> 29%
where the time goes in v3:
time: 79.3 us; the launch traced here: 79 us
  Pallas kernels  35 us (44%)
  starting transfers between devices  20 us (25%)
  waiting for transfers between devices  19.6 us (25%)
  local copies, waits for them, and re-layouts  2 us (3%)
  other arithmetic  1.35 us (2%)
  between operations  1.06 us (1%)
    ppermute x16, starting transfers between devices, swap(): return lax.ppermute(x, axis, [(i, i ^ bit) for i in range(size)])  20 us
    ppermute x16, waiting for transfers between devices, swap(): return lax.ppermute(x, axis, [(i, i ^ bit) for i in range(size)])  19.6 us
    pallas_call x3, Pallas kernels, base_part(): pl.pallas_call(functools.partial(base_kernel, tiles, blocks, n, width), o...  14.2 us
    pallas_call x3, Pallas kernels, hidden_step(): pl.pallas_call(functools.partial(hidden_kernel, tiles, blocks, held, load...  11.4 us
    pallas_call x1, Pallas kernels, updates(): pl.pallas_call(functools.partial(update_kernel, n, high), out_shape=(jax....  6.46 us
    pallas_call x1, Pallas kernels, prep(): pl.pallas_call(prep_kernel, out_shape=(jax.ShapeDtypeStruct((rows, block)...  2.32 us
  transfers between devices with their start and end apart: 16, of which 6 were waited for; matrix products, arithmetic and copies ran while one was open for 3% of the time, Pallas kernels for 29%

profile of v3, /device:TPU:0, one launch (start us, length us, event | category | flops | bytes accessed | tf_op | source)
XLA Modules:
  0.0 79.0 jit_solution(16479382528430011540)
XLA Ops:
  0.6 2.3 %prep.1 = (bf16[24,1024]{1,0:T(8,128)(2,1)}, bf16[8,7552]{1,0:T(8,128)(2,1)}) custom-call(bf16[24,8192]{1,0:T(8,128)(2,1)} %x_ref.1, bf16[4,8192]{1,0:T(4,128)(2,1)} %bitcast.24, bf16[4,8192]{1,0:T(4,128)(2,1)} %bitcast.25, bf16[4,7424]{1,0:T(4,128)(2,1)} %bitcast.27, bf16[4,7424]{1,0:T(4,128)(2,1)} %bitcast.28), custom_call_target="tpu_custom_call" | custom-call | flops 1024 | bytes 1024 | tf_op jit(solution)/shard_map/prep/pallas_call | solution.py:187
  3.0 4.1 %collective-permute-start = (bf16[8,7552]{1,0:T(8,128)(2,1)}, bf16[8,7552]{1,0:T(8,128)(2,1)S(1)}, u32[]{:S(2)}, u32[]{:S(2)}) collective-permute-start(bf16[8,7552]{1,0:T(8,128)(2,1)} %get-tuple-element.21), channel_id=1, source_target_pairs={{0,8},{2,10},{4,12},{6,14},{8,0},{10,2},{12,4},{14,6},{1,9},{3,11}... | collective-permute-start | bytes 362504 | tf_op jit(solution)/shard_map/ppermute | solution.py:154
  7.1 1.0 %constant_dynamic-slice_fusion = bf16[1024,128]{1,0:T(8,128)(2,1)S(1)} fusion(bf16[4096,128]{1,0:T(8,128)(2,1)} %param.22, s32[]{:T(128)S(6)} %select_n.25), kind=kLoop, calls=%fused_computation.7 | loop fusion | bytes 524292 | tf_op jit(solution)/shard_map/dynamic_slice | solution.py:573
  8.0 0.1 collective-permute-start.3
  8.1 0.8 copy-done.1
  8.9 6.6 %base_y1z1_y1z0.1 = (bf16[2,24,1920]{2,1,0:T(8,128)(2,1)S(1)}, bf16[2,24,1920]{2,1,0:T(8,128)(2,1)S(1)}) custom-call(bf16[24,1024]{1,0:T(8,128)(2,1)S(1)} %copy-done.1, bf16[1024,7424]{1,0:T(8,128)(2,1)} %wg_ref.5, bf16[1024,7424]{1,0:T(8,128)(2,1)} %wu_ref.5), custom_call_target="tpu_custom_call" | custom-call | flops 1024 | bytes 1024 | tf_op jit(solution)/shard_map/base_y1z1_y1z0/pallas_call | solution.py:239
  15.5 1.6 %collective-permute-start.5 = (bf16[2,24,1920]{2,1,0:T(8,128)(2,1)S(1)}, bf16[2,24,1920]{2,1,0:T(8,128)(2,1)S(1)}, u32[]{:S(2)}, u32[]{:S(2)}) collective-permute-start(bf16[2,24,1920]{2,1,0:T(8,128)(2,1)S(1)} %get-tuple-element.26), channel_id=1, source_target_pairs={{0,2},{2,0},{4,6},{6,4},{8,10},{10,8},{12,14},{14,12},{1,3},{3,1},... | collective-permute-start | bytes 552968 | tf_op jit(solution)/shard_map/ppermute | solution.py:154
  17.1 0.5 collective-permute-start.4
  17.6 0.1 reshape.13.refs_5_.refs_7_.dif_ref
  17.8 0.0 collective-permute-done
  17.8 1.6 %collective-permute-start.1 = (bf16[2,8,7552]{2,1,0:T(8,128)(2,1)S(1)}, bf16[2,8,7552]{2,1,0:T(8,128)(2,1)S(1)}, u32[]{:S(2)}, u32[]{:S(2)}) collective-permute-start(bf16[2,8,7552]{2,1,0:T(8,128)(2,1)S(1)} %pad_maximum_fusion.1), channel_id=1, source_target_pairs={{0,4},{2,6},{4,0},{6,2},{8,12},{10,14},{12,8},{14,10},{1,5},{3,7},... | collective-permute-start | bytes 725000 | tf_op jit(solution)/shard_map/ppermute | solution.py:154
  19.5 3.8 %base_y0z1.1 = f32[2,24,1920]{2,1,0:T(8,128)S(1)} custom-call(bf16[24,1024]{1,0:T(8,128)(2,1)S(1)} %copy-done.2, bf16[1024,7424]{1,0:T(8,128)(2,1)} %wg_ref.5, bf16[1024,7424]{1,0:T(8,128)(2,1)} %wu_ref.5), custom_call_target="tpu_custom_call" | custom-call | flops 1024 | bytes 1024 | tf_op jit(solution)/shard_map/base_y0z1/pallas_call | solution.py:239
  23.3 1.4 %collective-permute-start.6 = (bf16[2,24,1920]{2,1,0:T(8,128)(2,1)S(1)}, bf16[2,24,1920]{2,1,0:T(8,128)(2,1)S(1)}, u32[]{:S(2)}, u32[]{:S(2)}) collective-permute-start(bf16[2,24,1920]{2,1,0:T(8,128)(2,1)S(1)} %add_convert_fusion.1), channel_id=1, source_target_pairs={{0,4},{2,6},{4,0},{6,2},{8,12},{10,14},{12,8},{14,10},{1,5},{3,7},... | collective-permute-start | bytes 552968 | tf_op jit(solution)/shard_map/ppermute | solution.py:154
  24.7 0.0 collective-permute-done.3
  24.7 1.0 %broadcast_select_fusion.head_ref = bf16[1024,128]{1,0:T(8,128)(2,1)S(1)} fusion(bf16[1024,128]{1,0:T(8,128)(2,1)S(1)} %collective-permute-done.3, pred[]{:T(512)S(6)} %eq.5, bf16[4096,128]{1,0:T(8,128)(2,1)} %param.22, s32[]{:T(128)S(6)} %select_n.25), kind=kLoop, calls=%fused_computation.4 | loop fusion | flops 131072 | bytes 786437 | tf_op jit(solution)/shard_map/jit(_where)/select_n | solution.py:574
  25.7 3.8 %base_y0z0.1 = f32[2,24,1920]{2,1,0:T(8,128)S(1)} custom-call(bf16[24,1024]{1,0:T(8,128)(2,1)S(1)} %copy-done.2, bf16[1024,7424]{1,0:T(8,128)(2,1)} %wg_ref.5, bf16[1024,7424]{1,0:T(8,128)(2,1)} %wu_ref.5), custom_call_target="tpu_custom_call" | custom-call | flops 1024 | bytes 1024 | tf_op jit(solution)/shard_map/base_y0z0/pallas_call | solution.py:239
  29.5 0.0 collective-permute-done.4
  29.6 0.0 collective-permute-done.6
  29.6 0.1 fusion
  29.7 0.4 collective-permute-start.7
  30.1 0.1 pad_maximum_fusion.near_ref.refs_1_
  30.1 1.6 %collective-permute-start.2 = (bf16[4,8,7552]{2,1,0:T(8,128)(2,1)S(1)}, bf16[4,8,7552]{2,1,0:T(8,128)(2,1)S(1)}, u32[]{:S(2)}, u32[]{:S(2)}) collective-permute-start(bf16[4,8,7552]{2,1,0:T(8,128)(2,1)S(1)} %pad_maximum_fusion.near_ref.refs_1_), channel_id=1, source_target_pairs={{0,2},{2,0},{4,6},{6,4},{8,10},{10,8},{12,14},{14,12},{1,3},{3,1},... | collective-permute-start | bytes 1449992 | tf_op jit(solution)/shard_map/ppermute | solution.py:154
  31.7 8.4 %collective-permute-done.7 = bf16[2,24,1920]{2,1,0:T(8,128)(2,1)S(1)} collective-permute-done((bf16[2,24,1920]{2,1,0:T(8,128)(2,1)S(1)}, bf16[2,24,1920]{2,1,0:T(8,128)(2,1)S(1)}, u32[]{:S(2)}, u32[]{:S(2)}) %collective-permute-start.7) | collective-permute-done | bytes 184352 | tf_op jit(solution)/shard_map/ppermute | solution.py:154
  40.1 0.1 add_convert_fusion.refs_3_
  40.2 0.1 collective-permute-start.8
  40.3 1.6 %collective-permute-start.10 = (bf16[2,24,1920]{2,1,0:T(8,128)(2,1)S(1)}, bf16[2,24,1920]{2,1,0:T(8,128)(2,1)S(1)}, u32[]{:S(2)}, u32[]{:S(2)}) collective-permute-start(bf16[2,24,1920]{2,1,0:T(8,128)(2,1)S(1)} %add_convert_fusion.refs_3_), channel_id=1, source_target_pairs={{0,2},{2,0},{4,6},{6,4},{8,10},{10,8},{12,14},{14,12},{1,3},{3,1},... | collective-permute-start | bytes 552968 | tf_op jit(solution)/shard_map/ppermute | solution.py:154
  41.9 0.0 collective-permute-done.2.far_ref.refs_2_
  41.9 0.2 mixing.1.refs_0_
  42.1 3.8 %hidden_y0z0.1 = (f32[192,1024]{1,0:T(8,128)S(1)}, f32[192,32]{1,0:T(8,128)S(1)}, bf16[1920,1024]{1,0:T(8,128)(2,1)S(1)}) custom-call(bf16[384,112]{1,0:T(8,128)(2,1)S(1)} %mixing.1.refs_0_, bf16[4,8,7552]{2,1,0:T(8,128)(2,1)S(1)} %pad_maximum_fusion.near_ref.refs_1_, bf16[4,8,7552]{2,1,0:T(8,128)(2,1)S(1)} %collective-permute-done.2.far_ref.refs_2_, ...), custom_call_target="tpu_custom_call" | custom-call | flops 1024 | bytes 1024 | tf_op jit(solution)/shard_map/hidden_y0z0/pallas_call | solution.py:421
  45.9 0.0 copy-start
  45.9 0.0 copy-start.6
  46.0 1.6 %collective-permute-start.9 = (bf16[2,24,1920]{2,1,0:T(8,128)(2,1)S(1)}, bf16[2,24,1920]{2,1,0:T(8,128)(2,1)S(1)}, u32[]{:S(2)}, u32[]{:S(2)}) collective-permute-start(bf16[2,24,1920]{2,1,0:T(8,128)(2,1)S(1)} %collective-permute-done.8.refs_3_), channel_id=1, source_target_pairs={{0,2},{2,0},{4,6},{6,4},{8,10},{10,8},{12,14},{14,12},{1,3},{3,1},... | collective-permute-start | bytes 552968 | tf_op jit(solution)/shard_map/ppermute | solution.py:154
  47.5 5.1 %hidden_y0z1_y1z0.1 = (f32[192,1024]{1,0:T(8,128)S(1)}, f32[192,32]{1,0:T(8,128)S(1)}, bf16[1920,1024]{1,0:T(8,128)(2,1)S(1)}) custom-call(bf16[384,112]{1,0:T(8,128)(2,1)S(1)} %mixing.1.refs_0_, bf16[4,8,7552]{2,1,0:T(8,128)(2,1)S(1)} %pad_maximum_fusion.near_ref.refs_1_, bf16[4,8,7552]{2,1,0:T(8,128)(2,1)S(1)} %collective-permute-done.2.far_ref.refs_2_, ...), custom_call_target="tpu_custom_call" | custom-call | flops 1024 | bytes 1024 | tf_op jit(solution)/shard_map/hidden_y0z1_y1z0/pallas_call | solution.py:421
  52.7 2.5 %hidden_y1z1.1 = (f32[96,1024]{1,0:T(8,128)S(1)}, f32[96,1024]{1,0:T(8,128)S(1)}) custom-call(bf16[384,112]{1,0:T(8,128)(2,1)S(1)} %mixing.1.refs_0_, bf16[4,8,7552]{2,1,0:T(8,128)(2,1)S(1)} %pad_maximum_fusion.near_ref.refs_1_, bf16[4,8,7552]{2,1,0:T(8,128)(2,1)S(1)} %collective-permute-done.2.far_ref.refs_2_, ...), custom_call_target="tpu_custom_call" | custom-call | flops 1024 | bytes 1024 | tf_op jit(solution)/shard_map/hidden_y1z1/pallas_call | solution.py:421
  55.2 0.1 collective-permute-start.11
  55.2 1.7 %collective-permute-done.11.recv_ref = f32[96,1024]{1,0:T(8,128)S(1)} collective-permute-done((f32[96,1024]{1,0:T(8,128)S(1)}, f32[96,1024]{1,0:T(8,128)S(1)}, u32[]{:S(2)}, u32[]{:S(2)}) %collective-permute-start.11) | collective-permute-done | bytes 393248 | tf_op jit(solution)/shard_map/ppermute | solution.py:154
  57.0 0.3 part_logits.1
  57.2 0.6 collective-permute-start.12
  57.8 3.6 %collective-permute-done.12 = f32[104,128]{1,0:T(8,128)S(1)} collective-permute-done((f32[104,128]{1,0:T(8,128)S(1)}, f32[104,128]{1,0:T(8,128)S(1)}, u32[]{:S(2)}, u32[]{:S(2)}) %collective-permute-start.12) | collective-permute-done | bytes 53280 | tf_op jit(solution)/shard_map/ppermute | solution.py:154
  61.5 1.5 %collective-permute-start.13 = (f32[104,128]{1,0:T(8,128)S(1)}, f32[104,128]{1,0:T(8,128)S(1)}, u32[]{:S(2)}, u32[]{:S(2)}) collective-permute-start(f32[104,128]{1,0:T(8,128)S(1)} %add.32), channel_id=1, source_target_pairs={{0,4},{2,6},{4,0},{6,2},{8,12},{10,14},{12,8},{14,10},{1,5},{3,7},... | collective-permute-start | bytes 159752 | tf_op jit(solution)/shard_map/ppermute | solution.py:154
  63.0 2.7 %collective-permute-done.13 = f32[104,128]{1,0:T(8,128)S(1)} collective-permute-done((f32[104,128]{1,0:T(8,128)S(1)}, f32[104,128]{1,0:T(8,128)S(1)}, u32[]{:S(2)}, u32[]{:S(2)}) %collective-permute-start.13) | collective-permute-done | bytes 53280 | tf_op jit(solution)/shard_map/ppermute | solution.py:154
  65.7 3.2 %collective-permute-start.14 = (f32[104,128]{1,0:T(8,128)S(1)}, f32[104,128]{1,0:T(8,128)S(1)}, u32[]{:S(2)}, u32[]{:S(2)}) collective-permute-start(f32[104,128]{1,0:T(8,128)S(1)} %add.33.a_ref), channel_id=1, source_target_pairs={{0,8},{2,10},{4,12},{6,14},{8,0},{10,2},{12,4},{14,6},{1,9},{3,11}... | collective-permute-start | bytes 159752 | tf_op jit(solution)/shard_map/ppermute | solution.py:154
  68.9 0.1 copy.14.targets_ref
  68.9 2.0 %collective-permute-done.14.b_ref = f32[104,128]{1,0:T(8,128)S(1)} collective-permute-done((f32[104,128]{1,0:T(8,128)S(1)}, f32[104,128]{1,0:T(8,128)S(1)}, u32[]{:S(2)}, u32[]{:S(2)}) %collective-permute-start.14) | collective-permute-done | bytes 53280 | tf_op jit(solution)/shard_map/ppermute | solution.py:154
  71.0 0.2 part_rewards.1.a_ref
  71.2 0.1 collective-permute-start.15
  71.3 1.2 %collective-permute-done.15.b_ref = f32[8,128]{1,0:T(8,128)S(1)} collective-permute-done((f32[8,128]{1,0:T(8,128)S(1)}, f32[8,128]{1,0:T(8,128)S(1)}, u32[]{:S(2)}, u32[]{:S(2)}) %collective-permute-start.15) | collective-permute-done | bytes 4128 | tf_op jit(solution)/shard_map/ppermute | solution.py:154
  72.4 6.5 %updates.1 = (bf16[7424,1024]{1,0:T(8,128)(2,1)}, f32[1,128]{1,0:T(1,128)}) custom-call(f32[8,128]{1,0:T(8,128)S(1)} %part_rewards.1.a_ref, f32[8,128]{1,0:T(8,128)S(1)} %collective-permute-done.15.b_ref, bf16[32,7424]{1,0:T(8,128)(2,1)S(1)} %reshape.13.refs_5_.refs_7_.dif_ref, bf16[32,1024]{1,0:T(8,128)(2,1)S(1)} %reshape.14.refs_8_.dout_ref), custom_call_target="tpu_custom_call" | custom-call | tf_op jit(solution)/shard_map/updates/pallas_call | solution.py:523
  (21 shorter events, 0.1 us)
Async XLA Ops:
  3.0 14.8 %collective-permute-start = (bf16[8,7552]{1,0:T(8,128)(2,1)}, bf16[8,7552]{1,0:T(8,128)(2,1)S(1)}, u32[]{:S(2)}, u32[]{:S(2)}) collective-permute-start(bf16[8,7552]{1,0:T(8,128)(2,1)} %get-tuple-element.21), channel_id=1, source_target_pairs={{0,8},{2,10},{4,12},{6,14},{8,0},{10,2},{12,4},{14,6},{1,9},{3,11}... | collective-permute-start | bytes 362504 | tf_op jit(solution)/shard_map/ppermute | solution.py:154
  8.0 16.7 %collective-permute-start.3 = (bf16[1024,128]{1,0:T(8,128)(2,1)S(1)}, bf16[1024,128]{1,0:T(8,128)(2,1)S(1)}, u32[]{:S(2)}, u32[]{:S(2)}) collective-permute-start(bf16[1024,128]{1,0:T(8,128)(2,1)S(1)} %constant_dynamic-slice_fusion), channel_id=1, source_target_pairs={{0,1},{1,0},{2,3},{3,2},{4,5},{5,4},{6,7},{7,6},{8,9},{9,8},{10,11... | collective-permute-start | bytes 786440 | tf_op jit(solution)/shard_map/ppermute | solution.py:154
  8.1 0.8 %copy-start.1 = (bf16[24,1024]{1,0:T(8,128)(2,1)S(1)}, bf16[24,1024]{1,0:T(8,128)(2,1)}, u32[]{:S(2)}) copy-start(bf16[24,1024]{1,0:T(8,128)(2,1)} %get-tuple-element.25.xn_ref) | copy-start | bytes 147460
  8.9 8.7 %copy-start.5 = (bf16[8,1024,4]{1,2,0:T(4,128)(2,1)S(1)}, bf16[8,1024,4]{1,2,0:T(4,128)(2,1)}, u32[]{:S(2)}) copy-start(bf16[8,1024,4]{1,2,0:T(4,128)(2,1)} %param.21) | copy-start | bytes 196612
  8.9 8.7 %copy-start.4 = (bf16[8,7424,4]{1,2,0:T(4,128)(2,1)S(1)}, bf16[8,7424,4]{1,2,0:T(4,128)(2,1)}, u32[]{:S(2)}) copy-start(bf16[8,7424,4]{1,2,0:T(4,128)(2,1)} %param.20) | copy-start | bytes 1425412
  8.9 8.9 %copy-start.3 = (bf16[8,7552]{1,0:T(8,128)(2,1)S(1)}, bf16[8,7552]{1,0:T(8,128)(2,1)}, u32[]{:S(2)}) copy-start(bf16[8,7552]{1,0:T(8,128)(2,1)} %get-tuple-element.21) | copy-start | bytes 362500
  8.9 10.6 %copy-start.2 = (bf16[24,1024]{1,0:T(8,128)(2,1)S(1)}, bf16[24,1024]{1,0:T(8,128)(2,1)}, u32[]{:S(2)}) copy-start(bf16[24,1024]{1,0:T(8,128)(2,1)} %get-tuple-element.25.xn_ref) | copy-start | bytes 147460
  15.5 7.8 %collective-permute-start.5 = (bf16[2,24,1920]{2,1,0:T(8,128)(2,1)S(1)}, bf16[2,24,1920]{2,1,0:T(8,128)(2,1)S(1)}, u32[]{:S(2)}, u32[]{:S(2)}) collective-permute-start(bf16[2,24,1920]{2,1,0:T(8,128)(2,1)S(1)} %get-tuple-element.26), channel_id=1, source_target_pairs={{0,2},{2,0},{4,6},{6,4},{8,10},{10,8},{12,14},{14,12},{1,3},{3,1},... | collective-permute-start | bytes 552968 | tf_op jit(solution)/shard_map/ppermute | solution.py:154
  17.1 12.5 %collective-permute-start.4 = (bf16[2,24,1920]{2,1,0:T(8,128)(2,1)S(1)}, bf16[2,24,1920]{2,1,0:T(8,128)(2,1)S(1)}, u32[]{:S(2)}, u32[]{:S(2)}) collective-permute-start(bf16[2,24,1920]{2,1,0:T(8,128)(2,1)S(1)} %get-tuple-element.23), channel_id=1, source_target_pairs={{0,2},{2,0},{4,6},{6,4},{8,10},{10,8},{12,14},{14,12},{1,3},{3,1},... | collective-permute-start | bytes 552968 | tf_op jit(solution)/shard_map/ppermute | solution.py:154
  17.8 7.9 %collective-permute-start.1 = (bf16[2,8,7552]{2,1,0:T(8,128)(2,1)S(1)}, bf16[2,8,7552]{2,1,0:T(8,128)(2,1)S(1)}, u32[]{:S(2)}, u32[]{:S(2)}) collective-permute-start(bf16[2,8,7552]{2,1,0:T(8,128)(2,1)S(1)} %pad_maximum_fusion.1), channel_id=1, source_target_pairs={{0,4},{2,6},{4,0},{6,2},{8,12},{10,14},{12,8},{14,10},{1,5},{3,7},... | collective-permute-start | bytes 725000 | tf_op jit(solution)/shard_map/ppermute | solution.py:154
  23.3 6.3 %collective-permute-start.6 = (bf16[2,24,1920]{2,1,0:T(8,128)(2,1)S(1)}, bf16[2,24,1920]{2,1,0:T(8,128)(2,1)S(1)}, u32[]{:S(2)}, u32[]{:S(2)}) collective-permute-start(bf16[2,24,1920]{2,1,0:T(8,128)(2,1)S(1)} %add_convert_fusion.1), channel_id=1, source_target_pairs={{0,4},{2,6},{4,0},{6,2},{8,12},{10,14},{12,8},{14,10},{1,5},{3,7},... | collective-permute-start | bytes 552968 | tf_op jit(solution)/shard_map/ppermute | solution.py:154
  29.7 10.5 %collective-permute-start.7 = (bf16[2,24,1920]{2,1,0:T(8,128)(2,1)S(1)}, bf16[2,24,1920]{2,1,0:T(8,128)(2,1)S(1)}, u32[]{:S(2)}, u32[]{:S(2)}) collective-permute-start(bf16[2,24,1920]{2,1,0:T(8,128)(2,1)S(1)} %fusion), channel_id=1, source_target_pairs={{0,8},{2,10},{4,12},{6,14},{8,0},{10,2},{12,4},{14,6},{1,9},{3,11}... | collective-permute-start | bytes 552968 | tf_op jit(solution)/shard_map/ppermute | solution.py:154
  30.1 11.8 %collective-permute-start.2 = (bf16[4,8,7552]{2,1,0:T(8,128)(2,1)S(1)}, bf16[4,8,7552]{2,1,0:T(8,128)(2,1)S(1)}, u32[]{:S(2)}, u32[]{:S(2)}) collective-permute-start(bf16[4,8,7552]{2,1,0:T(8,128)(2,1)S(1)} %pad_maximum_fusion.near_ref.refs_1_), channel_id=1, source_target_pairs={{0,2},{2,0},{4,6},{6,4},{8,10},{10,8},{12,14},{14,12},{1,3},{3,1},... | collective-permute-start | bytes 1449992 | tf_op jit(solution)/shard_map/ppermute | solution.py:154
  40.2 5.7 %collective-permute-start.8 = (bf16[2,24,1920]{2,1,0:T(8,128)(2,1)S(1)}, bf16[2,24,1920]{2,1,0:T(8,128)(2,1)S(1)}, u32[]{:S(2)}, u32[]{:S(2)}) collective-permute-start(bf16[2,24,1920]{2,1,0:T(8,128)(2,1)S(1)} %add_convert_fusion.refs_3_), channel_id=1, source_target_pairs={{0,4},{2,6},{4,0},{6,2},{8,12},{10,14},{12,8},{14,10},{1,5},{3,7},... | collective-permute-start | bytes 552968 | tf_op jit(solution)/shard_map/ppermute | solution.py:154
  40.3 7.2 %collective-permute-start.10 = (bf16[2,24,1920]{2,1,0:T(8,128)(2,1)S(1)}, bf16[2,24,1920]{2,1,0:T(8,128)(2,1)S(1)}, u32[]{:S(2)}, u32[]{:S(2)}) collective-permute-start(bf16[2,24,1920]{2,1,0:T(8,128)(2,1)S(1)} %add_convert_fusion.refs_3_), channel_id=1, source_target_pairs={{0,2},{2,0},{4,6},{6,4},{8,10},{10,8},{12,14},{14,12},{1,3},{3,1},... | collective-permute-start | bytes 552968 | tf_op jit(solution)/shard_map/ppermute | solution.py:154
  45.9 11.0 %copy-start = (bf16[24,8192]{1,0:T(8,128)(2,1)S(1)}, bf16[24,8192]{1,0:T(8,128)(2,1)}, u32[]{:S(2)}) copy-start(bf16[24,8192]{1,0:T(8,128)(2,1)} %x_ref.1) | copy-start | bytes 1179652
  45.9 22.9 %copy-start.6 = (s32[24]{0:T(128)S(1)}, s32[24]{0:T(128)}, u32[]{:S(2)}) copy-start(s32[24]{0:T(128)} %param.23) | copy-start | bytes 292
  46.0 6.7 %collective-permute-start.9 = (bf16[2,24,1920]{2,1,0:T(8,128)(2,1)S(1)}, bf16[2,24,1920]{2,1,0:T(8,128)(2,1)S(1)}, u32[]{:S(2)}, u32[]{:S(2)}) collective-permute-start(bf16[2,24,1920]{2,1,0:T(8,128)(2,1)S(1)} %collective-permute-done.8.refs_3_), channel_id=1, source_target_pairs={{0,2},{2,0},{4,6},{6,4},{8,10},{10,8},{12,14},{14,12},{1,3},{3,1},... | collective-permute-start | bytes 552968 | tf_op jit(solution)/shard_map/ppermute | solution.py:154
  55.2 1.8 %collective-permute-start.11 = (f32[96,1024]{1,0:T(8,128)S(1)}, f32[96,1024]{1,0:T(8,128)S(1)}, u32[]{:S(2)}, u32[]{:S(2)}) collective-permute-start(f32[96,1024]{1,0:T(8,128)S(1)} %get-tuple-element.37), channel_id=1, source_target_pairs={{0,1},{1,0},{2,3},{3,2},{4,5},{5,4},{6,7},{7,6},{8,9},{9,8},{10,11... | collective-permute-start | bytes 1179656 | tf_op jit(solution)/shard_map/ppermute | solution.py:154
  57.2 4.2 %collective-permute-start.12 = (f32[104,128]{1,0:T(8,128)S(1)}, f32[104,128]{1,0:T(8,128)S(1)}, u32[]{:S(2)}, u32[]{:S(2)}) collective-permute-start(f32[104,128]{1,0:T(8,128)S(1)} %part_logits.1), channel_id=1, source_target_pairs={{0,2},{2,0},{4,6},{6,4},{8,10},{10,8},{12,14},{14,12},{1,3},{3,1},... | collective-permute-start | bytes 159752 | tf_op jit(solution)/shard_map/ppermute | solution.py:154
  61.5 4.2 %collective-permute-start.13 = (f32[104,128]{1,0:T(8,128)S(1)}, f32[104,128]{1,0:T(8,128)S(1)}, u32[]{:S(2)}, u32[]{:S(2)}) collective-permute-start(f32[104,128]{1,0:T(8,128)S(1)} %add.32), channel_id=1, source_target_pairs={{0,4},{2,6},{4,0},{6,2},{8,12},{10,14},{12,8},{14,10},{1,5},{3,7},... | collective-permute-start | bytes 159752 | tf_op jit(solution)/shard_map/ppermute | solution.py:154
  65.7 5.3 %collective-permute-start.14 = (f32[104,128]{1,0:T(8,128)S(1)}, f32[104,128]{1,0:T(8,128)S(1)}, u32[]{:S(2)}, u32[]{:S(2)}) collective-permute-start(f32[104,128]{1,0:T(8,128)S(1)} %add.33.a_ref), channel_id=1, source_target_pairs={{0,8},{2,10},{4,12},{6,14},{8,0},{10,2},{12,4},{14,6},{1,9},{3,11}... | collective-permute-start | bytes 159752 | tf_op jit(solution)/shard_map/ppermute | solution.py:154
  71.2 1.2 %collective-permute-start.15 = (f32[8,128]{1,0:T(8,128)S(1)}, f32[8,128]{1,0:T(8,128)S(1)}, u32[]{:S(2)}, u32[]{:S(2)}) collective-permute-start(f32[8,128]{1,0:T(8,128)S(1)} %part_rewards.1.a_ref), channel_id=1, source_target_pairs={{0,1},{1,0},{2,3},{3,2},{4,5},{5,4},{6,7},{7,6},{8,9},{9,8},{10,11... | collective-permute-start | bytes 12296 | tf_op jit(solution)/shard_map/ppermute | solution.py:154

commit v4 on v3

--- a/solution.py
+++ b/solution.py
@@ -17,6 +17,7 @@
 small_cost = pl.CostEstimate(flops=1024, bytes_accessed=1024, transcendentals=0)
 in_vmem = pl.BlockSpec(memory_space=pltpu.VMEM)
 in_hbm = pl.BlockSpec(memory_space=pltpu.HBM)
+in_any = pl.BlockSpec(memory_space=pl.ANY)
 
 
 def dot_nn(a, b, **kw):
@@ -137,6 +138,7 @@
         self.step = self.half - self.wide
         self.repeat = 2 * self.wide - self.half
         self.cols = self.wide * lane
+        self.ext = self.cols + lane
 
     def start(self, y, z1):
         return pl.multiple_of((y * self.half + z1 * self.step) * lane, lane)
@@ -154,77 +156,31 @@
     return lax.ppermute(x, axis, [(i, i ^ bit) for i in range(size)])
 
 
-def prep_kernel(*refs):
-    inputs, (xn_ref, fac_ref), held = refs[:5], refs[5:7], refs[7:12]
-    norm_ref, fac32, low32, sems = refs[12:]
-    copies = [pltpu.make_async_copy(a, b, sems.at[i]) for i, (a, b) in enumerate(zip(inputs, held))]
-    for copy in copies:
-        copy.start()
-    for copy in copies:
-        copy.wait()
-    x_ref, gin_ref, uin_ref, gof_ref, uof_ref = held
-    p = cube()[0]
-    rows, width = x_ref.shape
-    rank, units = gof_ref.shape
-    block = xn_ref.shape[1]
-    x = x_ref[...].astype(f32)
-    normed = scaled_rows(x).astype(bf16)
-    norm_ref[...] = normed
-    xn_ref[...] = norm_ref[:, pl.ds(pl.multiple_of(p * block, lane), block)]
-    fac32[0:rank, :] = gof_ref[...].astype(f32)
-    fac32[rank : 2 * rank, :] = uof_ref[...].astype(f32)
-    fac_ref[:, 0:units] = fac32[...].astype(bf16)
-    scale = noise_scale / math.sqrt(width)
-    low32[...] = jnp.zeros_like(low32)
-    low32[0:rank, 0:rows] = scale * dot_nt(gin_ref[...], normed)
-    low32[rank : 2 * rank, 0:rows] = scale * dot_nt(uin_ref[...], normed)
-    fac_ref[:, units : units + lane] = low32[...].astype(bf16)
-
-
-def prep(ins, block):
-    rows, features = ins[0].shape
-    rank, units = ins[3].shape
-    return pl.pallas_call(
-        prep_kernel,
-        out_shape=(
-            jax.ShapeDtypeStruct((rows, block), bf16),
-            jax.ShapeDtypeStruct((2 * rank, units + lane), bf16),
-        ),
-        in_specs=[in_hbm] * 5,
-        out_specs=(in_vmem,) * 2,
-        scratch_shapes=[pltpu.VMEM(x.shape, x.dtype) for x in ins]
-        + [
-            pltpu.VMEM((rows, features), bf16),
-            pltpu.VMEM((2 * rank, units), f32),
-            pltpu.VMEM((2 * rank, lane), f32),
-            pltpu.SemaphoreType.DMA((5,)),
-        ],
-        compiler_params=pltpu.CompilerParams(vmem_limit_bytes=62 * MiB),
-        cost_estimate=small_cost,
-        name="prep",
-    )(*ins)
-
-
-def base_kernel(tiles, blocks, n, width, xn_ref, wg_ref, wu_ref, *refs):
-    outs = refs[: len(blocks)]
-    wg, wu, sems = refs[len(blocks) :]
+def base_jobs(tiles, blocks, n, width, wg_ref, wu_ref, wg, wu, outs, sems):
     p, y, z1, z2 = cube()
     jobs = []
     for b, (dy, dz1) in enumerate(blocks):
         at = tiles.start(y ^ dy, z1 ^ dz1)
         for c in range(n):
-            for src, dst, slot, s in ((wg_ref, wg, 0, 0), (wu_ref, wu, 1, 1)):
+            for slot, (src, dst) in enumerate(((wg_ref, wg), (wu_ref, wu))):
                 span = pl.ds(c * width, width)
                 copy = pltpu.make_async_copy(
                     src.at[:, pl.ds(pl.multiple_of(at + c * width, lane), width)],
                     dst.at[b, :, span],
-                    sems.at[b, s, c],
+                    sems.at[b, slot, c],
                 )
                 jobs.append((copy, dst.at[b, :, span], outs[b], slot, span))
-    ahead = 2 * n
-    for job in jobs[:ahead]:
+    return jobs
+
+
+def products(tiles, jobs, started, ahead, xn_ref, outs):
+    depth = xn_ref.shape[1] - lane
+    for job in jobs[started:ahead]:
         job[0].start()
-    xn = xn_ref[...]
+    for out in outs:
+        out[0, :, tiles.cols : tiles.ext] = xn_ref[:, depth : depth + lane].astype(out.dtype)
+        out[1, :, tiles.cols : tiles.ext] = jnp.zeros((out.shape[1], lane), out.dtype)
+    xn = xn_ref[:, 0:depth]
     for i, (copy, weights, out, slot, span) in enumerate(jobs):
         copy.wait()
         if i + ahead < len(jobs):
@@ -232,14 +188,79 @@
         out[slot, :, span] = dot_nn(xn, weights[...]).astype(out.dtype)
 
 
-def base_part(xn, wg, wu, tiles, blocks, dtype):
+def first_kernel(tiles, blocks, n, width, *refs):
+    inputs, refs = refs[:3], refs[3:]
+    wg_ref, wu_ref, xn_ref = refs[:3]
+    outs, refs = refs[3 : 3 + len(blocks)], refs[3 + len(blocks) :]
+    held, (norm_ref, wg, wu, in_sems, sems) = refs[:3], refs[3:]
+    copies = [pltpu.make_async_copy(a, b, in_sems.at[i]) for i, (a, b) in enumerate(zip(inputs, held))]
+    for copy in copies:
+        copy.start()
+    jobs = base_jobs(tiles, blocks, n, width, wg_ref, wu_ref, wg, wu, outs, sems)
+    early = 2
+    for job in jobs[:early]:
+        job[0].start()
+    for copy in copies:
+        copy.wait()
+    for job in jobs[early : 2 * n]:
+        job[0].start()
+    p = cube()[0]
+    x_ref, gin_ref, uin_ref = held
+    rows, features = x_ref.shape
+    rank = gin_ref.shape[0]
+    depth = xn_ref.shape[1] - lane
+    normed = scaled_rows(x_ref[...].astype(f32)).astype(bf16)
+    norm_ref[...] = normed
+    xn_ref[:, 0:depth] = norm_ref[:, pl.ds(pl.multiple_of(p * depth, lane), depth)]
+    scale = noise_scale / math.sqrt(features)
+    place = lax.broadcasted_iota(jnp.int32, (rows, lane), 1) - p * (2 * rank)
+    tile = jnp.zeros((rows, lane), f32)
+    for i, ref in enumerate((gin_ref, uin_ref)):
+        low = scale * dot_nt(normed, ref[...])
+        for k in range(rank):
+            tile = jnp.where(place == i * rank + k, jnp.broadcast_to(low[:, k : k + 1], tile.shape), tile)
+    xn_ref[:, depth : depth + lane] = tile.astype(bf16)
+    products(tiles, jobs, 2 * n, 2 * n, xn_ref, outs)
+
+
+def base_kernel(tiles, blocks, n, width, xn_ref, wg_ref, wu_ref, dep_ref, *refs):
+    outs = refs[: len(blocks)]
+    wg, wu, sems = refs[len(blocks) :]
+    jobs = base_jobs(tiles, blocks, n, width, wg_ref, wu_ref, wg, wu, outs, sems)
+    products(tiles, jobs, 0, 2 * n, xn_ref, outs)
+
+
+def first_part(ins, wg, wu, tiles, blocks, dtype):
     n, width = chunks_of(tiles.cols, 512)
-    rows, depth = xn.shape
-    k = len(blocks)
+    rows, features = ins[0].shape
+    depth, k = wg.shape[0], len(blocks)
+    return pl.pallas_call(
+        functools.partial(first_kernel, tiles, blocks, n, width),
+        out_shape=(jax.ShapeDtypeStruct((rows, depth + lane), bf16),)
+        + (jax.ShapeDtypeStruct((2, rows, tiles.ext), dtype),) * k,
+        in_specs=[in_hbm] * 5,
+        out_specs=(in_vmem,) * (1 + k),
+        scratch_shapes=[pltpu.VMEM(x.shape, x.dtype) for x in ins]
+        + [
+            pltpu.VMEM((rows, features), bf16),
+            pltpu.VMEM((k, depth, tiles.cols), bf16),
+            pltpu.VMEM((k, depth, tiles.cols), bf16),
+            pltpu.SemaphoreType.DMA((len(ins),)),
+            pltpu.SemaphoreType.DMA((k, 2, n)),
+        ],
+        compiler_params=pltpu.CompilerParams(vmem_limit_bytes=62 * MiB),
+        cost_estimate=small_cost,
+        name="first",
+    )(*ins, wg, wu)
+
+
+def base_part(xn, wg, wu, dep, tiles, blocks, dtype):
+    n, width = chunks_of(tiles.cols, 512)
+    rows, depth, k = xn.shape[0], wg.shape[0], len(blocks)
     return pl.pallas_call(
         functools.partial(base_kernel, tiles, blocks, n, width),
-        out_shape=(jax.ShapeDtypeStruct((2, rows, tiles.cols), dtype),) * k,
-        in_specs=[in_vmem, in_hbm, in_hbm],
+        out_shape=(jax.ShapeDtypeStruct((2, rows, tiles.ext), dtype),) * k,
+        in_specs=[in_vmem, in_hbm, in_hbm, in_any],
         out_specs=(in_vmem,) * k,
         scratch_shapes=[
             pltpu.VMEM((k, depth, tiles.cols), bf16),
@@ -249,7 +270,7 @@
         compiler_params=pltpu.CompilerParams(vmem_limit_bytes=44 * MiB),
         cost_estimate=small_cost,
         name="base_" + "_".join(f"y{dy}z{dz1}" for dy, dz1 in blocks),
-    )(xn, wg, wu)
+    )(xn, wg, wu, dep)
 
 
 def count_steps(index, size, times):
@@ -259,56 +280,66 @@
     return total
 
 
-def mix_kernel(rows, near_ref, far_ref, mix_ref, low_ref):
+def collect_kernel(near_ref, far_ref, all_ref):
     p = cube()[0]
+    group = near_ref.shape[1]
+    for m in range(8):
+        rel = p ^ m
+        at = (rel & 2) | (rel >> 2)
+        all_ref[m * group : (m + 1) * group, :] = jnp.where((rel & 1) == 0, near_ref[at], far_ref[at])
+
+
+def collect(near, far):
+    _, group, units = near.shape
+    return pl.pallas_call(
+        collect_kernel,
+        out_shape=jax.ShapeDtypeStruct((8 * group, units), bf16),
+        in_specs=[in_vmem] * 2,
+        out_specs=in_vmem,
+        compiler_params=pltpu.CompilerParams(vmem_limit_bytes=8 * MiB),
+        cost_estimate=small_cost,
+        name="collect",
+    )(near, far)
+
+
+def mix_kernel(tiles, group, pair_ref, mix_ref):
     members = 8
-    group = near_ref.shape[1]
     rank = group // 2
-    units = near_ref.shape[2] - lane
-    low_ref[...] = jnp.zeros_like(low_ref)
-    for q in range(members):
-        ref = near_ref if q < 4 else far_ref
-        low_ref[q * group : (q + 1) * group, :] = ref[q % 4, :, units : units + lane].astype(f32)
+    rows = pair_ref.shape[1]
     height, depth = mix_ref.shape
-    r0 = lax.broadcasted_iota(jnp.int32, (height, lane), 0)
-    c0 = lax.broadcasted_iota(jnp.int32, (height, lane), 1)
+    r0 = lax.broadcasted_iota(jnp.int32, (height, rows), 0)
+    c0 = lax.broadcasted_iota(jnp.int32, (height, rows), 1)
     picks = (r0 - rows * count_steps(r0, rows, 2 * members) == c0).astype(f32).astype(bf16)
-    spread = dot_nt(picks, low_ref[...].astype(bf16))
+    spread = dot_nn(picks, pair_ref[0, :, tiles.cols : tiles.ext])[:, 0:depth]
     r = lax.broadcasted_iota(jnp.int32, (height, depth), 0)
     c = lax.broadcasted_iota(jnp.int32, (height, depth), 1)
     step = count_steps(r, rows, 2 * members)
-    in_rows = r - rows * step
     kind = (step >= members).astype(jnp.int32)
-    member = step - members * kind
-    q = c // group if group & (group - 1) else c >> (group.bit_length() - 1)
-    rel = ((q & 1) << 2) | (q & 2) | ((q >> 2) & 1)
-    second = ((c - q * group) >= rank).astype(jnp.int32)
     top = members * group
-    own = (c < top) & ((member ^ p) == rel) & (second == kind)
-    base = (c >= top) & (c - top - rows * kind == in_rows)
+    own = (c < top) & (count_steps(c, rank, 2 * members) == 2 * (step - members * kind) + kind)
+    base = (c >= top) & (c - top - rows * kind == r - rows * step)
     share = jnp.where(kind == 0, 0.5, 1.0)
     mix_ref[...] = (share * (jnp.where(own, spread, 0.0) + jnp.where(base, 1.0, 0.0))).astype(bf16)
 
 
-def mixing(near, far, rows):
-    group = near.shape[1]
-    depth = 8 * group + 2 * rows
-    return pl.pallas_call(
-        functools.partial(mix_kernel, rows),
-        out_shape=jax.ShapeDtypeStruct((16 * rows, depth), bf16),
-        in_specs=[in_vmem] * 2,
+def mixing(pair, tiles, group):
+    rows = pair.shape[1]
+    return pl.pallas_call(
+        functools.partial(mix_kernel, tiles, group),
+        out_shape=jax.ShapeDtypeStruct((16 * rows, 8 * group + 2 * rows), bf16),
+        in_specs=[in_vmem],
         out_specs=in_vmem,
-        scratch_shapes=[pltpu.VMEM((depth, lane), f32)],
         compiler_params=pltpu.CompilerParams(vmem_limit_bytes=8 * MiB),
+        cost_estimate=small_cost,
         name="mixing",
-    )(near, far)
+    )(pair)
 
 
 def hidden_kernel(tiles, blocks, held, loads, first, last, ahead, rows, down_scale, *refs):
     refs = list(refs)
     take = lambda: refs.pop(0)
     p, y, z1, z2 = cube()
-    mix_ref, near_ref, far_ref = take(), take(), take()
+    mix_ref, fac_ref = take(), take()
     pair_refs = [take() for _ in blocks]
     wd = [take() for _ in range(held)]
     wd_ref = take() if loads else None
@@ -331,8 +362,7 @@
         for b, (at, place) in enumerate(places):
             copies.append(pltpu.make_async_copy(wd_ref.at[pl.ds(at, tiles.cols), :], place, sems.at[b]))
         copies[0].start()
-    group = near_ref.shape[1]
-    top = 8 * group
+    top = fac_ref.shape[0]
     mix = mix_ref[...]
     height = mix.shape[0] // 2
     out = wd[0].shape[1]
@@ -341,11 +371,9 @@
     low = None if first else low_in[...]
     n, width = chunks_of(tiles.cols, 640)
     for b, ((dy, dz1), at, pair_ref) in enumerate(zip(blocks, starts, pair_refs)):
-        for q in range(8):
-            ref = near_ref if q < 4 else far_ref
-            right_ref[q * group : (q + 1) * group, :] = ref[q % 4, :, pl.ds(at, tiles.cols)]
-        right_ref[top : top + rows, :] = pair_ref[0]
-        right_ref[top + rows : top + 2 * rows, :] = pair_ref[1]
+        right_ref[0:top, :] = fac_ref[:, pl.ds(at, tiles.cols)]
+        right_ref[top : top + rows, :] = pair_ref[0, :, 0 : tiles.cols]
+        right_ref[top + rows : top + 2 * rows, :] = pair_ref[1, :, 0 : tiles.cols]
         for c in range(n):
             span = pl.ds(c * width, width)
             both = dot_nn(mix, right_ref[:, span])
@@ -390,15 +418,15 @@
         copy.wait()
 
 
-def hidden_step(mix, near, far, pairs, wds, dif, tiles, blocks, rows, scale, state=None, dout=None, ahead=None):
+def hidden_step(mix, fac, pairs, wds, dif, tiles, blocks, rows, scale, state=None, dout=None, ahead=None):
     height = mix.shape[0] // 2
     out = wds[0].shape[1]
     terms = dif.shape[0]
     first, last, k = state is None, dout is not None, len(blocks)
     loads = wds[-1].shape[0] != tiles.cols
     held = len(wds) - loads
-    args = [mix, near, far, *pairs, *wds, dif]
-    specs = [in_vmem] * (3 + k + held) + [in_hbm] * loads + [in_vmem]
+    args = [mix, fac, *pairs, *wds, dif]
+    specs = [in_vmem] * (2 + k + held) + [in_hbm] * loads + [in_vmem]
     if not first:
         args += list(state)
     if last:
@@ -424,7 +452,7 @@
         in_specs=specs,
         out_specs=(in_vmem,) * len(shapes),
         scratch_shapes=scratch,
-        compiler_params=pltpu.CompilerParams(vmem_limit_bytes=(41 if loads else 16) * MiB),
+        compiler_params=pltpu.CompilerParams(vmem_limit_bytes=(36 if loads else 16) * MiB),
         cost_estimate=small_cost,
         name="hidden_" + "_".join(f"y{dy}z{dz1}" for dy, dz1 in blocks),
     )(*args)
@@ -560,40 +588,37 @@
     dif = turned(down_input_factors).reshape(members * rank, units)
     dout = turned(down_out).reshape(members * rank, block)
 
-    ins = (
-        prompts,
-        turned(gate_in)[0],
-        turned(up_in)[0],
-        turned(gate_output_factors)[0],
-        turned(up_output_factors)[0],
-    )
+    ins = (prompts, turned(gate_in)[0], turned(up_in)[0])
+    fac = jnp.concatenate([turned(gate_output_factors)[0], turned(up_output_factors)[0]])
     after = lambda x, *done: lax.optimization_barrier((x, *done))[0]
-    part = lambda x, blocks, dtype: base_part(x, gate_weight, up_weight, tiles, blocks, dtype)
-
-    head_rows = lax.dynamic_slice_in_dim(label_head, (p * block) % label_head.shape[0], block, 0)
-    head = jnp.where((p * block) // label_head.shape[0] == t, head_rows, over_t(head_rows))
-
-    xn, fac = prep(ins, block)
-    fac_z2 = over_z2(fac)
-    far0, far1 = part(xn, ((1, 1), (1, 0)), bf16)
-    xn, dif, dout = lax.optimization_barrier((xn, dif, dout, far1, fac_z2))[:3]
-    far0, far1 = over_y(far0), over_y(far1)
-    two = jnp.stack([fac, fac_z2])
+    weights = gate_weight, up_weight
+
+    two = jnp.stack([fac, over_z2(fac)])
+    xn, far0, far1 = first_part(ins, *weights, tiles, ((1, 1), (1, 0)), bf16)
+    far0 = over_y(far0)
     two_z1 = over_z1(two)
-    (near0,) = part(xn, ((0, 1),), f32)
+    dif, dout, two = lax.optimization_barrier((dif, dout, two))
+    (near0,) = base_part(xn, *weights, two, tiles, ((0, 1),), f32)
     from_z1 = over_z1((near0 + far0.astype(f32)).astype(bf16))
-    (near1,) = part(after(xn, near0, two_z1, head), ((0, 0),), f32)
+    (near1,) = base_part(xn, *weights, two_z1, tiles, ((0, 0),), f32)
     four = jnp.concatenate([two, two_z1])
     far_four = over_y(four)
 
+    far1 = over_y(after(far1, near0))
     mine = near1 + far1.astype(f32) + from_z1.astype(f32)
-    pair = (mine + over_z2(mine.astype(bf16)).astype(f32)).astype(bf16)
-
-    mix = mixing(four, far_four, rows)
-    step = functools.partial(hidden_step, mix, four, far_four)
+    send = mine.astype(bf16)
+    from_z2 = over_z2(send)
+    heads = after(label_head, send)
+    head_rows = lax.dynamic_slice_in_dim(heads, (p * block) % heads.shape[0], block, 0)
+    head = jnp.where((p * block) // heads.shape[0] == t, head_rows, over_t(head_rows))
+    far_four = after(far_four, head)
+    pair = (mine + from_z2.astype(f32)).astype(bf16)
+
+    mix = mixing(pair, tiles, 2 * rank)
+    step = functools.partial(hidden_step, mix, collect(four, far_four))
     tail, wd = (dif, tiles), down_weight_matrix
     pair_z = over_z1(pair)
-    pair_y = over_y(pair)
+    pair_y = over_y(after(pair, mix))
     *state, wd1 = step((pair,), (wd,), *tail, ((0, 0),), rows, down_scale, ahead=(0, 1))
     pair_yz = over_y(after(pair_z, state[0]))
     *state, wd3 = step((pair_z, pair_y), (wd1, wd), *tail, ((0, 1), (1, 0)), rows, down_scale, state, ahead=(1, 1))

time: 79.3 us -> 77.7 us (0.980)
  waiting for transfers between devices: 19.6 us -> 22.8 us
  starting transfers between devices: 20 us -> 17 us
  Pallas kernels: 35 us -> 34.1 us
  local copies, waits for them, and re-layouts: 2 us -> 1.11 us
    pallas_call x3 -> x2, Pallas kernels: 14.2 us -> 7.71 us  [base_part(): pl.pallas_call(functools.partial(base_kernel, tiles, blocks, n, width), o...]
    pallas_call x2 -> x3, Pallas kernels: 2.5 us -> 8.13 us  [the longest x1 7.86 us: first_part(): pl.pallas_call(functools.partial(first_kernel, tiles, blocks, n, width),...]
    ppermute x16, waiting for transfers between devices: 19.6 us -> 22.8 us  [swap(): return lax.ppermute(x, axis, [(i, i ^ bit) for i in range(size)])]
    ppermute x16, starting transfers between devices: 20 us -> 17 us  [swap(): return lax.ppermute(x, axis, [(i, i ^ bit) for i in range(size)])]
    select_n x1, other arithmetic: 1.02 us -> 0.07 us  [cube_body(): jnp.where(p * block // heads.shape[0] == t, head_rows, over_t(head_rows))]
    dynamic_slice x1, local copies, waits for them, and re-layouts: 0.97 us -> 0.02 us  [cube_body(): lax.dynamic_slice_in_dim(heads, p * block % heads.shape[0], block, 0)]
    another operation x1 -> x2, other arithmetic: 0.03 us -> 0.94 us  [cube_body(): two = jnp.stack([fac, over_z2(fac)])]
  transfers between devices with their start and end apart: 16 -> 16, of which waited for: 6 -> 9; matrix products, arithmetic and copies ran while one was open for 3% -> 1% of each run, Pallas kernels for 29% -> 32%
where the time goes in v4:
time: 77.7 us; the launch traced here: 77.4 us
  Pallas kernels  34.1 us (44%)
  waiting for transfers between devices  22.8 us (29%)
  starting transfers between devices  17 us (22%)
  other arithmetic  1.24 us (2%)
  local copies, waits for them, and re-layouts  1.11 us (1%)
  between operations  1.05 us (1%)
    ppermute x16, waiting for transfers between devices, swap(): return lax.ppermute(x, axis, [(i, i ^ bit) for i in range(size)])  22.8 us
    ppermute x16, starting transfers between devices, swap(): return lax.ppermute(x, axis, [(i, i ^ bit) for i in range(size)])  17 us
    pallas_call x3, Pallas kernels, hidden_step(): pl.pallas_call(functools.partial(hidden_kernel, tiles, blocks, held, load...  11.4 us
    pallas_call x1, Pallas kernels, first_part(): pl.pallas_call(functools.partial(first_kernel, tiles, blocks, n, width),...  7.86 us
    pallas_call x2, Pallas kernels, base_part(): pl.pallas_call(functools.partial(base_kernel, tiles, blocks, n, width), o...  7.71 us
    pallas_call x1, Pallas kernels, updates(): pl.pallas_call(functools.partial(update_kernel, n, high), out_shape=(jax....  6.46 us
  transfers between devices with their start and end apart: 16, of which 9 were waited for; matrix products, arithmetic and copies ran while one was open for 1% of the time, Pallas kernels for 32%

profile of v4, /device:TPU:0, one launch (start us, length us, event | category | flops | bytes accessed | tf_op | source)
XLA Modules:
  0.0 77.4 jit_solution(10082341044529663787)
XLA Ops:
  0.6 0.9 %fusion.1 = (bf16[1,8,7424]{2,1,0:T(8,128)(2,1)S(1)}, bf16[8,7424]{1,0:T(8,128)(2,1)S(1)}) fusion(bf16[4,7424]{1,0:T(4,128)(2,1)} %bitcast.25, bf16[4,7424]{1,0:T(4,128)(2,1)} %bitcast.26), kind=kLoop, calls=%fused_computation.10 | loop fusion | flops 237568 | bytes 356352 | tf_op jit(solution)/shard_map/stack | solution.py:596
  1.5 4.1 %collective-permute-start = (bf16[8,7424]{1,0:T(8,128)(2,1)S(1)}, bf16[8,7424]{1,0:T(8,128)(2,1)S(1)}, u32[]{:S(2)}, u32[]{:S(2)}) collective-permute-start(bf16[8,7424]{1,0:T(8,128)(2,1)S(1)} %get-tuple-element.45), channel_id=1, source_target_pairs={{0,8},{2,10},{4,12},{6,14},{8,0},{10,2},{12,4},{14,6},{1,9},{3,11}... | collective-permute-start | bytes 356360 | tf_op jit(solution)/shard_map/ppermute | solution.py:156
  5.7 7.9 %first.1 = (bf16[24,1152]{1,0:T(8,128)(2,1)}, bf16[2,24,2048]{2,1,0:T(8,128)(2,1)}, bf16[2,24,2048]{2,1,0:T(8,128)(2,1)}) custom-call(bf16[24,8192]{1,0:T(8,128)(2,1)} %x_ref.1, bf16[4,8192]{1,0:T(4,128)(2,1)} %bitcast.22, bf16[4,8192]{1,0:T(4,128)(2,1)} %bitcast.23, bf16[1024,7424]{1,0:T(8,128)(2,1)} %wg_ref.3, bf16[1024,7424]{1,0:T(8,128)(2,1)} %wu_ref.3), custom_call_target="tpu_custom_call" | custom-call | flops 1024 | bytes 1024 | tf_op jit(solution)/shard_map/first/pallas_call | solution.py:237
  13.5 1.6 %collective-permute-start.3 = (bf16[2,24,2048]{2,1,0:T(8,128)(2,1)}, bf16[2,24,2048]{2,1,0:T(8,128)(2,1)S(1)}, u32[]{:S(2)}, u32[]{:S(2)}) collective-permute-start(bf16[2,24,2048]{2,1,0:T(8,128)(2,1)} %get-tuple-element.27), channel_id=1, source_target_pairs={{0,2},{2,0},{4,6},{6,4},{8,10},{10,8},{12,14},{14,12},{1,3},{3,1},... | collective-permute-start | bytes 589832 | tf_op jit(solution)/shard_map/ppermute | solution.py:156
  15.1 0.1 reshape.13.refs_4_.refs_6_.dif_ref
  15.3 0.0 collective-permute-done
  15.3 1.6 %collective-permute-start.1 = (bf16[2,8,7424]{2,1,0:T(8,128)(2,1)S(1)}, bf16[2,8,7424]{2,1,0:T(8,128)(2,1)S(1)}, u32[]{:S(2)}, u32[]{:S(2)}) collective-permute-start(bf16[2,8,7424]{2,1,0:T(8,128)(2,1)S(1)} %pad_maximum_fusion.dep_ref), channel_id=1, source_target_pairs={{0,4},{2,6},{4,0},{6,2},{8,12},{10,14},{12,8},{14,10},{1,5},{3,7},... | collective-permute-start | bytes 712712 | tf_op jit(solution)/shard_map/ppermute | solution.py:156
  17.0 0.8 %copy-done.1 = bf16[24,1152]{1,0:T(8,128)(2,1)S(1)} copy-done((bf16[24,1152]{1,0:T(8,128)(2,1)S(1)}, bf16[24,1152]{1,0:T(8,128)(2,1)}, u32[]{:S(2)}) %copy-start.1) | copy-done | bytes 55320
  17.8 3.8 %base_y0z1.1 = f32[2,24,2048]{2,1,0:T(8,128)S(1)} custom-call(bf16[24,1152]{1,0:T(8,128)(2,1)S(1)} %copy-done.1, bf16[1024,7424]{1,0:T(8,128)(2,1)} %wg_ref.3, bf16[1024,7424]{1,0:T(8,128)(2,1)} %wu_ref.3, bf16[2,8,7424]{2,1,0:T(8,128)(2,1)S(1)} %pad_maximum_fusion.dep_ref), custom_call_target="tpu_custom_call" | custom-call | flops 1024 | bytes 1024 | tf_op jit(solution)/shard_map/base_y0z1/pallas_call | solution.py:260
  21.6 0.6 collective-permute-start.2
  22.2 0.1 add_convert_fusion.1
  22.2 0.5 collective-permute-start.4
  22.8 0.0 copy-start.3
  22.8 3.9 %base_y0z0.1 = f32[2,24,2048]{2,1,0:T(8,128)S(1)} custom-call(bf16[24,1152]{1,0:T(8,128)(2,1)S(1)} %copy-done.1, bf16[1024,7424]{1,0:T(8,128)(2,1)} %wg_ref.3, bf16[1024,7424]{1,0:T(8,128)(2,1)} %wu_ref.3, bf16[2,8,7424]{2,1,0:T(8,128)(2,1)S(1)} %collective-permute-done.1.dep_ref), custom_call_target="tpu_custom_call" | custom-call | flops 1024 | bytes 1024 | tf_op jit(solution)/shard_map/base_y0z0/pallas_call | solution.py:260
  26.7 0.8 %collective-permute-done.2 = bf16[2,24,2048]{2,1,0:T(8,128)(2,1)S(1)} collective-permute-done((bf16[2,24,2048]{2,1,0:T(8,128)(2,1)S(1)}, bf16[2,24,2048]{2,1,0:T(8,128)(2,1)S(1)}, u32[]{:S(2)}, u32[]{:S(2)}) %collective-permute-start.2) | collective-permute-done | bytes 196640 | tf_op jit(solution)/shard_map/ppermute | solution.py:156
  27.5 0.5 collective-permute-done.4
  28.0 0.1 fusion
  28.1 0.4 collective-permute-start.5
  28.5 1.6 %collective-permute-start.6 = (bf16[4,8,7424]{2,1,0:T(8,128)(2,1)S(1)}, bf16[4,8,7424]{2,1,0:T(8,128)(2,1)S(1)}, u32[]{:S(2)}, u32[]{:S(2)}) collective-permute-start(bf16[4,8,7424]{2,1,0:T(8,128)(2,1)S(1)} %constant_dynamic-update-slice_fusion.near_ref), channel_id=1, source_target_pairs={{0,2},{2,0},{4,6},{6,4},{8,10},{10,8},{12,14},{14,12},{1,3},{3,1},... | collective-permute-start | bytes 1425416 | tf_op jit(solution)/shard_map/ppermute | solution.py:156
  30.1 0.1 collective-permute-start.7
  30.2 7.7 %collective-permute-done.5 = bf16[2,24,2048]{2,1,0:T(8,128)(2,1)S(1)} collective-permute-done((bf16[2,24,2048]{2,1,0:T(8,128)(2,1)S(1)}, bf16[2,24,2048]{2,1,0:T(8,128)(2,1)S(1)}, u32[]{:S(2)}, u32[]{:S(2)}) %collective-permute-start.5) | collective-permute-done | bytes 196640 | tf_op jit(solution)/shard_map/ppermute | solution.py:156
  37.9 0.1 add_convert_fusion.pair_ref.refs_2_
  38.0 0.2 mixing.1.refs_0_
  38.2 0.1 collective-permute-start.8
  38.2 1.6 %collective-permute-start.10 = (bf16[2,24,2048]{2,1,0:T(8,128)(2,1)S(1)}, bf16[2,24,2048]{2,1,0:T(8,128)(2,1)S(1)}, u32[]{:S(2)}, u32[]{:S(2)}) collective-permute-start(bf16[2,24,2048]{2,1,0:T(8,128)(2,1)S(1)} %add_convert_fusion.pair_ref.refs_2_), channel_id=1, source_target_pairs={{0,2},{2,0},{4,6},{6,4},{8,10},{10,8},{12,14},{14,12},{1,3},{3,1},... | collective-permute-start | bytes 589832 | tf_op jit(solution)/shard_map/ppermute | solution.py:156
  39.8 0.1 broadcast_select_fusion.head_ref
  39.9 0.1 collect.1.refs_1_
  40.0 3.8 %hidden_y0z0.1 = (f32[192,1024]{1,0:T(8,128)S(1)}, f32[192,32]{1,0:T(8,128)S(1)}, bf16[1920,1024]{1,0:T(8,128)(2,1)S(1)}) custom-call(bf16[384,112]{1,0:T(8,128)(2,1)S(1)} %mixing.1.refs_0_, bf16[64,7424]{1,0:T(8,128)(2,1)S(1)} %collect.1.refs_1_, bf16[2,24,2048]{2,1,0:T(8,128)(2,1)S(1)} %add_convert_fusion.pair_ref.refs_2_, bf16[7424,1024]{1,0:T(8,128)(2,1)} %refs_5_.1, ...), custom_call_target="tpu_custom_call" | custom-call | flops 1024 | bytes 1024 | tf_op jit(solution)/shard_map/hidden_y0z0/pallas_call | solution.py:449
  43.9 0.0 copy-start
  43.9 0.0 copy-start.5
  43.9 0.2 collective-permute-done.8.refs_2_
  44.1 1.5 %collective-permute-start.9 = (bf16[2,24,2048]{2,1,0:T(8,128)(2,1)S(1)}, bf16[2,24,2048]{2,1,0:T(8,128)(2,1)S(1)}, u32[]{:S(2)}, u32[]{:S(2)}) collective-permute-start(bf16[2,24,2048]{2,1,0:T(8,128)(2,1)S(1)} %collective-permute-done.8.refs_2_), channel_id=1, source_target_pairs={{0,2},{2,0},{4,6},{6,4},{8,10},{10,8},{12,14},{14,12},{1,3},{3,1},... | collective-permute-start | bytes 589832 | tf_op jit(solution)/shard_map/ppermute | solution.py:156
  45.6 5.1 %hidden_y0z1_y1z0.1 = (f32[192,1024]{1,0:T(8,128)S(1)}, f32[192,32]{1,0:T(8,128)S(1)}, bf16[1920,1024]{1,0:T(8,128)(2,1)S(1)}) custom-call(bf16[384,112]{1,0:T(8,128)(2,1)S(1)} %mixing.1.refs_0_, bf16[64,7424]{1,0:T(8,128)(2,1)S(1)} %collect.1.refs_1_, bf16[2,24,2048]{2,1,0:T(8,128)(2,1)S(1)} %collective-permute-done.8.refs_2_, ...), custom_call_target="tpu_custom_call" | custom-call | flops 1024 | bytes 1024 | tf_op jit(solution)/shard_map/hidden_y0z1_y1z0/pallas_call | solution.py:449
  50.7 2.5 %hidden_y1z1.1 = (f32[96,1024]{1,0:T(8,128)S(1)}, f32[96,1024]{1,0:T(8,128)S(1)}) custom-call(bf16[384,112]{1,0:T(8,128)(2,1)S(1)} %mixing.1.refs_0_, bf16[64,7424]{1,0:T(8,128)(2,1)S(1)} %collect.1.refs_1_, bf16[2,24,2048]{2,1,0:T(8,128)(2,1)S(1)} %collective-permute-done.9.refs_2_, bf16[1920,1024]{1,0:T(8,128)(2,1)S(1)} %get-tuple-element.36.refs_3_, ...), custom_call_target="tpu_custom_call" | custom-call | flops 1024 | bytes 1024 | tf_op jit(solution)/shard_map/hidden_y1z1/pallas_call | solution.py:449
  53.2 0.1 collective-permute-start.11
  53.3 1.7 %collective-permute-done.11.recv_ref = f32[96,1024]{1,0:T(8,128)S(1)} collective-permute-done((f32[96,1024]{1,0:T(8,128)S(1)}, f32[96,1024]{1,0:T(8,128)S(1)}, u32[]{:S(2)}, u32[]{:S(2)}) %collective-permute-start.11) | collective-permute-done | bytes 393248 | tf_op jit(solution)/shard_map/ppermute | solution.py:156
  55.0 0.3 part_logits.1
  55.3 0.6 collective-permute-start.12
  55.9 3.6 %collective-permute-done.12 = f32[104,128]{1,0:T(8,128)S(1)} collective-permute-done((f32[104,128]{1,0:T(8,128)S(1)}, f32[104,128]{1,0:T(8,128)S(1)}, u32[]{:S(2)}, u32[]{:S(2)}) %collective-permute-start.12) | collective-permute-done | bytes 53280 | tf_op jit(solution)/shard_map/ppermute | solution.py:156
  59.5 0.9 %collective-permute-start.13 = (f32[104,128]{1,0:T(8,128)S(1)}, f32[104,128]{1,0:T(8,128)S(1)}, u32[]{:S(2)}, u32[]{:S(2)}) collective-permute-start(f32[104,128]{1,0:T(8,128)S(1)} %add.32), channel_id=1, source_target_pairs={{0,4},{2,6},{4,0},{6,2},{8,12},{10,14},{12,8},{14,10},{1,5},{3,7},... | collective-permute-start | bytes 159752 | tf_op jit(solution)/shard_map/ppermute | solution.py:156
  60.4 3.3 %collective-permute-done.13 = f32[104,128]{1,0:T(8,128)S(1)} collective-permute-done((f32[104,128]{1,0:T(8,128)S(1)}, f32[104,128]{1,0:T(8,128)S(1)}, u32[]{:S(2)}, u32[]{:S(2)}) %collective-permute-start.13) | collective-permute-done | bytes 53280 | tf_op jit(solution)/shard_map/ppermute | solution.py:156
  63.7 1.8 %collective-permute-start.14 = (f32[104,128]{1,0:T(8,128)S(1)}, f32[104,128]{1,0:T(8,128)S(1)}, u32[]{:S(2)}, u32[]{:S(2)}) collective-permute-start(f32[104,128]{1,0:T(8,128)S(1)} %add.33.a_ref), channel_id=1, source_target_pairs={{0,8},{2,10},{4,12},{6,14},{8,0},{10,2},{12,4},{14,6},{1,9},{3,11}... | collective-permute-start | bytes 159752 | tf_op jit(solution)/shard_map/ppermute | solution.py:156
  65.5 0.1 copy.14.targets_ref
  65.5 3.8 %collective-permute-done.14.b_ref = f32[104,128]{1,0:T(8,128)S(1)} collective-permute-done((f32[104,128]{1,0:T(8,128)S(1)}, f32[104,128]{1,0:T(8,128)S(1)}, u32[]{:S(2)}, u32[]{:S(2)}) %collective-permute-start.14) | collective-permute-done | bytes 53280 | tf_op jit(solution)/shard_map/ppermute | solution.py:156
  69.4 0.2 part_rewards.1.a_ref
  69.6 0.1 collective-permute-start.15
  69.7 1.2 %collective-permute-done.15.b_ref = f32[8,128]{1,0:T(8,128)S(1)} collective-permute-done((f32[8,128]{1,0:T(8,128)S(1)}, f32[8,128]{1,0:T(8,128)S(1)}, u32[]{:S(2)}, u32[]{:S(2)}) %collective-permute-start.15) | collective-permute-done | bytes 4128 | tf_op jit(solution)/shard_map/ppermute | solution.py:156
  70.8 6.5 %updates.1 = (bf16[7424,1024]{1,0:T(8,128)(2,1)}, f32[1,128]{1,0:T(1,128)}) custom-call(f32[8,128]{1,0:T(8,128)S(1)} %part_rewards.1.a_ref, f32[8,128]{1,0:T(8,128)S(1)} %collective-permute-done.15.b_ref, bf16[32,7424]{1,0:T(8,128)(2,1)S(1)} %reshape.13.refs_4_.refs_6_.dif_ref, bf16[32,1024]{1,0:T(8,128)(2,1)S(1)} %reshape.14.refs_7_.dout_ref), custom_call_target="tpu_custom_call" | custom-call | tf_op jit(solution)/shard_map/updates/pallas_call | solution.py:551
  (23 shorter events, 0.1 us)
Async XLA Ops:
  1.5 13.7 %collective-permute-start = (bf16[8,7424]{1,0:T(8,128)(2,1)S(1)}, bf16[8,7424]{1,0:T(8,128)(2,1)S(1)}, u32[]{:S(2)}, u32[]{:S(2)}) collective-permute-start(bf16[8,7424]{1,0:T(8,128)(2,1)S(1)} %get-tuple-element.45), channel_id=1, source_target_pairs={{0,8},{2,10},{4,12},{6,14},{8,0},{10,2},{12,4},{14,6},{1,9},{3,11}... | collective-permute-start | bytes 356360 | tf_op jit(solution)/shard_map/ppermute | solution.py:156
  5.7 9.5 %copy-start.4 = (bf16[8,1024,4]{1,2,0:T(4,128)(2,1)S(1)}, bf16[8,1024,4]{1,2,0:T(4,128)(2,1)}, u32[]{:S(2)}) copy-start(bf16[8,1024,4]{1,2,0:T(4,128)(2,1)} %param.21) | copy-start | bytes 196612
  5.7 9.5 %copy-start.2 = (bf16[8,7424,4]{1,2,0:T(4,128)(2,1)S(1)}, bf16[8,7424,4]{1,2,0:T(4,128)(2,1)}, u32[]{:S(2)}) copy-start(bf16[8,7424,4]{1,2,0:T(4,128)(2,1)} %param.20) | copy-start | bytes 1425412
  13.5 8.7 %collective-permute-start.3 = (bf16[2,24,2048]{2,1,0:T(8,128)(2,1)}, bf16[2,24,2048]{2,1,0:T(8,128)(2,1)S(1)}, u32[]{:S(2)}, u32[]{:S(2)}) collective-permute-start(bf16[2,24,2048]{2,1,0:T(8,128)(2,1)} %get-tuple-element.27), channel_id=1, source_target_pairs={{0,2},{2,0},{4,6},{6,4},{8,10},{10,8},{12,14},{14,12},{1,3},{3,1},... | collective-permute-start | bytes 589832 | tf_op jit(solution)/shard_map/ppermute | solution.py:156
  15.3 7.5 %collective-permute-start.1 = (bf16[2,8,7424]{2,1,0:T(8,128)(2,1)S(1)}, bf16[2,8,7424]{2,1,0:T(8,128)(2,1)S(1)}, u32[]{:S(2)}, u32[]{:S(2)}) collective-permute-start(bf16[2,8,7424]{2,1,0:T(8,128)(2,1)S(1)} %pad_maximum_fusion.dep_ref), channel_id=1, source_target_pairs={{0,4},{2,6},{4,0},{6,2},{8,12},{10,14},{12,8},{14,10},{1,5},{3,7},... | collective-permute-start | bytes 712712 | tf_op jit(solution)/shard_map/ppermute | solution.py:156
  17.0 0.8 %copy-start.1 = (bf16[24,1152]{1,0:T(8,128)(2,1)S(1)}, bf16[24,1152]{1,0:T(8,128)(2,1)}, u32[]{:S(2)}) copy-start(bf16[24,1152]{1,0:T(8,128)(2,1)} %get-tuple-element.23.xn_ref) | copy-start | bytes 165892
  17.8 3.8 %copy-start.6 = (bf16[2,24,2048]{2,1,0:T(8,128)(2,1)S(1)}, bf16[2,24,2048]{2,1,0:T(8,128)(2,1)}, u32[]{:S(2)}) copy-start(bf16[2,24,2048]{2,1,0:T(8,128)(2,1)} %get-tuple-element.26) | copy-start | bytes 589828
  21.6 5.9 %collective-permute-start.2 = (bf16[2,24,2048]{2,1,0:T(8,128)(2,1)S(1)}, bf16[2,24,2048]{2,1,0:T(8,128)(2,1)S(1)}, u32[]{:S(2)}, u32[]{:S(2)}) collective-permute-start(bf16[2,24,2048]{2,1,0:T(8,128)(2,1)S(1)} %copy-done.6), channel_id=1, source_target_pairs={{0,2},{2,0},{4,6},{6,4},{8,10},{10,8},{12,14},{14,12},{1,3},{3,1},... | collective-permute-start | bytes 589832 | tf_op jit(solution)/shard_map/ppermute | solution.py:156
  22.2 5.7 %collective-permute-start.4 = (bf16[2,24,2048]{2,1,0:T(8,128)(2,1)S(1)}, bf16[2,24,2048]{2,1,0:T(8,128)(2,1)S(1)}, u32[]{:S(2)}, u32[]{:S(2)}) collective-permute-start(bf16[2,24,2048]{2,1,0:T(8,128)(2,1)S(1)} %add_convert_fusion.1), channel_id=1, source_target_pairs={{0,4},{2,6},{4,0},{6,2},{8,12},{10,14},{12,8},{14,10},{1,5},{3,7},... | collective-permute-start | bytes 589832 | tf_op jit(solution)/shard_map/ppermute | solution.py:156
  22.8 7.3 %copy-start.3 = (bf16[4096,128]{1,0:T(8,128)(2,1)S(1)}, bf16[4096,128]{1,0:T(8,128)(2,1)}, u32[]{:S(2)}) copy-start(bf16[4096,128]{1,0:T(8,128)(2,1)} %param.22) | copy-start | bytes 3145732
  28.1 9.8 %collective-permute-start.5 = (bf16[2,24,2048]{2,1,0:T(8,128)(2,1)S(1)}, bf16[2,24,2048]{2,1,0:T(8,128)(2,1)S(1)}, u32[]{:S(2)}, u32[]{:S(2)}) collective-permute-start(bf16[2,24,2048]{2,1,0:T(8,128)(2,1)S(1)} %fusion), channel_id=1, source_target_pairs={{0,8},{2,10},{4,12},{6,14},{8,0},{10,2},{12,4},{14,6},{1,9},{3,11}... | collective-permute-start | bytes 589832 | tf_op jit(solution)/shard_map/ppermute | solution.py:156
  28.5 11.4 %collective-permute-start.6 = (bf16[4,8,7424]{2,1,0:T(8,128)(2,1)S(1)}, bf16[4,8,7424]{2,1,0:T(8,128)(2,1)S(1)}, u32[]{:S(2)}, u32[]{:S(2)}) collective-permute-start(bf16[4,8,7424]{2,1,0:T(8,128)(2,1)S(1)} %constant_dynamic-update-slice_fusion.near_ref), channel_id=1, source_target_pairs={{0,2},{2,0},{4,6},{6,4},{8,10},{10,8},{12,14},{14,12},{1,3},{3,1},... | collective-permute-start | bytes 1425416 | tf_op jit(solution)/shard_map/ppermute | solution.py:156
  30.1 9.8 %collective-permute-start.7 = (bf16[1024,128]{1,0:T(8,128)(2,1)S(1)}, bf16[1024,128]{1,0:T(8,128)(2,1)S(1)}, u32[]{:S(2)}, u32[]{:S(2)}) collective-permute-start(bf16[1024,128]{1,0:T(8,128)(2,1)S(1)} %constant_dynamic-slice_fusion), channel_id=1, source_target_pairs={{0,1},{1,0},{2,3},{3,2},{4,5},{5,4},{6,7},{7,6},{8,9},{9,8},{10,11... | collective-permute-start | bytes 786440 | tf_op jit(solution)/shard_map/ppermute | solution.py:156
  38.2 5.9 %collective-permute-start.8 = (bf16[2,24,2048]{2,1,0:T(8,128)(2,1)S(1)}, bf16[2,24,2048]{2,1,0:T(8,128)(2,1)S(1)}, u32[]{:S(2)}, u32[]{:S(2)}) collective-permute-start(bf16[2,24,2048]{2,1,0:T(8,128)(2,1)S(1)} %add_convert_fusion.pair_ref.refs_2_), channel_id=1, source_target_pairs={{0,4},{2,6},{4,0},{6,2},{8,12},{10,14},{12,8},{14,10},{1,5},{3,7},... | collective-permute-start | bytes 589832 | tf_op jit(solution)/shard_map/ppermute | solution.py:156
  38.2 7.4 %collective-permute-start.10 = (bf16[2,24,2048]{2,1,0:T(8,128)(2,1)S(1)}, bf16[2,24,2048]{2,1,0:T(8,128)(2,1)S(1)}, u32[]{:S(2)}, u32[]{:S(2)}) collective-permute-start(bf16[2,24,2048]{2,1,0:T(8,128)(2,1)S(1)} %add_convert_fusion.pair_ref.refs_2_), channel_id=1, source_target_pairs={{0,2},{2,0},{4,6},{6,4},{8,10},{10,8},{12,14},{14,12},{1,3},{3,1},... | collective-permute-start | bytes 589832 | tf_op jit(solution)/shard_map/ppermute | solution.py:156
  43.9 11.1 %copy-start = (bf16[24,8192]{1,0:T(8,128)(2,1)S(1)}, bf16[24,8192]{1,0:T(8,128)(2,1)}, u32[]{:S(2)}) copy-start(bf16[24,8192]{1,0:T(8,128)(2,1)} %x_ref.1) | copy-start | bytes 1179652
  43.9 21.6 %copy-start.5 = (s32[24]{0:T(128)S(1)}, s32[24]{0:T(128)}, u32[]{:S(2)}) copy-start(s32[24]{0:T(128)} %param.23) | copy-start | bytes 292
  44.1 6.6 %collective-permute-start.9 = (bf16[2,24,2048]{2,1,0:T(8,128)(2,1)S(1)}, bf16[2,24,2048]{2,1,0:T(8,128)(2,1)S(1)}, u32[]{:S(2)}, u32[]{:S(2)}) collective-permute-start(bf16[2,24,2048]{2,1,0:T(8,128)(2,1)S(1)} %collective-permute-done.8.refs_2_), channel_id=1, source_target_pairs={{0,2},{2,0},{4,6},{6,4},{8,10},{10,8},{12,14},{14,12},{1,3},{3,1},... | collective-permute-start | bytes 589832 | tf_op jit(solution)/shard_map/ppermute | solution.py:156
  53.2 1.8 %collective-permute-start.11 = (f32[96,1024]{1,0:T(8,128)S(1)}, f32[96,1024]{1,0:T(8,128)S(1)}, u32[]{:S(2)}, u32[]{:S(2)}) collective-permute-start(f32[96,1024]{1,0:T(8,128)S(1)} %get-tuple-element.41), channel_id=1, source_target_pairs={{0,1},{1,0},{2,3},{3,2},{4,5},{5,4},{6,7},{7,6},{8,9},{9,8},{10,11... | collective-permute-start | bytes 1179656 | tf_op jit(solution)/shard_map/ppermute | solution.py:156
  55.3 4.2 %collective-permute-start.12 = (f32[104,128]{1,0:T(8,128)S(1)}, f32[104,128]{1,0:T(8,128)S(1)}, u32[]{:S(2)}, u32[]{:S(2)}) collective-permute-start(f32[104,128]{1,0:T(8,128)S(1)} %part_logits.1), channel_id=1, source_target_pairs={{0,2},{2,0},{4,6},{6,4},{8,10},{10,8},{12,14},{14,12},{1,3},{3,1},... | collective-permute-start | bytes 159752 | tf_op jit(solution)/shard_map/ppermute | solution.py:156
  59.5 4.2 %collective-permute-start.13 = (f32[104,128]{1,0:T(8,128)S(1)}, f32[104,128]{1,0:T(8,128)S(1)}, u32[]{:S(2)}, u32[]{:S(2)}) collective-permute-start(f32[104,128]{1,0:T(8,128)S(1)} %add.32), channel_id=1, source_target_pairs={{0,4},{2,6},{4,0},{6,2},{8,12},{10,14},{12,8},{14,10},{1,5},{3,7},... | collective-permute-start | bytes 159752 | tf_op jit(solution)/shard_map/ppermute | solution.py:156
  63.7 5.7 %collective-permute-start.14 = (f32[104,128]{1,0:T(8,128)S(1)}, f32[104,128]{1,0:T(8,128)S(1)}, u32[]{:S(2)}, u32[]{:S(2)}) collective-permute-start(f32[104,128]{1,0:T(8,128)S(1)} %add.33.a_ref), channel_id=1, source_target_pairs={{0,8},{2,10},{4,12},{6,14},{8,0},{10,2},{12,4},{14,6},{1,9},{3,11}... | collective-permute-start | bytes 159752 | tf_op jit(solution)/shard_map/ppermute | solution.py:156
  69.6 1.2 %collective-permute-start.15 = (f32[8,128]{1,0:T(8,128)S(1)}, f32[8,128]{1,0:T(8,128)S(1)}, u32[]{:S(2)}, u32[]{:S(2)}) collective-permute-start(f32[8,128]{1,0:T(8,128)S(1)} %part_rewards.1.a_ref), channel_id=1, source_target_pairs={{0,1},{1,0},{2,3},{3,2},{4,5},{5,4},{6,7},{7,6},{8,9},{9,8},{10,11... | collective-permute-start | bytes 12296 | tf_op jit(solution)/shard_map/ppermute | solution.py:156

commit v5 on v4

--- a/solution.py
+++ b/solution.py
@@ -231,7 +231,7 @@
 
 
 def first_part(ins, wg, wu, tiles, blocks, dtype):
-    n, width = chunks_of(tiles.cols, 512)
+    n, width = chunks_of(tiles.cols, 640)
     rows, features = ins[0].shape
     depth, k = wg.shape[0], len(blocks)
     return pl.pallas_call(
@@ -255,7 +255,7 @@
 
 
 def base_part(xn, wg, wu, dep, tiles, blocks, dtype):
-    n, width = chunks_of(tiles.cols, 512)
+    n, width = chunks_of(tiles.cols, 640)
     rows, depth, k = xn.shape[0], wg.shape[0], len(blocks)
     return pl.pallas_call(
         functools.partial(base_kernel, tiles, blocks, n, width),
@@ -302,15 +302,15 @@
     )(near, far)
 
 
-def mix_kernel(tiles, group, pair_ref, mix_ref):
+def mix_kernel(group, lows_ref, mix_ref):
     members = 8
     rank = group // 2
-    rows = pair_ref.shape[1]
+    rows = lows_ref.shape[0]
     height, depth = mix_ref.shape
     r0 = lax.broadcasted_iota(jnp.int32, (height, rows), 0)
     c0 = lax.broadcasted_iota(jnp.int32, (height, rows), 1)
     picks = (r0 - rows * count_steps(r0, rows, 2 * members) == c0).astype(f32).astype(bf16)
-    spread = dot_nn(picks, pair_ref[0, :, tiles.cols : tiles.ext])[:, 0:depth]
+    spread = dot_nn(picks, lows_ref[...])[:, 0:depth]
     r = lax.broadcasted_iota(jnp.int32, (height, depth), 0)
     c = lax.broadcasted_iota(jnp.int32, (height, depth), 1)
     step = count_steps(r, rows, 2 * members)
@@ -322,17 +322,17 @@
     mix_ref[...] = (share * (jnp.where(own, spread, 0.0) + jnp.where(base, 1.0, 0.0))).astype(bf16)
 
 
-def mixing(pair, tiles, group):
-    rows = pair.shape[1]
-    return pl.pallas_call(
-        functools.partial(mix_kernel, tiles, group),
+def mixing(lows, group):
+    rows = lows.shape[0]
+    return pl.pallas_call(
+        functools.partial(mix_kernel, group),
         out_shape=jax.ShapeDtypeStruct((16 * rows, 8 * group + 2 * rows), bf16),
         in_specs=[in_vmem],
         out_specs=in_vmem,
         compiler_params=pltpu.CompilerParams(vmem_limit_bytes=8 * MiB),
         cost_estimate=small_cost,
         name="mixing",
-    )(pair)
+    )(lows)
 
 
 def hidden_kernel(tiles, blocks, held, loads, first, last, ahead, rows, down_scale, *refs):
@@ -372,8 +372,8 @@
     n, width = chunks_of(tiles.cols, 640)
     for b, ((dy, dz1), at, pair_ref) in enumerate(zip(blocks, starts, pair_refs)):
         right_ref[0:top, :] = fac_ref[:, pl.ds(at, tiles.cols)]
-        right_ref[top : top + rows, :] = pair_ref[0, :, 0 : tiles.cols]
-        right_ref[top + rows : top + 2 * rows, :] = pair_ref[1, :, 0 : tiles.cols]
+        right_ref[top : top + rows, :] = pair_ref[0]
+        right_ref[top + rows : top + 2 * rows, :] = pair_ref[1]
         for c in range(n):
             span = pl.ds(c * width, width)
             both = dot_nn(mix, right_ref[:, span])
@@ -604,7 +604,7 @@
     four = jnp.concatenate([two, two_z1])
     far_four = over_y(four)
 
-    far1 = over_y(after(far1, near0))
+    far1 = over_y(after(far1, two))
     mine = near1 + far1.astype(f32) + from_z1.astype(f32)
     send = mine.astype(bf16)
     from_z2 = over_z2(send)
@@ -612,9 +612,10 @@
     head_rows = lax.dynamic_slice_in_dim(heads, (p * block) % heads.shape[0], block, 0)
     head = jnp.where((p * block) // heads.shape[0] == t, head_rows, over_t(head_rows))
     far_four = after(far_four, head)
-    pair = (mine + from_z2.astype(f32)).astype(bf16)
-
-    mix = mixing(pair, tiles, 2 * rank)
+    sums = (mine + from_z2.astype(f32)).astype(bf16)
+    pair, lows = sums[:, :, : tiles.cols], sums[0, :, tiles.cols :]
+
+    mix = mixing(lows, 2 * rank)
     step = functools.partial(hidden_step, mix, collect(four, far_four))
     tail, wd = (dif, tiles), down_weight_matrix
     pair_z = over_z1(pair)

time: 77.7 us -> 75.8 us (0.976)
  waiting for transfers between devices: 22.8 us -> 19.7 us
  starting transfers between devices: 17 us -> 19 us
    ppermute x16, waiting for transfers between devices: 22.8 us -> 19.7 us  [swap(): return lax.ppermute(x, axis, [(i, i ^ bit) for i in range(size)])]
    ppermute x16, starting transfers between devices: 17 us -> 19 us  [swap(): return lax.ppermute(x, axis, [(i, i ^ bit) for i in range(size)])]
  transfers between devices with their start and end apart: 16 -> 16, of which waited for: 9 -> 8; matrix products, arithmetic and copies ran while one was open for 1% -> 1% of each run, Pallas kernels for 32% -> 32%
where the time goes in v5:
time: 75.8 us; the launch traced here: 75.6 us
  Pallas kernels  33.4 us (44%)
  waiting for transfers between devices  19.7 us (26%)
  starting transfers between devices  19 us (25%)
  other arithmetic  1.24 us (2%)
  local copies, waits for them, and re-layouts  1.12 us (1%)
  between operations  1.07 us (1%)
    ppermute x16, waiting for transfers between devices, swap(): return lax.ppermute(x, axis, [(i, i ^ bit) for i in range(size)])  19.7 us
    ppermute x16, starting transfers between devices, swap(): return lax.ppermute(x, axis, [(i, i ^ bit) for i in range(size)])  19 us
    pallas_call x3, Pallas kernels, hidden_step(): pl.pallas_call(functools.partial(hidden_kernel, tiles, blocks, held, load...  11.3 us
    pallas_call x2, Pallas kernels, base_part(): pl.pallas_call(functools.partial(base_kernel, tiles, blocks, n, width), o...  7.5 us
    pallas_call x1, Pallas kernels, first_part(): pl.pallas_call(functools.partial(first_kernel, tiles, blocks, n, width),...  7.29 us
    pallas_call x1, Pallas kernels, updates(): pl.pallas_call(functools.partial(update_kernel, n, high), out_shape=(jax....  6.46 us
  transfers between devices with their start and end apart: 16, of which 8 were waited for; matrix products, arithmetic and copies ran while one was open for 1% of the time, Pallas kernels for 32%

profile of v5, /device:TPU:0, one launch (start us, length us, event | category | flops | bytes accessed | tf_op | source)
XLA Modules:
  0.0 75.6 jit_solution(6178611218510264910)
XLA Ops:
  0.6 0.9 %fusion.1 = (bf16[1,8,7424]{2,1,0:T(8,128)(2,1)S(1)}, bf16[8,7424]{1,0:T(8,128)(2,1)S(1)}) fusion(bf16[4,7424]{1,0:T(4,128)(2,1)} %bitcast.27, bf16[4,7424]{1,0:T(4,128)(2,1)} %bitcast.28), kind=kLoop, calls=%fused_computation.11 | loop fusion | flops 237568 | bytes 356352 | tf_op jit(solution)/shard_map/stack | solution.py:596
  1.5 4.1 %collective-permute-start = (bf16[8,7424]{1,0:T(8,128)(2,1)S(1)}, bf16[8,7424]{1,0:T(8,128)(2,1)S(1)}, u32[]{:S(2)}, u32[]{:S(2)}) collective-permute-start(bf16[8,7424]{1,0:T(8,128)(2,1)S(1)} %get-tuple-element.45), channel_id=1, source_target_pairs={{0,8},{2,10},{4,12},{6,14},{8,0},{10,2},{12,4},{14,6},{1,9},{3,11}... | collective-permute-start | bytes 356360 | tf_op jit(solution)/shard_map/ppermute | solution.py:156
  5.7 7.3 %first.1 = (bf16[24,1152]{1,0:T(8,128)(2,1)}, bf16[2,24,2048]{2,1,0:T(8,128)(2,1)}, bf16[2,24,2048]{2,1,0:T(8,128)(2,1)}) custom-call(bf16[24,8192]{1,0:T(8,128)(2,1)} %x_ref.1, bf16[4,8192]{1,0:T(4,128)(2,1)} %bitcast.24, bf16[4,8192]{1,0:T(4,128)(2,1)} %bitcast.25, bf16[1024,7424]{1,0:T(8,128)(2,1)} %wg_ref.3, bf16[1024,7424]{1,0:T(8,128)(2,1)} %wu_ref.3), custom_call_target="tpu_custom_call" | custom-call | flops 1024 | bytes 1024 | tf_op jit(solution)/shard_map/first/pallas_call | solution.py:237
  13.0 1.6 %collective-permute-start.3 = (bf16[2,24,2048]{2,1,0:T(8,128)(2,1)}, bf16[2,24,2048]{2,1,0:T(8,128)(2,1)S(1)}, u32[]{:S(2)}, u32[]{:S(2)}) collective-permute-start(bf16[2,24,2048]{2,1,0:T(8,128)(2,1)} %get-tuple-element.27), channel_id=1, source_target_pairs={{0,2},{2,0},{4,6},{6,4},{8,10},{10,8},{12,14},{14,12},{1,3},{3,1},... | collective-permute-start | bytes 589832 | tf_op jit(solution)/shard_map/ppermute | solution.py:156
  14.6 0.1 reshape.13.refs_4_.refs_6_.dif_ref
  14.7 0.0 collective-permute-done
  14.7 1.6 %collective-permute-start.1 = (bf16[2,8,7424]{2,1,0:T(8,128)(2,1)S(1)}, bf16[2,8,7424]{2,1,0:T(8,128)(2,1)S(1)}, u32[]{:S(2)}, u32[]{:S(2)}) collective-permute-start(bf16[2,8,7424]{2,1,0:T(8,128)(2,1)S(1)} %pad_maximum_fusion.dep_ref), channel_id=1, source_target_pairs={{0,4},{2,6},{4,0},{6,2},{8,12},{10,14},{12,8},{14,10},{1,5},{3,7},... | collective-permute-start | bytes 712712 | tf_op jit(solution)/shard_map/ppermute | solution.py:156
  16.4 0.5 collective-permute-start.2
  16.9 0.8 %copy-done.1 = bf16[24,1152]{1,0:T(8,128)(2,1)S(1)} copy-done((bf16[24,1152]{1,0:T(8,128)(2,1)S(1)}, bf16[24,1152]{1,0:T(8,128)(2,1)}, u32[]{:S(2)}) %copy-start.1) | copy-done | bytes 55320
  17.7 3.7 %base_y0z1.1 = f32[2,24,2048]{2,1,0:T(8,128)S(1)} custom-call(bf16[24,1152]{1,0:T(8,128)(2,1)S(1)} %copy-done.1, bf16[1024,7424]{1,0:T(8,128)(2,1)} %wg_ref.3, bf16[1024,7424]{1,0:T(8,128)(2,1)} %wu_ref.3, bf16[2,8,7424]{2,1,0:T(8,128)(2,1)S(1)} %pad_maximum_fusion.dep_ref), custom_call_target="tpu_custom_call" | custom-call | flops 1024 | bytes 1024 | tf_op jit(solution)/shard_map/base_y0z1/pallas_call | solution.py:260
  21.4 0.1 add_convert_fusion.1
  21.5 1.3 %collective-permute-start.4 = (bf16[2,24,2048]{2,1,0:T(8,128)(2,1)S(1)}, bf16[2,24,2048]{2,1,0:T(8,128)(2,1)S(1)}, u32[]{:S(2)}, u32[]{:S(2)}) collective-permute-start(bf16[2,24,2048]{2,1,0:T(8,128)(2,1)S(1)} %add_convert_fusion.1), channel_id=1, source_target_pairs={{0,4},{2,6},{4,0},{6,2},{8,12},{10,14},{12,8},{14,10},{1,5},{3,7},... | collective-permute-start | bytes 589832 | tf_op jit(solution)/shard_map/ppermute | solution.py:156
  22.8 0.0 copy-start.3
  22.8 0.0 collective-permute-done.1.dep_ref
  22.8 3.8 %base_y0z0.1 = f32[2,24,2048]{2,1,0:T(8,128)S(1)} custom-call(bf16[24,1152]{1,0:T(8,128)(2,1)S(1)} %copy-done.1, bf16[1024,7424]{1,0:T(8,128)(2,1)} %wg_ref.3, bf16[1024,7424]{1,0:T(8,128)(2,1)} %wu_ref.3, bf16[2,8,7424]{2,1,0:T(8,128)(2,1)S(1)} %collective-permute-done.1.dep_ref), custom_call_target="tpu_custom_call" | custom-call | flops 1024 | bytes 1024 | tf_op jit(solution)/shard_map/base_y0z0/pallas_call | solution.py:260
  26.6 0.6 collective-permute-done.4
  27.2 0.1 fusion
  27.3 0.9 %collective-permute-start.5 = (bf16[2,24,2048]{2,1,0:T(8,128)(2,1)S(1)}, bf16[2,24,2048]{2,1,0:T(8,128)(2,1)S(1)}, u32[]{:S(2)}, u32[]{:S(2)}) collective-permute-start(bf16[2,24,2048]{2,1,0:T(8,128)(2,1)S(1)} %fusion), channel_id=1, source_target_pairs={{0,8},{2,10},{4,12},{6,14},{8,0},{10,2},{12,4},{14,6},{1,9},{3,11}... | collective-permute-start | bytes 589832 | tf_op jit(solution)/shard_map/ppermute | solution.py:156
  28.2 1.1 %collective-permute-start.6 = (bf16[4,8,7424]{2,1,0:T(8,128)(2,1)S(1)}, bf16[4,8,7424]{2,1,0:T(8,128)(2,1)S(1)}, u32[]{:S(2)}, u32[]{:S(2)}) collective-permute-start(bf16[4,8,7424]{2,1,0:T(8,128)(2,1)S(1)} %constant_dynamic-update-slice_fusion.near_ref), channel_id=1, source_target_pairs={{0,2},{2,0},{4,6},{6,4},{8,10},{10,8},{12,14},{14,12},{1,3},{3,1},... | collective-permute-start | bytes 1425416 | tf_op jit(solution)/shard_map/ppermute | solution.py:156
  29.3 0.1 collective-permute-start.7
  29.4 7.4 %collective-permute-done.5 = bf16[2,24,2048]{2,1,0:T(8,128)(2,1)S(1)} collective-permute-done((bf16[2,24,2048]{2,1,0:T(8,128)(2,1)S(1)}, bf16[2,24,2048]{2,1,0:T(8,128)(2,1)S(1)}, u32[]{:S(2)}, u32[]{:S(2)}) %collective-permute-start.5) | collective-permute-done | bytes 196640 | tf_op jit(solution)/shard_map/ppermute | solution.py:156
  36.8 0.1 add_convert_fusion
  37.0 0.2 mixing.1.refs_0_
  37.1 0.1 collective-permute-start.8
  37.2 1.6 %collective-permute-start.10 = (bf16[2,24,1920]{2,1,0:T(8,128)(2,1)S(1)}, bf16[2,24,1920]{2,1,0:T(8,128)(2,1)S(1)}, u32[]{:S(2)}, u32[]{:S(2)}) collective-permute-start(bf16[2,24,1920]{2,1,0:T(8,128)(2,1)S(1)} %slice.13.refs_2_), channel_id=1, source_target_pairs={{0,2},{2,0},{4,6},{6,4},{8,10},{10,8},{12,14},{14,12},{1,3},{3,1},... | collective-permute-start | bytes 552968 | tf_op jit(solution)/shard_map/ppermute | solution.py:156
  38.8 0.1 broadcast_select_fusion.head_ref
  38.9 0.9 %collective-permute-done.6.far_ref = bf16[4,8,7424]{2,1,0:T(8,128)(2,1)S(1)} collective-permute-done((bf16[4,8,7424]{2,1,0:T(8,128)(2,1)S(1)}, bf16[4,8,7424]{2,1,0:T(8,128)(2,1)S(1)}, u32[]{:S(2)}, u32[]{:S(2)}) %collective-permute-start.6) | collective-permute-done | bytes 475168 | tf_op jit(solution)/shard_map/ppermute | solution.py:156
  39.8 0.1 collect.1.refs_1_
  39.9 3.8 %hidden_y0z0.1 = (f32[192,1024]{1,0:T(8,128)S(1)}, f32[192,32]{1,0:T(8,128)S(1)}, bf16[1920,1024]{1,0:T(8,128)(2,1)S(1)}) custom-call(bf16[384,112]{1,0:T(8,128)(2,1)S(1)} %mixing.1.refs_0_, bf16[64,7424]{1,0:T(8,128)(2,1)S(1)} %collect.1.refs_1_, bf16[2,24,1920]{2,1,0:T(8,128)(2,1)S(1)} %slice.13.refs_2_, bf16[7424,1024]{1,0:T(8,128)(2,1)} %refs_5_.1, ...), custom_call_target="tpu_custom_call" | custom-call | flops 1024 | bytes 1024 | tf_op jit(solution)/shard_map/hidden_y0z0/pallas_call | solution.py:449
  43.7 0.0 copy-start
  43.7 0.0 copy-start.5
  43.7 0.6 collective-permute-start.9
  44.3 5.1 %hidden_y0z1_y1z0.1 = (f32[192,1024]{1,0:T(8,128)S(1)}, f32[192,32]{1,0:T(8,128)S(1)}, bf16[1920,1024]{1,0:T(8,128)(2,1)S(1)}) custom-call(bf16[384,112]{1,0:T(8,128)(2,1)S(1)} %mixing.1.refs_0_, bf16[64,7424]{1,0:T(8,128)(2,1)S(1)} %collect.1.refs_1_, bf16[2,24,1920]{2,1,0:T(8,128)(2,1)S(1)} %collective-permute-done.8.refs_2_, ...), custom_call_target="tpu_custom_call" | custom-call | flops 1024 | bytes 1024 | tf_op jit(solution)/shard_map/hidden_y0z1_y1z0/pallas_call | solution.py:449
  49.4 2.3 %hidden_y1z1.1 = (f32[96,1024]{1,0:T(8,128)S(1)}, f32[96,1024]{1,0:T(8,128)S(1)}) custom-call(bf16[384,112]{1,0:T(8,128)(2,1)S(1)} %mixing.1.refs_0_, bf16[64,7424]{1,0:T(8,128)(2,1)S(1)} %collect.1.refs_1_, bf16[2,24,1920]{2,1,0:T(8,128)(2,1)S(1)} %collective-permute-done.9.refs_2_, bf16[1920,1024]{1,0:T(8,128)(2,1)S(1)} %get-tuple-element.36.refs_3_, ...), custom_call_target="tpu_custom_call" | custom-call | flops 1024 | bytes 1024 | tf_op jit(solution)/shard_map/hidden_y1z1/pallas_call | solution.py:449
  51.8 0.1 collective-permute-start.11
  51.8 1.7 %collective-permute-done.11.recv_ref = f32[96,1024]{1,0:T(8,128)S(1)} collective-permute-done((f32[96,1024]{1,0:T(8,128)S(1)}, f32[96,1024]{1,0:T(8,128)S(1)}, u32[]{:S(2)}, u32[]{:S(2)}) %collective-permute-start.11) | collective-permute-done | bytes 393248 | tf_op jit(solution)/shard_map/ppermute | solution.py:156
  53.5 0.4 part_logits.1
  54.0 1.6 %collective-permute-start.12 = (f32[104,128]{1,0:T(8,128)S(1)}, f32[104,128]{1,0:T(8,128)S(1)}, u32[]{:S(2)}, u32[]{:S(2)}) collective-permute-start(f32[104,128]{1,0:T(8,128)S(1)} %part_logits.1), channel_id=1, source_target_pairs={{0,2},{2,0},{4,6},{6,4},{8,10},{10,8},{12,14},{14,12},{1,3},{3,1},... | collective-permute-start | bytes 159752 | tf_op jit(solution)/shard_map/ppermute | solution.py:156
  55.6 2.6 %collective-permute-done.12 = f32[104,128]{1,0:T(8,128)S(1)} collective-permute-done((f32[104,128]{1,0:T(8,128)S(1)}, f32[104,128]{1,0:T(8,128)S(1)}, u32[]{:S(2)}, u32[]{:S(2)}) %collective-permute-start.12) | collective-permute-done | bytes 53280 | tf_op jit(solution)/shard_map/ppermute | solution.py:156
  58.2 1.2 %collective-permute-start.13 = (f32[104,128]{1,0:T(8,128)S(1)}, f32[104,128]{1,0:T(8,128)S(1)}, u32[]{:S(2)}, u32[]{:S(2)}) collective-permute-start(f32[104,128]{1,0:T(8,128)S(1)} %add.32), channel_id=1, source_target_pairs={{0,4},{2,6},{4,0},{6,2},{8,12},{10,14},{12,8},{14,10},{1,5},{3,7},... | collective-permute-start | bytes 159752 | tf_op jit(solution)/shard_map/ppermute | solution.py:156
  59.4 3.0 %collective-permute-done.13 = f32[104,128]{1,0:T(8,128)S(1)} collective-permute-done((f32[104,128]{1,0:T(8,128)S(1)}, f32[104,128]{1,0:T(8,128)S(1)}, u32[]{:S(2)}, u32[]{:S(2)}) %collective-permute-start.13) | collective-permute-done | bytes 53280 | tf_op jit(solution)/shard_map/ppermute | solution.py:156
  62.4 2.7 %collective-permute-start.14 = (f32[104,128]{1,0:T(8,128)S(1)}, f32[104,128]{1,0:T(8,128)S(1)}, u32[]{:S(2)}, u32[]{:S(2)}) collective-permute-start(f32[104,128]{1,0:T(8,128)S(1)} %add.33.a_ref), channel_id=1, source_target_pairs={{0,8},{2,10},{4,12},{6,14},{8,0},{10,2},{12,4},{14,6},{1,9},{3,11}... | collective-permute-start | bytes 159752 | tf_op jit(solution)/shard_map/ppermute | solution.py:156
  65.2 0.1 copy.14.targets_ref
  65.2 2.3 %collective-permute-done.14.b_ref = f32[104,128]{1,0:T(8,128)S(1)} collective-permute-done((f32[104,128]{1,0:T(8,128)S(1)}, f32[104,128]{1,0:T(8,128)S(1)}, u32[]{:S(2)}, u32[]{:S(2)}) %collective-permute-start.14) | collective-permute-done | bytes 53280 | tf_op jit(solution)/shard_map/ppermute | solution.py:156
  67.5 0.2 part_rewards.1.a_ref
  67.7 0.1 collective-permute-start.15
  67.8 1.2 %collective-permute-done.15.b_ref = f32[8,128]{1,0:T(8,128)S(1)} collective-permute-done((f32[8,128]{1,0:T(8,128)S(1)}, f32[8,128]{1,0:T(8,128)S(1)}, u32[]{:S(2)}, u32[]{:S(2)}) %collective-permute-start.15) | collective-permute-done | bytes 4128 | tf_op jit(solution)/shard_map/ppermute | solution.py:156
  69.0 6.5 %updates.1 = (bf16[7424,1024]{1,0:T(8,128)(2,1)}, f32[1,128]{1,0:T(1,128)}) custom-call(f32[8,128]{1,0:T(8,128)S(1)} %part_rewards.1.a_ref, f32[8,128]{1,0:T(8,128)S(1)} %collective-permute-done.15.b_ref, bf16[32,7424]{1,0:T(8,128)(2,1)S(1)} %reshape.13.refs_4_.refs_6_.dif_ref, bf16[32,1024]{1,0:T(8,128)(2,1)S(1)} %reshape.14.refs_7_.dout_ref), custom_call_target="tpu_custom_call" | custom-call | tf_op jit(solution)/shard_map/updates/pallas_call | solution.py:551
  (23 shorter events, 0.2 us)
Async XLA Ops:
  1.5 13.2 %collective-permute-start = (bf16[8,7424]{1,0:T(8,128)(2,1)S(1)}, bf16[8,7424]{1,0:T(8,128)(2,1)S(1)}, u32[]{:S(2)}, u32[]{:S(2)}) collective-permute-start(bf16[8,7424]{1,0:T(8,128)(2,1)S(1)} %get-tuple-element.45), channel_id=1, source_target_pairs={{0,8},{2,10},{4,12},{6,14},{8,0},{10,2},{12,4},{14,6},{1,9},{3,11}... | collective-permute-start | bytes 356360 | tf_op jit(solution)/shard_map/ppermute | solution.py:156
  5.7 8.9 %copy-start.4 = (bf16[8,1024,4]{1,2,0:T(4,128)(2,1)S(1)}, bf16[8,1024,4]{1,2,0:T(4,128)(2,1)}, u32[]{:S(2)}) copy-start(bf16[8,1024,4]{1,2,0:T(4,128)(2,1)} %param.21) | copy-start | bytes 196612
  5.7 8.9 %copy-start.2 = (bf16[8,7424,4]{1,2,0:T(4,128)(2,1)S(1)}, bf16[8,7424,4]{1,2,0:T(4,128)(2,1)}, u32[]{:S(2)}) copy-start(bf16[8,7424,4]{1,2,0:T(4,128)(2,1)} %param.20) | copy-start | bytes 1425412
  13.0 8.5 %collective-permute-start.3 = (bf16[2,24,2048]{2,1,0:T(8,128)(2,1)}, bf16[2,24,2048]{2,1,0:T(8,128)(2,1)S(1)}, u32[]{:S(2)}, u32[]{:S(2)}) collective-permute-start(bf16[2,24,2048]{2,1,0:T(8,128)(2,1)} %get-tuple-element.27), channel_id=1, source_target_pairs={{0,2},{2,0},{4,6},{6,4},{8,10},{10,8},{12,14},{14,12},{1,3},{3,1},... | collective-permute-start | bytes 589832 | tf_op jit(solution)/shard_map/ppermute | solution.py:156
  14.7 8.0 %collective-permute-start.1 = (bf16[2,8,7424]{2,1,0:T(8,128)(2,1)S(1)}, bf16[2,8,7424]{2,1,0:T(8,128)(2,1)S(1)}, u32[]{:S(2)}, u32[]{:S(2)}) collective-permute-start(bf16[2,8,7424]{2,1,0:T(8,128)(2,1)S(1)} %pad_maximum_fusion.dep_ref), channel_id=1, source_target_pairs={{0,4},{2,6},{4,0},{6,2},{8,12},{10,14},{12,8},{14,10},{1,5},{3,7},... | collective-permute-start | bytes 712712 | tf_op jit(solution)/shard_map/ppermute | solution.py:156
  16.4 10.2 %collective-permute-start.2 = (bf16[2,24,2048]{2,1,0:T(8,128)(2,1)}, bf16[2,24,2048]{2,1,0:T(8,128)(2,1)S(1)}, u32[]{:S(2)}, u32[]{:S(2)}) collective-permute-start(bf16[2,24,2048]{2,1,0:T(8,128)(2,1)} %get-tuple-element.26), channel_id=1, source_target_pairs={{0,2},{2,0},{4,6},{6,4},{8,10},{10,8},{12,14},{14,12},{1,3},{3,1},... | collective-permute-start | bytes 589832 | tf_op jit(solution)/shard_map/ppermute | solution.py:156
  16.9 0.8 %copy-start.1 = (bf16[24,1152]{1,0:T(8,128)(2,1)S(1)}, bf16[24,1152]{1,0:T(8,128)(2,1)}, u32[]{:S(2)}) copy-start(bf16[24,1152]{1,0:T(8,128)(2,1)} %get-tuple-element.23.xn_ref) | copy-start | bytes 165892
  21.5 5.7 %collective-permute-start.4 = (bf16[2,24,2048]{2,1,0:T(8,128)(2,1)S(1)}, bf16[2,24,2048]{2,1,0:T(8,128)(2,1)S(1)}, u32[]{:S(2)}, u32[]{:S(2)}) collective-permute-start(bf16[2,24,2048]{2,1,0:T(8,128)(2,1)S(1)} %add_convert_fusion.1), channel_id=1, source_target_pairs={{0,4},{2,6},{4,0},{6,2},{8,12},{10,14},{12,8},{14,10},{1,5},{3,7},... | collective-permute-start | bytes 589832 | tf_op jit(solution)/shard_map/ppermute | solution.py:156
  22.8 6.5 %copy-start.3 = (bf16[4096,128]{1,0:T(8,128)(2,1)S(1)}, bf16[4096,128]{1,0:T(8,128)(2,1)}, u32[]{:S(2)}) copy-start(bf16[4096,128]{1,0:T(8,128)(2,1)} %param.22) | copy-start | bytes 3145732
  27.3 9.6 %collective-permute-start.5 = (bf16[2,24,2048]{2,1,0:T(8,128)(2,1)S(1)}, bf16[2,24,2048]{2,1,0:T(8,128)(2,1)S(1)}, u32[]{:S(2)}, u32[]{:S(2)}) collective-permute-start(bf16[2,24,2048]{2,1,0:T(8,128)(2,1)S(1)} %fusion), channel_id=1, source_target_pairs={{0,8},{2,10},{4,12},{6,14},{8,0},{10,2},{12,4},{14,6},{1,9},{3,11}... | collective-permute-start | bytes 589832 | tf_op jit(solution)/shard_map/ppermute | solution.py:156
  28.2 11.5 %collective-permute-start.6 = (bf16[4,8,7424]{2,1,0:T(8,128)(2,1)S(1)}, bf16[4,8,7424]{2,1,0:T(8,128)(2,1)S(1)}, u32[]{:S(2)}, u32[]{:S(2)}) collective-permute-start(bf16[4,8,7424]{2,1,0:T(8,128)(2,1)S(1)} %constant_dynamic-update-slice_fusion.near_ref), channel_id=1, source_target_pairs={{0,2},{2,0},{4,6},{6,4},{8,10},{10,8},{12,14},{14,12},{1,3},{3,1},... | collective-permute-start | bytes 1425416 | tf_op jit(solution)/shard_map/ppermute | solution.py:156
  29.3 9.5 %collective-permute-start.7 = (bf16[1024,128]{1,0:T(8,128)(2,1)S(1)}, bf16[1024,128]{1,0:T(8,128)(2,1)S(1)}, u32[]{:S(2)}, u32[]{:S(2)}) collective-permute-start(bf16[1024,128]{1,0:T(8,128)(2,1)S(1)} %constant_dynamic-slice_fusion), channel_id=1, source_target_pairs={{0,1},{1,0},{2,3},{3,2},{4,5},{5,4},{6,7},{7,6},{8,9},{9,8},{10,11... | collective-permute-start | bytes 786440 | tf_op jit(solution)/shard_map/ppermute | solution.py:156
  37.1 6.6 %collective-permute-start.8 = (bf16[2,24,1920]{2,1,0:T(8,128)(2,1)S(1)}, bf16[2,24,1920]{2,1,0:T(8,128)(2,1)S(1)}, u32[]{:S(2)}, u32[]{:S(2)}) collective-permute-start(bf16[2,24,1920]{2,1,0:T(8,128)(2,1)S(1)} %slice.13.refs_2_), channel_id=1, source_target_pairs={{0,4},{2,6},{4,0},{6,2},{8,12},{10,14},{12,8},{14,10},{1,5},{3,7},... | collective-permute-start | bytes 552968 | tf_op jit(solution)/shard_map/ppermute | solution.py:156
  37.2 7.0 %collective-permute-start.10 = (bf16[2,24,1920]{2,1,0:T(8,128)(2,1)S(1)}, bf16[2,24,1920]{2,1,0:T(8,128)(2,1)S(1)}, u32[]{:S(2)}, u32[]{:S(2)}) collective-permute-start(bf16[2,24,1920]{2,1,0:T(8,128)(2,1)S(1)} %slice.13.refs_2_), channel_id=1, source_target_pairs={{0,2},{2,0},{4,6},{6,4},{8,10},{10,8},{12,14},{14,12},{1,3},{3,1},... | collective-permute-start | bytes 552968 | tf_op jit(solution)/shard_map/ppermute | solution.py:156
  43.7 9.9 %copy-start = (bf16[24,8192]{1,0:T(8,128)(2,1)S(1)}, bf16[24,8192]{1,0:T(8,128)(2,1)}, u32[]{:S(2)}) copy-start(bf16[24,8192]{1,0:T(8,128)(2,1)} %x_ref.1) | copy-start | bytes 1179652
  43.7 21.5 %copy-start.5 = (s32[24]{0:T(128)S(1)}, s32[24]{0:T(128)}, u32[]{:S(2)}) copy-start(s32[24]{0:T(128)} %param.23) | copy-start | bytes 292
  43.7 5.7 %collective-permute-start.9 = (bf16[2,24,1920]{2,1,0:T(8,128)(2,1)S(1)}, bf16[2,24,1920]{2,1,0:T(8,128)(2,1)S(1)}, u32[]{:S(2)}, u32[]{:S(2)}) collective-permute-start(bf16[2,24,1920]{2,1,0:T(8,128)(2,1)S(1)} %collective-permute-done.8.refs_2_), channel_id=1, source_target_pairs={{0,2},{2,0},{4,6},{6,4},{8,10},{10,8},{12,14},{14,12},{1,3},{3,1},... | collective-permute-start | bytes 552968 | tf_op jit(solution)/shard_map/ppermute | solution.py:156
  51.8 1.8 %collective-permute-start.11 = (f32[96,1024]{1,0:T(8,128)S(1)}, f32[96,1024]{1,0:T(8,128)S(1)}, u32[]{:S(2)}, u32[]{:S(2)}) collective-permute-start(f32[96,1024]{1,0:T(8,128)S(1)} %get-tuple-element.41), channel_id=1, source_target_pairs={{0,1},{1,0},{2,3},{3,2},{4,5},{5,4},{6,7},{7,6},{8,9},{9,8},{10,11... | collective-permute-start | bytes 1179656 | tf_op jit(solution)/shard_map/ppermute | solution.py:156
  54.0 4.2 %collective-permute-start.12 = (f32[104,128]{1,0:T(8,128)S(1)}, f32[104,128]{1,0:T(8,128)S(1)}, u32[]{:S(2)}, u32[]{:S(2)}) collective-permute-start(f32[104,128]{1,0:T(8,128)S(1)} %part_logits.1), channel_id=1, source_target_pairs={{0,2},{2,0},{4,6},{6,4},{8,10},{10,8},{12,14},{14,12},{1,3},{3,1},... | collective-permute-start | bytes 159752 | tf_op jit(solution)/shard_map/ppermute | solution.py:156
  58.2 4.2 %collective-permute-start.13 = (f32[104,128]{1,0:T(8,128)S(1)}, f32[104,128]{1,0:T(8,128)S(1)}, u32[]{:S(2)}, u32[]{:S(2)}) collective-permute-start(f32[104,128]{1,0:T(8,128)S(1)} %add.32), channel_id=1, source_target_pairs={{0,4},{2,6},{4,0},{6,2},{8,12},{10,14},{12,8},{14,10},{1,5},{3,7},... | collective-permute-start | bytes 159752 | tf_op jit(solution)/shard_map/ppermute | solution.py:156
  62.4 5.1 %collective-permute-start.14 = (f32[104,128]{1,0:T(8,128)S(1)}, f32[104,128]{1,0:T(8,128)S(1)}, u32[]{:S(2)}, u32[]{:S(2)}) collective-permute-start(f32[104,128]{1,0:T(8,128)S(1)} %add.33.a_ref), channel_id=1, source_target_pairs={{0,8},{2,10},{4,12},{6,14},{8,0},{10,2},{12,4},{14,6},{1,9},{3,11}... | collective-permute-start | bytes 159752 | tf_op jit(solution)/shard_map/ppermute | solution.py:156
  67.7 1.2 %collective-permute-start.15 = (f32[8,128]{1,0:T(8,128)S(1)}, f32[8,128]{1,0:T(8,128)S(1)}, u32[]{:S(2)}, u32[]{:S(2)}) collective-permute-start(f32[8,128]{1,0:T(8,128)S(1)} %part_rewards.1.a_ref), channel_id=1, source_target_pairs={{0,1},{1,0},{2,3},{3,2},{4,5},{5,4},{6,7},{7,6},{8,9},{9,8},{10,11... | collective-permute-start | bytes 12296 | tf_op jit(solution)/shard_map/ppermute | solution.py:156

commit v6 on v5

--- a/solution.py
+++ b/solution.py
@@ -189,11 +189,11 @@
 
 
 def first_kernel(tiles, blocks, n, width, *refs):
-    inputs, refs = refs[:3], refs[3:]
+    inputs, refs = refs[:2], refs[2:]
     wg_ref, wu_ref, xn_ref = refs[:3]
     outs, refs = refs[3 : 3 + len(blocks)], refs[3 + len(blocks) :]
-    held, (norm_ref, wg, wu, in_sems, sems) = refs[:3], refs[3:]
-    copies = [pltpu.make_async_copy(a, b, in_sems.at[i]) for i, (a, b) in enumerate(zip(inputs, held))]
+    held, (norm_ref, wg, wu, in_sems, sems) = refs[:2], refs[2:]
+    copies = [pltpu.make_async_copy(a, b, in_sems.at[i]) for i, (a, b) in enumerate(zip((inputs[0], inputs[1].at[:, 0 : held[1].shape[1]]), held))]
     for copy in copies:
         copy.start()
     jobs = base_jobs(tiles, blocks, n, width, wg_ref, wu_ref, wg, wu, outs, sems)
@@ -205,20 +205,19 @@
     for job in jobs[early : 2 * n]:
         job[0].start()
     p = cube()[0]
-    x_ref, gin_ref, uin_ref = held
+    x_ref, in_ref = held
     rows, features = x_ref.shape
-    rank = gin_ref.shape[0]
+    terms = in_ref.shape[0]
     depth = xn_ref.shape[1] - lane
     normed = scaled_rows(x_ref[...].astype(f32)).astype(bf16)
     norm_ref[...] = normed
     xn_ref[:, 0:depth] = norm_ref[:, pl.ds(pl.multiple_of(p * depth, lane), depth)]
     scale = noise_scale / math.sqrt(features)
-    place = lax.broadcasted_iota(jnp.int32, (rows, lane), 1) - p * (2 * rank)
+    place = lax.broadcasted_iota(jnp.int32, (rows, lane), 1) - p * terms
     tile = jnp.zeros((rows, lane), f32)
-    for i, ref in enumerate((gin_ref, uin_ref)):
-        low = scale * dot_nt(normed, ref[...])
-        for k in range(rank):
-            tile = jnp.where(place == i * rank + k, jnp.broadcast_to(low[:, k : k + 1], tile.shape), tile)
+    low = scale * dot_nt(normed, in_ref[...])
+    for k in range(terms):
+        tile = jnp.where(place == k, jnp.broadcast_to(low[:, k : k + 1], tile.shape), tile)
     xn_ref[:, depth : depth + lane] = tile.astype(bf16)
     products(tiles, jobs, 2 * n, 2 * n, xn_ref, outs)
 
@@ -238,9 +237,9 @@
         functools.partial(first_kernel, tiles, blocks, n, width),
         out_shape=(jax.ShapeDtypeStruct((rows, depth + lane), bf16),)
         + (jax.ShapeDtypeStruct((2, rows, tiles.ext), dtype),) * k,
-        in_specs=[in_hbm] * 5,
+        in_specs=[in_hbm] * 4,
         out_specs=(in_vmem,) * (1 + k),
-        scratch_shapes=[pltpu.VMEM(x.shape, x.dtype) for x in ins]
+        scratch_shapes=[pltpu.VMEM((x.shape[0], features), x.dtype) for x in ins]
         + [
             pltpu.VMEM((rows, features), bf16),
             pltpu.VMEM((k, depth, tiles.cols), bf16),
@@ -248,7 +247,7 @@
             pltpu.SemaphoreType.DMA((len(ins),)),
             pltpu.SemaphoreType.DMA((k, 2, n)),
         ],
-        compiler_params=pltpu.CompilerParams(vmem_limit_bytes=62 * MiB),
+        compiler_params=pltpu.CompilerParams(vmem_limit_bytes=52 * MiB),
         cost_estimate=small_cost,
         name="first",
     )(*ins, wg, wu)
@@ -588,8 +587,10 @@
     dif = turned(down_input_factors).reshape(members * rank, units)
     dout = turned(down_out).reshape(members * rank, block)
 
-    ins = (prompts, turned(gate_in)[0], turned(up_in)[0])
+    ends = jnp.concatenate([turned(gate_in)[0], turned(up_in)[0]])
     fac = jnp.concatenate([turned(gate_output_factors)[0], turned(up_output_factors)[0]])
+    packed = lax.optimization_barrier(jnp.concatenate([ends, fac], axis=1))
+    ins, fac = (prompts, packed), packed[:, width:]
     after = lambda x, *done: lax.optimization_barrier((x, *done))[0]
     weights = gate_weight, up_weight
 

time: 75.8 us -> 76.3 us (level)
  starting transfers between devices: 19 us -> 19.9 us
  Pallas kernels: 33.4 us -> 32.6 us
    concatenate x0 -> x1, other arithmetic: none -> 1.06 us  [cube_body(): packed = lax.optimization_barrier(jnp.concatenate([ends, fac], axis=1))]
    another operation x2 -> x1, other arithmetic: 0.94 us -> 0.03 us  [cube_body(): two = jnp.stack([fac, over_z2(fac)])]
    ppermute x16, starting transfers between devices: 19 us -> 19.9 us  [swap(): return lax.ppermute(x, axis, [(i, i ^ bit) for i in range(size)])]
  transfers between devices with their start and end apart: 16 -> 16, of which waited for: 8 -> 9; matrix products, arithmetic and copies ran while one was open for 1% -> 1% of each run, Pallas kernels for 32% -> 31%
where the time goes in v6:
time: 76.3 us; the launch traced here: 76.1 us
  Pallas kernels  32.6 us (43%)
  starting transfers between devices  19.9 us (26%)
  waiting for transfers between devices  19.9 us (26%)
  other arithmetic  1.36 us (2%)
  local copies, waits for them, and re-layouts  1.32 us (2%)
  between operations  1.07 us (1%)
    ppermute x16, waiting for transfers between devices, swap(): return lax.ppermute(x, axis, [(i, i ^ bit) for i in range(size)])  19.9 us
    ppermute x16, starting transfers between devices, swap(): return lax.ppermute(x, axis, [(i, i ^ bit) for i in range(size)])  19.9 us
    pallas_call x3, Pallas kernels, hidden_step(): pl.pallas_call(functools.partial(hidden_kernel, tiles, blocks, held, load...  11.3 us
    pallas_call x2, Pallas kernels, base_part(): pl.pallas_call(functools.partial(base_kernel, tiles, blocks, n, width), o...  7.49 us
    pallas_call x1, Pallas kernels, first_part(): pl.pallas_call(functools.partial(first_kernel, tiles, blocks, n, width),...  6.61 us
    pallas_call x1, Pallas kernels, updates(): pl.pallas_call(functools.partial(update_kernel, n, high), out_shape=(jax....  6.46 us
  transfers between devices with their start and end apart: 16, of which 9 were waited for; matrix products, arithmetic and copies ran while one was open for 1% of the time, Pallas kernels for 31%

profile of v6, /device:TPU:0, one launch (start us, length us, event | category | flops | bytes accessed | tf_op | source)
XLA Modules:
  0.0 76.1 jit_solution(8835945229565000170)
XLA Ops:
  0.6 1.1 %maximum_maximum_fusion.refs_1_ = bf16[8,15616]{1,0:T(8,128)(2,1)S(1)} fusion(bf16[4,7424]{1,0:T(4,128)(2,1)} %bitcast.27, bf16[4,7424]{1,0:T(4,128)(2,1)} %bitcast.28, bf16[4,8192]{1,0:T(4,128)(2,1)} %bitcast.24, bf16[4,8192]{1,0:T(4,128)(2,1)} %bitcast.25), kind=kLoop, calls=%fused_computation.4 | loop fusion | flops 999424 | bytes 499712 | tf_op jit(solution)/shard_map/concatenate | solution.py:592
  1.7 4.1 %collective-permute-start = (bf16[8,7424]{1,0:T(8,128)(2,1)S(1)}, bf16[8,7424]{1,0:T(8,128)(2,1)S(1)}, u32[]{:S(2)}, u32[]{:S(2)}) collective-permute-start(bf16[8,7424]{1,0:T(8,128)(2,1)S(1)} %get-tuple-element.45), channel_id=1, source_target_pairs={{0,8},{2,10},{4,12},{6,14},{8,0},{10,2},{12,4},{14,6},{1,9},{3,11}... | collective-permute-start | bytes 356360 | tf_op jit(solution)/shard_map/ppermute | solution.py:156
  5.8 1.0 %copy-done = bf16[24,8192]{1,0:T(8,128)(2,1)S(1)} copy-done((bf16[24,8192]{1,0:T(8,128)(2,1)S(1)}, bf16[24,8192]{1,0:T(8,128)(2,1)}, u32[]{:S(2)}) %copy-start) | copy-done | bytes 393240
  6.8 6.6 %first.1 = (bf16[24,1152]{1,0:T(8,128)(2,1)S(1)}, bf16[2,24,2048]{2,1,0:T(8,128)(2,1)S(1)}, bf16[2,24,2048]{2,1,0:T(8,128)(2,1)S(1)}) custom-call(bf16[24,8192]{1,0:T(8,128)(2,1)S(1)} %copy-done, bf16[8,15616]{1,0:T(8,128)(2,1)S(1)} %maximum_maximum_fusion.refs_1_, bf16[1024,7424]{1,0:T(8,128)(2,1)} %wg_ref.3, bf16[1024,7424]{1,0:T(8,128)(2,1)} %wu_ref.3), custom_call_target="tpu_custom_call" | custom-call | flops 1024 | bytes 1024 | tf_op jit(solution)/shard_map/first/pallas_call | solution.py:236
  13.4 1.6 %collective-permute-start.3 = (bf16[2,24,2048]{2,1,0:T(8,128)(2,1)S(1)}, bf16[2,24,2048]{2,1,0:T(8,128)(2,1)S(1)}, u32[]{:S(2)}, u32[]{:S(2)}) collective-permute-start(bf16[2,24,2048]{2,1,0:T(8,128)(2,1)S(1)} %get-tuple-element.27), channel_id=1, source_target_pairs={{0,2},{2,0},{4,6},{6,4},{8,10},{10,8},{12,14},{14,12},{1,3},{3,1},... | collective-permute-start | bytes 589832 | tf_op jit(solution)/shard_map/ppermute | solution.py:156
  15.1 0.1 reshape.13.refs_4_.refs_6_.dif_ref
  15.2 1.6 %collective-permute-start.1 = (bf16[2,8,7424]{2,1,0:T(8,128)(2,1)S(1)}, bf16[2,8,7424]{2,1,0:T(8,128)(2,1)S(1)}, u32[]{:S(2)}, u32[]{:S(2)}) collective-permute-start(bf16[2,8,7424]{2,1,0:T(8,128)(2,1)S(1)} %pad_maximum_fusion.dep_ref), channel_id=1, source_target_pairs={{0,4},{2,6},{4,0},{6,2},{8,12},{10,14},{12,8},{14,10},{1,5},{3,7},... | collective-permute-start | bytes 712712 | tf_op jit(solution)/shard_map/ppermute | solution.py:156
  16.9 0.5 collective-permute-start.2
  17.4 3.7 %base_y0z1.1 = f32[2,24,2048]{2,1,0:T(8,128)S(1)} custom-call(bf16[24,1152]{1,0:T(8,128)(2,1)S(1)} %get-tuple-element.23.xn_ref, bf16[1024,7424]{1,0:T(8,128)(2,1)} %wg_ref.3, bf16[1024,7424]{1,0:T(8,128)(2,1)} %wu_ref.3, bf16[2,8,7424]{2,1,0:T(8,128)(2,1)S(1)} %pad_maximum_fusion.dep_ref), custom_call_target="tpu_custom_call" | custom-call | flops 1024 | bytes 1024 | tf_op jit(solution)/shard_map/base_y0z1/pallas_call | solution.py:259
  21.1 0.1 collective-permute-done.3
  21.3 1.8 %collective-permute-start.4 = (bf16[2,24,2048]{2,1,0:T(8,128)(2,1)S(1)}, bf16[2,24,2048]{2,1,0:T(8,128)(2,1)S(1)}, u32[]{:S(2)}, u32[]{:S(2)}) collective-permute-start(bf16[2,24,2048]{2,1,0:T(8,128)(2,1)S(1)} %add_convert_fusion.1), channel_id=1, source_target_pairs={{0,4},{2,6},{4,0},{6,2},{8,12},{10,14},{12,8},{14,10},{1,5},{3,7},... | collective-permute-start | bytes 589832 | tf_op jit(solution)/shard_map/ppermute | solution.py:156
  23.0 0.0 copy-start.3
  23.0 0.0 collective-permute-done.1.dep_ref
  23.1 3.8 %base_y0z0.1 = f32[2,24,2048]{2,1,0:T(8,128)S(1)} custom-call(bf16[24,1152]{1,0:T(8,128)(2,1)S(1)} %get-tuple-element.23.xn_ref, bf16[1024,7424]{1,0:T(8,128)(2,1)} %wg_ref.3, bf16[1024,7424]{1,0:T(8,128)(2,1)} %wu_ref.3, bf16[2,8,7424]{2,1,0:T(8,128)(2,1)S(1)} %collective-permute-done.1.dep_ref), custom_call_target="tpu_custom_call" | custom-call | flops 1024 | bytes 1024 | tf_op jit(solution)/shard_map/base_y0z0/pallas_call | solution.py:259
  26.9 0.1 collective-permute-done.4
  27.0 0.1 fusion
  27.1 0.5 collective-permute-start.5
  27.6 1.6 %collective-permute-start.6 = (bf16[4,8,7424]{2,1,0:T(8,128)(2,1)S(1)}, bf16[4,8,7424]{2,1,0:T(8,128)(2,1)S(1)}, u32[]{:S(2)}, u32[]{:S(2)}) collective-permute-start(bf16[4,8,7424]{2,1,0:T(8,128)(2,1)S(1)} %constant_dynamic-update-slice_fusion.near_ref), channel_id=1, source_target_pairs={{0,2},{2,0},{4,6},{6,4},{8,10},{10,8},{12,14},{14,12},{1,3},{3,1},... | collective-permute-start | bytes 1425416 | tf_op jit(solution)/shard_map/ppermute | solution.py:156
  29.2 0.1 collective-permute-start.7
  29.3 7.3 %collective-permute-done.5 = bf16[2,24,2048]{2,1,0:T(8,128)(2,1)S(1)} collective-permute-done((bf16[2,24,2048]{2,1,0:T(8,128)(2,1)S(1)}, bf16[2,24,2048]{2,1,0:T(8,128)(2,1)S(1)}, u32[]{:S(2)}, u32[]{:S(2)}) %collective-permute-start.5) | collective-permute-done | bytes 196640 | tf_op jit(solution)/shard_map/ppermute | solution.py:156
  36.5 0.1 add_convert_fusion
  36.7 0.2 mixing.1.refs_0_
  36.8 0.1 collective-permute-start.8
  36.9 1.6 %collective-permute-start.10 = (bf16[2,24,1920]{2,1,0:T(8,128)(2,1)S(1)}, bf16[2,24,1920]{2,1,0:T(8,128)(2,1)S(1)}, u32[]{:S(2)}, u32[]{:S(2)}) collective-permute-start(bf16[2,24,1920]{2,1,0:T(8,128)(2,1)S(1)} %slice.18.refs_2_), channel_id=1, source_target_pairs={{0,2},{2,0},{4,6},{6,4},{8,10},{10,8},{12,14},{14,12},{1,3},{3,1},... | collective-permute-start | bytes 552968 | tf_op jit(solution)/shard_map/ppermute | solution.py:156
  38.6 0.0 collective-permute-done.7
  38.6 0.1 broadcast_select_fusion.head_ref
  38.6 1.5 %collective-permute-done.6.far_ref = bf16[4,8,7424]{2,1,0:T(8,128)(2,1)S(1)} collective-permute-done((bf16[4,8,7424]{2,1,0:T(8,128)(2,1)S(1)}, bf16[4,8,7424]{2,1,0:T(8,128)(2,1)S(1)}, u32[]{:S(2)}, u32[]{:S(2)}) %collective-permute-start.6) | collective-permute-done | bytes 475168 | tf_op jit(solution)/shard_map/ppermute | solution.py:156
  40.1 0.1 collect.1.refs_1_
  40.2 3.8 %hidden_y0z0.1 = (f32[192,1024]{1,0:T(8,128)S(1)}, f32[192,32]{1,0:T(8,128)S(1)}, bf16[1920,1024]{1,0:T(8,128)(2,1)S(1)}) custom-call(bf16[384,112]{1,0:T(8,128)(2,1)S(1)} %mixing.1.refs_0_, bf16[64,7424]{1,0:T(8,128)(2,1)S(1)} %collect.1.refs_1_, bf16[2,24,1920]{2,1,0:T(8,128)(2,1)S(1)} %slice.18.refs_2_, bf16[7424,1024]{1,0:T(8,128)(2,1)} %refs_5_.1, ...), custom_call_target="tpu_custom_call" | custom-call | flops 1024 | bytes 1024 | tf_op jit(solution)/shard_map/hidden_y0z0/pallas_call | solution.py:448
  44.0 0.0 copy-start.1
  44.0 0.0 copy-start.5
  44.1 0.7 collective-permute-start.9
  44.8 5.2 %hidden_y0z1_y1z0.1 = (f32[192,1024]{1,0:T(8,128)S(1)}, f32[192,32]{1,0:T(8,128)S(1)}, bf16[1920,1024]{1,0:T(8,128)(2,1)S(1)}) custom-call(bf16[384,112]{1,0:T(8,128)(2,1)S(1)} %mixing.1.refs_0_, bf16[64,7424]{1,0:T(8,128)(2,1)S(1)} %collect.1.refs_1_, bf16[2,24,1920]{2,1,0:T(8,128)(2,1)S(1)} %collective-permute-done.8.refs_2_, ...), custom_call_target="tpu_custom_call" | custom-call | flops 1024 | bytes 1024 | tf_op jit(solution)/shard_map/hidden_y0z1_y1z0/pallas_call | solution.py:448
  50.0 2.3 %hidden_y1z1.1 = (f32[96,1024]{1,0:T(8,128)S(1)}, f32[96,1024]{1,0:T(8,128)S(1)}) custom-call(bf16[384,112]{1,0:T(8,128)(2,1)S(1)} %mixing.1.refs_0_, bf16[64,7424]{1,0:T(8,128)(2,1)S(1)} %collect.1.refs_1_, bf16[2,24,1920]{2,1,0:T(8,128)(2,1)S(1)} %collective-permute-done.9.refs_2_, bf16[1920,1024]{1,0:T(8,128)(2,1)S(1)} %get-tuple-element.36.refs_3_, ...), custom_call_target="tpu_custom_call" | custom-call | flops 1024 | bytes 1024 | tf_op jit(solution)/shard_map/hidden_y1z1/pallas_call | solution.py:448
  52.3 0.1 collective-permute-start.11
  52.4 1.7 %collective-permute-done.11.recv_ref = f32[96,1024]{1,0:T(8,128)S(1)} collective-permute-done((f32[96,1024]{1,0:T(8,128)S(1)}, f32[96,1024]{1,0:T(8,128)S(1)}, u32[]{:S(2)}, u32[]{:S(2)}) %collective-permute-start.11) | collective-permute-done | bytes 393248 | tf_op jit(solution)/shard_map/ppermute | solution.py:156
  54.1 0.3 part_logits.1
  54.4 1.4 %collective-permute-start.12 = (f32[104,128]{1,0:T(8,128)S(1)}, f32[104,128]{1,0:T(8,128)S(1)}, u32[]{:S(2)}, u32[]{:S(2)}) collective-permute-start(f32[104,128]{1,0:T(8,128)S(1)} %part_logits.1), channel_id=1, source_target_pairs={{0,2},{2,0},{4,6},{6,4},{8,10},{10,8},{12,14},{14,12},{1,3},{3,1},... | collective-permute-start | bytes 159752 | tf_op jit(solution)/shard_map/ppermute | solution.py:156
  55.8 2.8 %collective-permute-done.12 = f32[104,128]{1,0:T(8,128)S(1)} collective-permute-done((f32[104,128]{1,0:T(8,128)S(1)}, f32[104,128]{1,0:T(8,128)S(1)}, u32[]{:S(2)}, u32[]{:S(2)}) %collective-permute-start.12) | collective-permute-done | bytes 53280 | tf_op jit(solution)/shard_map/ppermute | solution.py:156
  58.6 1.7 %collective-permute-start.13 = (f32[104,128]{1,0:T(8,128)S(1)}, f32[104,128]{1,0:T(8,128)S(1)}, u32[]{:S(2)}, u32[]{:S(2)}) collective-permute-start(f32[104,128]{1,0:T(8,128)S(1)} %add.32), channel_id=1, source_target_pairs={{0,4},{2,6},{4,0},{6,2},{8,12},{10,14},{12,8},{14,10},{1,5},{3,7},... | collective-permute-start | bytes 159752 | tf_op jit(solution)/shard_map/ppermute | solution.py:156
  60.3 2.7 %collective-permute-done.13 = f32[104,128]{1,0:T(8,128)S(1)} collective-permute-done((f32[104,128]{1,0:T(8,128)S(1)}, f32[104,128]{1,0:T(8,128)S(1)}, u32[]{:S(2)}, u32[]{:S(2)}) %collective-permute-start.13) | collective-permute-done | bytes 53280 | tf_op jit(solution)/shard_map/ppermute | solution.py:156
  63.0 2.4 %collective-permute-start.14 = (f32[104,128]{1,0:T(8,128)S(1)}, f32[104,128]{1,0:T(8,128)S(1)}, u32[]{:S(2)}, u32[]{:S(2)}) collective-permute-start(f32[104,128]{1,0:T(8,128)S(1)} %add.33.a_ref), channel_id=1, source_target_pairs={{0,8},{2,10},{4,12},{6,14},{8,0},{10,2},{12,4},{14,6},{1,9},{3,11}... | collective-permute-start | bytes 159752 | tf_op jit(solution)/shard_map/ppermute | solution.py:156
  65.4 0.1 copy.14.targets_ref
  65.5 2.6 %collective-permute-done.14.b_ref = f32[104,128]{1,0:T(8,128)S(1)} collective-permute-done((f32[104,128]{1,0:T(8,128)S(1)}, f32[104,128]{1,0:T(8,128)S(1)}, u32[]{:S(2)}, u32[]{:S(2)}) %collective-permute-start.14) | collective-permute-done | bytes 53280 | tf_op jit(solution)/shard_map/ppermute | solution.py:156
  68.1 0.2 part_rewards.1.a_ref
  68.3 0.1 collective-permute-start.15
  68.3 1.2 %collective-permute-done.15.b_ref = f32[8,128]{1,0:T(8,128)S(1)} collective-permute-done((f32[8,128]{1,0:T(8,128)S(1)}, f32[8,128]{1,0:T(8,128)S(1)}, u32[]{:S(2)}, u32[]{:S(2)}) %collective-permute-start.15) | collective-permute-done | bytes 4128 | tf_op jit(solution)/shard_map/ppermute | solution.py:156
  69.5 6.5 %updates.1 = (bf16[7424,1024]{1,0:T(8,128)(2,1)}, f32[1,128]{1,0:T(1,128)}) custom-call(f32[8,128]{1,0:T(8,128)S(1)} %part_rewards.1.a_ref, f32[8,128]{1,0:T(8,128)S(1)} %collective-permute-done.15.b_ref, bf16[32,7424]{1,0:T(8,128)(2,1)S(1)} %reshape.13.refs_4_.refs_6_.dif_ref, bf16[32,1024]{1,0:T(8,128)(2,1)S(1)} %reshape.14.refs_7_.dout_ref), custom_call_target="tpu_custom_call" | custom-call | tf_op jit(solution)/shard_map/updates/pallas_call | solution.py:550
  (24 shorter events, 0.2 us)
Async XLA Ops:
  1.7 13.5 %collective-permute-start = (bf16[8,7424]{1,0:T(8,128)(2,1)S(1)}, bf16[8,7424]{1,0:T(8,128)(2,1)S(1)}, u32[]{:S(2)}, u32[]{:S(2)}) collective-permute-start(bf16[8,7424]{1,0:T(8,128)(2,1)S(1)} %get-tuple-element.45), channel_id=1, source_target_pairs={{0,8},{2,10},{4,12},{6,14},{8,0},{10,2},{12,4},{14,6},{1,9},{3,11}... | collective-permute-start | bytes 356360 | tf_op jit(solution)/shard_map/ppermute | solution.py:156
  5.8 1.0 %copy-start = (bf16[24,8192]{1,0:T(8,128)(2,1)S(1)}, bf16[24,8192]{1,0:T(8,128)(2,1)}, u32[]{:S(2)}) copy-start(bf16[24,8192]{1,0:T(8,128)(2,1)} %x_ref.1) | copy-start | bytes 1179652
  6.8 8.2 %copy-start.4 = (bf16[8,1024,4]{1,2,0:T(4,128)(2,1)S(1)}, bf16[8,1024,4]{1,2,0:T(4,128)(2,1)}, u32[]{:S(2)}) copy-start(bf16[8,1024,4]{1,2,0:T(4,128)(2,1)} %param.21) | copy-start | bytes 196612
  6.8 8.2 %copy-start.2 = (bf16[8,7424,4]{1,2,0:T(4,128)(2,1)S(1)}, bf16[8,7424,4]{1,2,0:T(4,128)(2,1)}, u32[]{:S(2)}) copy-start(bf16[8,7424,4]{1,2,0:T(4,128)(2,1)} %param.20) | copy-start | bytes 1425412
  13.4 7.8 %collective-permute-start.3 = (bf16[2,24,2048]{2,1,0:T(8,128)(2,1)S(1)}, bf16[2,24,2048]{2,1,0:T(8,128)(2,1)S(1)}, u32[]{:S(2)}, u32[]{:S(2)}) collective-permute-start(bf16[2,24,2048]{2,1,0:T(8,128)(2,1)S(1)} %get-tuple-element.27), channel_id=1, source_target_pairs={{0,2},{2,0},{4,6},{6,4},{8,10},{10,8},{12,14},{14,12},{1,3},{3,1},... | collective-permute-start | bytes 589832 | tf_op jit(solution)/shard_map/ppermute | solution.py:156
  15.2 7.8 %collective-permute-start.1 = (bf16[2,8,7424]{2,1,0:T(8,128)(2,1)S(1)}, bf16[2,8,7424]{2,1,0:T(8,128)(2,1)S(1)}, u32[]{:S(2)}, u32[]{:S(2)}) collective-permute-start(bf16[2,8,7424]{2,1,0:T(8,128)(2,1)S(1)} %pad_maximum_fusion.dep_ref), channel_id=1, source_target_pairs={{0,4},{2,6},{4,0},{6,2},{8,12},{10,14},{12,8},{14,10},{1,5},{3,7},... | collective-permute-start | bytes 712712 | tf_op jit(solution)/shard_map/ppermute | solution.py:156
  16.9 10.0 %collective-permute-start.2 = (bf16[2,24,2048]{2,1,0:T(8,128)(2,1)S(1)}, bf16[2,24,2048]{2,1,0:T(8,128)(2,1)S(1)}, u32[]{:S(2)}, u32[]{:S(2)}) collective-permute-start(bf16[2,24,2048]{2,1,0:T(8,128)(2,1)S(1)} %get-tuple-element.26), channel_id=1, source_target_pairs={{0,2},{2,0},{4,6},{6,4},{8,10},{10,8},{12,14},{14,12},{1,3},{3,1},... | collective-permute-start | bytes 589832 | tf_op jit(solution)/shard_map/ppermute | solution.py:156
  21.3 5.7 %collective-permute-start.4 = (bf16[2,24,2048]{2,1,0:T(8,128)(2,1)S(1)}, bf16[2,24,2048]{2,1,0:T(8,128)(2,1)S(1)}, u32[]{:S(2)}, u32[]{:S(2)}) collective-permute-start(bf16[2,24,2048]{2,1,0:T(8,128)(2,1)S(1)} %add_convert_fusion.1), channel_id=1, source_target_pairs={{0,4},{2,6},{4,0},{6,2},{8,12},{10,14},{12,8},{14,10},{1,5},{3,7},... | collective-permute-start | bytes 589832 | tf_op jit(solution)/shard_map/ppermute | solution.py:156
  23.0 6.1 %copy-start.3 = (bf16[4096,128]{1,0:T(8,128)(2,1)S(1)}, bf16[4096,128]{1,0:T(8,128)(2,1)}, u32[]{:S(2)}) copy-start(bf16[4096,128]{1,0:T(8,128)(2,1)} %param.22) | copy-start | bytes 3145732
  27.1 9.5 %collective-permute-start.5 = (bf16[2,24,2048]{2,1,0:T(8,128)(2,1)S(1)}, bf16[2,24,2048]{2,1,0:T(8,128)(2,1)S(1)}, u32[]{:S(2)}, u32[]{:S(2)}) collective-permute-start(bf16[2,24,2048]{2,1,0:T(8,128)(2,1)S(1)} %fusion), channel_id=1, source_target_pairs={{0,8},{2,10},{4,12},{6,14},{8,0},{10,2},{12,4},{14,6},{1,9},{3,11}... | collective-permute-start | bytes 589832 | tf_op jit(solution)/shard_map/ppermute | solution.py:156
  27.6 12.5 %collective-permute-start.6 = (bf16[4,8,7424]{2,1,0:T(8,128)(2,1)S(1)}, bf16[4,8,7424]{2,1,0:T(8,128)(2,1)S(1)}, u32[]{:S(2)}, u32[]{:S(2)}) collective-permute-start(bf16[4,8,7424]{2,1,0:T(8,128)(2,1)S(1)} %constant_dynamic-update-slice_fusion.near_ref), channel_id=1, source_target_pairs={{0,2},{2,0},{4,6},{6,4},{8,10},{10,8},{12,14},{14,12},{1,3},{3,1},... | collective-permute-start | bytes 1425416 | tf_op jit(solution)/shard_map/ppermute | solution.py:156
  29.2 9.4 %collective-permute-start.7 = (bf16[1024,128]{1,0:T(8,128)(2,1)S(1)}, bf16[1024,128]{1,0:T(8,128)(2,1)S(1)}, u32[]{:S(2)}, u32[]{:S(2)}) collective-permute-start(bf16[1024,128]{1,0:T(8,128)(2,1)S(1)} %constant_dynamic-slice_fusion), channel_id=1, source_target_pairs={{0,1},{1,0},{2,3},{3,2},{4,5},{5,4},{6,7},{7,6},{8,9},{9,8},{10,11... | collective-permute-start | bytes 786440 | tf_op jit(solution)/shard_map/ppermute | solution.py:156
  36.8 7.2 %collective-permute-start.8 = (bf16[2,24,1920]{2,1,0:T(8,128)(2,1)S(1)}, bf16[2,24,1920]{2,1,0:T(8,128)(2,1)S(1)}, u32[]{:S(2)}, u32[]{:S(2)}) collective-permute-start(bf16[2,24,1920]{2,1,0:T(8,128)(2,1)S(1)} %slice.18.refs_2_), channel_id=1, source_target_pairs={{0,4},{2,6},{4,0},{6,2},{8,12},{10,14},{12,8},{14,10},{1,5},{3,7},... | collective-permute-start | bytes 552968 | tf_op jit(solution)/shard_map/ppermute | solution.py:156
  36.9 7.9 %collective-permute-start.10 = (bf16[2,24,1920]{2,1,0:T(8,128)(2,1)S(1)}, bf16[2,24,1920]{2,1,0:T(8,128)(2,1)S(1)}, u32[]{:S(2)}, u32[]{:S(2)}) collective-permute-start(bf16[2,24,1920]{2,1,0:T(8,128)(2,1)S(1)} %slice.18.refs_2_), channel_id=1, source_target_pairs={{0,2},{2,0},{4,6},{6,4},{8,10},{10,8},{12,14},{14,12},{1,3},{3,1},... | collective-permute-start | bytes 552968 | tf_op jit(solution)/shard_map/ppermute | solution.py:156
  44.0 10.0 %copy-start.1 = (bf16[24,8192]{1,0:T(8,128)(2,1)S(1)}, bf16[24,8192]{1,0:T(8,128)(2,1)}, u32[]{:S(2)}) copy-start(bf16[24,8192]{1,0:T(8,128)(2,1)} %x_ref.1) | copy-start | bytes 1179652
  44.0 21.3 %copy-start.5 = (s32[24]{0:T(128)S(1)}, s32[24]{0:T(128)}, u32[]{:S(2)}) copy-start(s32[24]{0:T(128)} %param.23) | copy-start | bytes 292
  44.1 5.9 %collective-permute-start.9 = (bf16[2,24,1920]{2,1,0:T(8,128)(2,1)S(1)}, bf16[2,24,1920]{2,1,0:T(8,128)(2,1)S(1)}, u32[]{:S(2)}, u32[]{:S(2)}) collective-permute-start(bf16[2,24,1920]{2,1,0:T(8,128)(2,1)S(1)} %collective-permute-done.8.refs_2_), channel_id=1, source_target_pairs={{0,2},{2,0},{4,6},{6,4},{8,10},{10,8},{12,14},{14,12},{1,3},{3,1},... | collective-permute-start | bytes 552968 | tf_op jit(solution)/shard_map/ppermute | solution.py:156
  52.3 1.8 %collective-permute-start.11 = (f32[96,1024]{1,0:T(8,128)S(1)}, f32[96,1024]{1,0:T(8,128)S(1)}, u32[]{:S(2)}, u32[]{:S(2)}) collective-permute-start(f32[96,1024]{1,0:T(8,128)S(1)} %get-tuple-element.41), channel_id=1, source_target_pairs={{0,1},{1,0},{2,3},{3,2},{4,5},{5,4},{6,7},{7,6},{8,9},{9,8},{10,11... | collective-permute-start | bytes 1179656 | tf_op jit(solution)/shard_map/ppermute | solution.py:156
  54.4 4.2 %collective-permute-start.12 = (f32[104,128]{1,0:T(8,128)S(1)}, f32[104,128]{1,0:T(8,128)S(1)}, u32[]{:S(2)}, u32[]{:S(2)}) collective-permute-start(f32[104,128]{1,0:T(8,128)S(1)} %part_logits.1), channel_id=1, source_target_pairs={{0,2},{2,0},{4,6},{6,4},{8,10},{10,8},{12,14},{14,12},{1,3},{3,1},... | collective-permute-start | bytes 159752 | tf_op jit(solution)/shard_map/ppermute | solution.py:156
  58.6 4.4 %collective-permute-start.13 = (f32[104,128]{1,0:T(8,128)S(1)}, f32[104,128]{1,0:T(8,128)S(1)}, u32[]{:S(2)}, u32[]{:S(2)}) collective-permute-start(f32[104,128]{1,0:T(8,128)S(1)} %add.32), channel_id=1, source_target_pairs={{0,4},{2,6},{4,0},{6,2},{8,12},{10,14},{12,8},{14,10},{1,5},{3,7},... | collective-permute-start | bytes 159752 | tf_op jit(solution)/shard_map/ppermute | solution.py:156
  63.0 5.1 %collective-permute-start.14 = (f32[104,128]{1,0:T(8,128)S(1)}, f32[104,128]{1,0:T(8,128)S(1)}, u32[]{:S(2)}, u32[]{:S(2)}) collective-permute-start(f32[104,128]{1,0:T(8,128)S(1)} %add.33.a_ref), channel_id=1, source_target_pairs={{0,8},{2,10},{4,12},{6,14},{8,0},{10,2},{12,4},{14,6},{1,9},{3,11}... | collective-permute-start | bytes 159752 | tf_op jit(solution)/shard_map/ppermute | solution.py:156
  68.3 1.2 %collective-permute-start.15 = (f32[8,128]{1,0:T(8,128)S(1)}, f32[8,128]{1,0:T(8,128)S(1)}, u32[]{:S(2)}, u32[]{:S(2)}) collective-permute-start(f32[8,128]{1,0:T(8,128)S(1)} %part_rewards.1.a_ref), channel_id=1, source_target_pairs={{0,1},{1,0},{2,3},{3,2},{4,5},{5,4},{6,7},{7,6},{8,9},{9,8},{10,11... | collective-permute-start | bytes 12296 | tf_op jit(solution)/shard_map/ppermute | solution.py:156
